TPU v7x, 32 devices: a whole 2x2x4 slice. The times are simulated.
32 devices in a mesh: dp: 8 (over y, x, core), loop: 4 (over z).
Axes of the slice: x: 2, y: 2, z: 4, core: 2. Of those that a mesh axis runs over, the one named last changes fastest.
Arguments:
- tokens: bfloat16 [3072, 4096], P('dp')
- cotangent: bfloat16 [3072, 4096], P('dp'), may hold values from -6 to 6
- proj_weight: bfloat16 [4096, 4096], P(None, 'dp')
- rotation: float32 [4096, 4096], P('dp', 'loop')
- doc_lengths: int32 [48], P('dp'), may hold values from 1 to 64, as said below
Outputs:
- riemannian: float32 [4096, 4096], P('dp', 'loop')
Inputs may be any that keep to these rules, and one draw needn't show every extreme that they name: `doc_lengths`: each slot holds 1 to 64 tokens; some slot holds exactly 64 in every draw.
All inputs are finite; a program needn't handle non-finite values.
Results may differ from a plain program's by a relative error of at most 0.009.
The roundings to bfloat16 on the way count: a program that leaves them out, or rounds other values in their place, can miss the bound.
Values may be sent and summed in bfloat16 or wider, within the bound.
No kernel may reach another device: no remote copies, remote signals or barrier semaphores. Data moves between devices by JAX's collectives and lax.ppermute only.
A program may use at most 128 MiB of HBM per device.

v0:
```python
import jax
import jax.numpy as jnp
from jax import lax
from jax.sharding import PartitionSpec as P

clip_ratio = 2.0
eps_power = 1e-06


def on_device(tokens, cotangent, proj_weight, rotation, doc_lengths):
    tok_rows, feat_width = tokens.shape
    slot_count = doc_lengths.shape[0]
    slot_len = tok_rows // slot_count
    positions = jnp.arange(tok_rows, dtype=jnp.int32)
    slot_match = (positions // slot_len)[:, None] == jnp.arange(slot_count, dtype=jnp.int32)[
        None, :
    ]
    row_lengths = jnp.sum(jnp.where(slot_match, doc_lengths[None, :], 0), axis=1)
    live_rows = positions % slot_len < row_lengths
    masked = cotangent * live_rows.astype(jnp.bfloat16)[:, None]
    block_piece = lax.all_gather(rotation.astype(jnp.bfloat16), "dp", axis=0, tiled=True)
    token_cols = tokens
    weight_rows = proj_weight
    act_sum = jnp.dot(token_cols, block_piece, preferred_element_type=jnp.float32)
    mixed_sum = lax.dot_general(
        block_piece, weight_rows, (((0,), (0,)), ((), ())), preferred_element_type=jnp.float32
    )
    row_power, col_power = lax.psum(
        (jnp.sum(act_sum * act_sum, axis=1), jnp.sum(mixed_sum * mixed_sum, axis=0)), "loop"
    )
    row_limit = clip_ratio * jnp.sqrt(row_power / feat_width + eps_power)[:, None]
    col_limit = clip_ratio * jnp.sqrt(col_power / feat_width + eps_power)[None, :]
    acts_q = jnp.clip(act_sum, -row_limit, row_limit).astype(jnp.bfloat16)
    mixed_q = jnp.clip(mixed_sum, -col_limit, col_limit).astype(jnp.bfloat16)
    grad_acts = lax.dot_general(
        masked,
        lax.all_gather(mixed_q, "dp", axis=1, tiled=True),
        (((1,), (1,)), ((), ())),
        preferred_element_type=jnp.float32,
    ).astype(jnp.bfloat16)
    cot_owned = lax.all_to_all(masked, "dp", split_axis=1, concat_axis=0, tiled=True)
    acts_every = lax.all_gather(acts_q, "dp", axis=0, tiled=True)
    grad_mixed = lax.dot_general(
        cot_owned, acts_every, (((0,), (0,)), ((), ())), preferred_element_type=jnp.float32
    ).astype(jnp.bfloat16)
    all_tokens = tok_rows * lax.axis_size("dp")
    token_cols = tokens
    weight_rows = proj_weight
    left_part = lax.dot_general(
        token_cols, grad_acts, (((0,), (0,)), ((), ())), preferred_element_type=jnp.float32
    )
    gradient = lax.psum_scatter(
        left_part + jnp.dot(weight_rows, grad_mixed, preferred_element_type=jnp.float32),
        "dp",
        scatter_dimension=0,
        tiled=True,
    ) * (1.0 / jnp.sqrt(jnp.float32(all_tokens)))
    grad_strip, rot_strip = (
        lax.all_gather(gradient, "loop", axis=1, tiled=True),
        lax.all_gather(rotation, "loop", axis=1, tiled=True),
    )
    cross = lax.psum_scatter(
        lax.dot_general(
            grad_strip,
            rotation,
            (((0,), (0,)), ((), ())),
            precision=lax.Precision.HIGHEST,
            preferred_element_type=jnp.float32,
        ),
        "dp",
        scatter_dimension=0,
        tiled=True,
    )
    correction = jnp.dot(
        rot_strip,
        lax.all_gather(cross, "dp", axis=0, tiled=True),
        precision=lax.Precision.HIGHEST,
        preferred_element_type=jnp.float32,
    )
    return gradient - correction


def solution(mesh):
    in_specs = (P("dp", None), P("dp", None), P(None, "dp"), P("dp", "loop"), P("dp"))
    out_specs = P("dp", "loop")
    return jax.shard_map(
        on_device, mesh=mesh, in_specs=in_specs, out_specs=out_specs, check_vma=False
    )
```

profile of v0, /device:TPU:0, one launch (start us, length us, event | category | flops | bytes accessed | tf_op | source)
XLA Modules:
  0.0 962.4 jit_solution(8967548232701451506)
XLA Ops:
  6.5 0.0 copy-start
  6.5 0.0 all-gather.7.cloned.1.call-start
  6.5 2.9 convert_element_type.23
  9.4 0.0 all-gather.7.cloned.1.call-update
  9.4 0.0 all-gather.11.cloned.1.call-start
  9.5 57.2 %all-gather.7.cloned.1.call-done = bf16[4096,1024]{1,0:T(8,128)(2,1)} async-done(((bf16[512,1024]{1,0:T(8,128)(2,1)}), bf16[4096,1024]{1,0:T(8,128)(2,1)}) %all-gather.7.cloned.1.call-update) | async-done | bytes 8388624 | tf_op jit(solution)/shard_map/all_gather | solution.py:21
  66.7 0.0 copy-start.5
  66.7 10.2 %multiply_reduce_fusion = (f32[512]{0:T(512)S(1)}, bf16[1024,512]{1,0:T(8,128)(2,1)}) fusion(bf16[4096,1024]{1,0:T(8,128)(2,1)} %all-gather.7.cloned.1.call-done, bf16[4096,512]{1,0:T(8,128)(2,1)} %param.7), kind=kOutput, calls=%fused_computation.3 | convolution fusion | flops 4296539648 | bytes 13633536 | tf_op jit(solution)/shard_map/dot_general | solution.py:25
  76.9 0.0 copy-done
  76.9 0.0 copy-done.5
  76.9 4.3 multiply_reduce_fusion.1
  81.2 11.7 %all-reduce = (f32[384]{0:T(512)S(1)}, f32[512]{0:T(512)S(1)}) all-reduce(f32[384]{0:T(512)S(1)} %get-tuple-element.11, f32[512]{0:T(512)S(1)} %get-tuple-element.13), channel_id=1, replica_groups=mesh['dp'=8,'loop'=4] {'loop'}, use_global_device_ids=true, to_apply=%region_4.5 | all-reduce | flops 896 | bytes 7168 | tf_op jit(solution)/shard_map/psum | solution.py:28
  92.9 2.2 minimum_convert_fusion.1
  95.1 0.0 all-gather.11.cloned.1.call-update
  95.1 0.0 all-gather.9.cloned.1.call-start
  95.2 2.3 minimum_convert_fusion
  97.5 0.0 all-gather.9.cloned.1.call-update
  97.5 0.0 copy-start.4
  97.5 0.0 reduce-scatter.3.cloned.1.call-start
  97.6 4.7 copy.11
  102.3 0.0 copy-done.4
  102.3 0.1 select_reduce_fusion
  102.4 2.2 broadcast_multiply_fusion
  104.6 0.0 copy-start.2
  104.6 57.9 %all_to_all.19 = bf16[384,8,512]{0,2,1:T(8,128)(2,1)} all-to-all(bf16[384,8,512]{0,2,1:T(8,128)(2,1)S(1)} %bitcast.39), channel_id=1, replica_groups=mesh['dp'=8,'loop'=4] {'dp'}, dimensions={1} | all-to-all | bytes 6291456 | tf_op jit(solution)/shard_map/all_to_all | solution.py:41
  162.5 0.0 copy-done.2
  162.5 4.8 copy.12
  167.3 0.0 all-gather.11.cloned.1.call-done
  167.3 15.6 %fusion.9 = f32[1024,4096]{1,0:T(8,128)} fusion(bf16[4096,512]{1,0:T(8,128)(2,1)} %param.7, bf16[3072,512]{1,0:T(8,128)(2,1)} %bitcast.41, bf16[3072,1024]{1,0:T(8,128)(2,1)} %all-gather.11.cloned.1.call-done), kind=kOutput, calls=%fused_computation.28 | convolution fusion | flops 7516717056 | bytes 30408704 | tf_op jit(solution)/shard_map/dot_general | solution.py:53
  182.9 39.1 %all-gather.9.cloned.1.call-done = bf16[1024,4096]{1,0:T(8,128)(2,1)} async-done(((bf16[1024,512]{1,0:T(8,128)(2,1)}), bf16[1024,4096]{1,0:T(8,128)(2,1)}) %all-gather.9.cloned.1.call-update) | async-done | bytes 8388624 | tf_op jit(solution)/shard_map/all_gather | solution.py:37
  222.0 17.1 %add_bitcast_fusion = f32[4096,1024]{0,1:T(8,128)} fusion(f32[1024,4096]{1,0:T(8,128)} %fusion.9, bf16[384,4096]{1,0:T(8,128)(2,1)S(1)} %copy-done, bf16[384,4096]{0,1:T(8,128)(2,1)} %copy-done.2, bf16[1024,4096]{1,0:T(8,128)(2,1)} %all-gather.9.cloned.1.call-done), kind=kOutput, calls=%fused_computation | convolution fusion | flops 6447038464 | bytes 48234496 | tf_op jit(solution)/shard_map/dot_general | solution.py:49
  239.1 0.0 reduce-scatter.3.cloned.1.call-update
  239.1 0.0 copy-start.3
  239.2 0.0 all-gather.13.cloned.1.call-start
  239.2 116.1 %reduce-scatter.3.cloned.1.call-done = f32[512,1024]{0,1:T(8,128)} async-done(((f32[4096,1024]{0,1:T(8,128)}), f32[512,1024]{0,1:T(8,128)}) %reduce-scatter.3.cloned.1.call-update) | async-done | bytes 2097168 | tf_op jit(solution)/shard_map/reduce_scatter | solution.py:52
  355.3 3.2 broadcast_multiply_fusion.1
  358.4 0.0 all-gather.13.cloned.1.call-update
  358.5 0.3 reduce-scatter.5.cloned.1.call-start
  358.7 149.5 %all-gather.13.cloned.1.call-done = f32[512,4096]{0,1:T(8,128)} async-done(((f32[512,1024]{0,1:T(8,128)}), f32[512,4096]{0,1:T(8,128)}) %all-gather.13.cloned.1.call-update) | async-done | bytes 8388624 | tf_op jit(solution)/shard_map/all_gather | solution.py:59
  508.2 0.0 copy-done.3
  508.2 31.0 %fusion.10 = f32[4096,1024]{1,0:T(8,128)} fusion(f32[512,4096]{0,1:T(8,128)} %all-gather.13.cloned.1.call-done, f32[512,1024]{1,0:T(8,128)S(1)} %copy-done.3), kind=kOutput, calls=%fused_computation.29 | convolution fusion | flops 25769803776 | bytes 27262976 | tf_op jit(solution)/shard_map/dot_general | solution.py:63
  539.3 0.0 reduce-scatter.5.cloned.1.call-update
  539.3 0.0 all-gather.17.cloned.1.call-start
  539.4 0.7 all-gather.17.cloned.1.call-update
  540.1 0.0 all-gather.15.cloned.1.call-start
  540.1 113.6 %reduce-scatter.5.cloned.1.call-done = f32[512,1024]{1,0:T(8,128)} async-done(((f32[4096,1024]{1,0:T(8,128)}), f32[512,1024]{1,0:T(8,128)}) %reduce-scatter.5.cloned.1.call-update) | async-done | bytes 2097168 | tf_op jit(solution)/shard_map/reduce_scatter | solution.py:62
  653.7 0.0 all-gather.15.cloned.1.call-update
  653.7 151.2 %all-gather.17.cloned.1.call-done = f32[512,4096]{1,0:T(8,128)} async-done(((f32[512,1024]{1,0:T(8,128)}), f32[512,4096]{1,0:T(8,128)}) %all-gather.17.cloned.1.call-update) | async-done | bytes 8388624 | tf_op jit(solution)/shard_map/all_gather | solution.py:60
  804.9 90.0 %all-gather.15.cloned.1.call-done = f32[4096,1024]{1,0:T(8,128)} async-done(((f32[512,1024]{1,0:T(8,128)}), f32[4096,1024]{1,0:T(8,128)}) %all-gather.15.cloned.1.call-update) | async-done | bytes 16777232 | tf_op jit(solution)/shard_map/all_gather | solution.py:76
  894.9 0.0 copy-start.1
  894.9 57.8 %bitcast_subtract_fusion = f32[512,1024]{0,1:T(8,128)} fusion(f32[4096,1024]{1,0:T(8,128)} %all-gather.15.cloned.1.call-done, f32[512,4096]{1,0:T(8,128)} %all-gather.17.cloned.1.call-done, f32[512,1024]{0,1:T(8,128)} %reduce-scatter.3.cloned.1.call-done), kind=kOutput, calls=%fused_computation.1 | convolution fusion | flops 25770852352 | bytes 29360128 | tf_op jit(solution)/shard_map/dot_general | solution.py:74
  952.7 2.9 copy.13
  955.5 0.0 copy-done.1
  (4 shorter events, 0.0 us)
Async XLA Ops:
  6.5 70.4 %copy-start = (bf16[384,4096]{1,0:T(8,128)(2,1)S(1)}, bf16[384,4096]{1,0:T(8,128)(2,1)}, u32[]{:S(2)}) copy-start(bf16[384,4096]{1,0:T(8,128)(2,1)} %param.5) | copy-start | bytes 9437188
  6.5 60.1 %all-gather.7.cloned.1.call-start = ((), (), s32[]{:S(2)}) async-start(), calls=%async_computation.3 | async-start | bytes 9437184 | tf_op jit(solution)/shard_map/all_gather | solution.py:21
  9.4 157.8 %all-gather.11.cloned.1.call-start = ((), (), s32[]{:S(2)}) async-start(), calls=%async_computation.5 | async-start | bytes 7077888 | tf_op jit(solution)/shard_map/all_gather | solution.py:42
  66.7 10.2 %copy-start.5 = (bf16[4096,1024]{1,0:T(8,128)(2,1)S(1)}, bf16[4096,1024]{1,0:T(8,128)(2,1)}, u32[]{:S(2)}) copy-start(bf16[4096,1024]{1,0:T(8,128)(2,1)} %all-gather.7.cloned.1.call-done) | copy-start | bytes 25165828
  95.1 126.8 %all-gather.9.cloned.1.call-start = ((), (), s32[]{:S(2)}) async-start(), calls=%async_computation.4 | async-start | bytes 9437184 | tf_op jit(solution)/shard_map/all_gather | solution.py:37
  97.5 4.8 copy-start.4
  97.5 257.8 %reduce-scatter.3.cloned.1.call-start = ((), (), s32[]{:S(2)}) async-start(), calls=%async_computation.6 | async-start | bytes 18874368 | tf_op jit(solution)/shard_map/reduce_scatter | solution.py:52
  104.6 57.9 %copy-start.2 = (bf16[384,4096]{0,1:T(8,128)(2,1)}, bf16[384,4096]{0,1:T(8,128)(2,1)S(1)}, u32[]{:S(2)}) copy-start(bf16[384,4096]{0,1:T(8,128)(2,1)S(1)} %broadcast_multiply_fusion) | copy-start | bytes 9437188
  239.1 269.1 %copy-start.3 = (f32[512,1024]{1,0:T(8,128)S(1)}, f32[512,1024]{1,0:T(8,128)}, u32[]{:S(2)}) copy-start(f32[512,1024]{1,0:T(8,128)} %param.8) | copy-start | bytes 6291460
  239.2 269.1 %all-gather.13.cloned.1.call-start = ((), (), s32[]{:S(2)}) async-start(), calls=%async_computation.7 | async-start | bytes 10485760 | tf_op jit(solution)/shard_map/all_gather | solution.py:59
  358.5 295.2 %reduce-scatter.5.cloned.1.call-start = ((), (), s32[]{:S(2)}) async-start(), calls=%async_computation.8 | async-start | bytes 18874368 | tf_op jit(solution)/shard_map/reduce_scatter | solution.py:62
  539.3 265.6 %all-gather.17.cloned.1.call-start = ((), (), s32[]{:S(2)}) async-start(), calls=%async_computation.10 | async-start | bytes 10485760 | tf_op jit(solution)/shard_map/all_gather | solution.py:60
  540.1 354.8 %all-gather.15.cloned.1.call-start = ((), (), s32[]{:S(2)}) async-start(), calls=%async_computation.9 | async-start | bytes 18874368 | tf_op jit(solution)/shard_map/all_gather | solution.py:76
  894.9 60.7 %copy-start.1 = (bf16[384,4096]{1,0:T(8,128)(2,1)S(1)}, bf16[384,4096]{1,0:T(8,128)(2,1)}, u32[]{:S(2)}) copy-start(bf16[384,4096]{1,0:T(8,128)(2,1)} %param.5) | copy-start | bytes 9437188
Sparse Core Ops, SparseCore 0:
  9.6 57.0 all-gather.6
  95.3 68.7 all-gather.10
  165.9 56.0 all-gather.8
  239.3 115.9 reduce-scatter.2
  358.6 149.5 all-gather.12
  539.4 114.1 reduce-scatter.4
  655.2 149.6 all-gather.16
  806.8 88.0 all-gather.14
where the time goes:
time: 963 us; the launch traced here: 962 us
  waiting for transfers between devices  717 us (74%)
  matrix products  136 us (14%)
  blocking collectives  69.6 us (7%)
  between operations  13.5 us (1%)
  other arithmetic  12.8 us (1%)
  local copies, waits for them, and re-layouts  12.4 us (1%)
    all_gather x1, waiting for transfers between devices, on_device(): lax.all_gather(rotation, 'loop', axis=1, tiled=True)  151 us
    all_gather x1, waiting for transfers between devices, on_device(): lax.all_gather(gradient, 'loop', axis=1, tiled=True)  149 us
    reduce_scatter x1, waiting for transfers between devices, on_device(): lax.psum_scatter(left_part + jnp.dot(weight_rows, grad_mixed, preferred_e...  116 us
    reduce_scatter x1, waiting for transfers between devices, on_device(): lax.psum_scatter(lax.dot_general(grad_strip, rotation, (((0,), (0,)), (()...  114 us
    all_gather x1, waiting for transfers between devices, on_device(): lax.all_gather(cross, 'dp', axis=0, tiled=True)  90 us
    all_to_all x1, blocking collectives, on_device(): lax.all_to_all(masked, 'dp', split_axis=1, concat_axis=0, tiled=True)  57.9 us
    dot_general x1, matrix products, on_device(): jnp.dot(rot_strip, lax.all_gather(cross, 'dp', axis=0, tiled=True), preci...  57.8 us
    all_gather x1, waiting for transfers between devices, on_device(): lax.all_gather(rotation.astype(jnp.bfloat16), 'dp', axis=0, tiled=True)  57.2 us
  transfers between devices with their start and end apart: 8, of which 7 were waited for; matrix products, arithmetic and copies ran while one was open for 3% of the time, Pallas kernels for 0%

commit v1 on v0

v1 whole, which is shorter than its diff:
```python
import jax
import jax.numpy as jnp
from jax import lax
from jax.sharding import PartitionSpec as P

clip_ratio = 2.0
eps_power = 1e-06
cot_limit = 6.0
code_top = 30000.0
BF16 = jnp.bfloat16
F16 = jnp.float16
F32 = jnp.float32


def swap(x, mask):
    n = lax.axis_size("dp")
    return lax.ppermute(x, "dp", [(i, i ^ mask) for i in range(n)])


def relative_masks():
    half = lax.axis_size("dp") // 2
    return [(q % half) * 2 + q // half for q in range(2 * half)]


def gather_chips(x):
    chips = lax.axis_size("dp") // 2
    if chips == 4:
        half = x.shape[0] // 2
        from_x, from_y = swap(x, 2), swap(x, 4)
        far = [swap(from_x[:half], 4), swap(from_y[half:], 2)]
        return jnp.concatenate([x, from_x, from_y] + far, axis=0)
    bit = 1
    while bit < chips:
        x = jnp.concatenate([x, swap(x, 2 * bit)], axis=0)
        bit *= 2
    return x


def gather(x):
    near = gather_chips(x)
    return jnp.concatenate([near, swap(near, 1)], axis=0)


def gather_small(x):
    return jnp.stack([x] + [swap(x, m) for m in relative_masks()[1:]])


def flip(x, mask):
    n = lax.axis_size("dp")
    place = (mask & 1) * (n // 2) + (mask >> 1)
    width = x.shape[1] // n
    parts = [x[:, (q ^ place) * width : ((q ^ place) + 1) * width] for q in range(n)]
    return jnp.concatenate(parts, axis=1)


def scatter(near, away):
    chips = lax.axis_size("dp") // 2

    def trade(x, mask):
        return flip(swap(x.astype(F16), mask), mask).astype(F32)

    total = near + trade(away, 1)
    size = near.shape[0] // chips
    if chips == 4:
        own, to_x, to_y, far = (total[i * size : (i + 1) * size] for i in range(4))
        half = size // 2
        via_x, via_y = trade(far[:half], 2), trade(far[half:], 4)
        to_y = jnp.concatenate([to_y[:half] + via_x, to_y[half:]], axis=0)
        to_x = jnp.concatenate([to_x[:half], to_x[half:] + via_y], axis=0)
        return own + trade(to_x, 2) + trade(to_y, 4)
    bit = chips // 2
    while bit:
        half = total.shape[0] // 2
        total = total[:half] + trade(total[half:], 2 * bit)
        bit //= 2
    return total


def gather_loop(x):
    n = lax.axis_size("loop")
    up, down = [x], [x]
    for step in range(1, n):
        up.append(lax.ppermute(up[-1], "loop", [(i, i - 1) for i in range(1, n - step + 1)]))
        down.append(lax.ppermute(down[-1], "loop", [(i, i + 1) for i in range(step - 1, n - 1)]))
    me = lax.axis_index("loop")
    return [x] + [jnp.where(me + r < n, up[r], down[n - r]) for r in range(1, n)]


def sum_loop(x):
    n = lax.axis_size("loop")
    bit = 1
    while bit < n:
        x = x + lax.ppermute(x, "loop", [(i, i ^ bit) for i in range(n)])
        bit *= 2
    return x


def dot(a, b, ca, cb):
    return lax.dot_general(a, b, (((ca,), (cb,)), ((), ())), preferred_element_type=F32)


def split(x):
    high = lax.reduce_precision(x, 8, 7)
    return high.astype(BF16), (x - high).astype(BF16)


def half_code(x, scale):
    return lax.reduce_precision(x * scale, 5, 10)


def on_device(tokens, cotangent, proj_weight, rotation, doc_lengths):
    tok_rows, feat_width = tokens.shape
    slot_count = doc_lengths.shape[0]
    slot_len = tok_rows // slot_count
    n, loops = lax.axis_size("dp"), lax.axis_size("loop")
    me, level = lax.axis_index("dp"), lax.axis_index("loop")
    place = (me & 1) * (n // 2) + (me >> 1)
    masks = relative_masks()
    row_block, panel = rotation.shape
    out_block = proj_weight.shape[1]
    all_tokens, all_outs = tok_rows * n, out_block * n
    chunks = max(1, panel // (n * 32))
    wide = panel // chunks
    sub = wide // n

    def relative(x, width, axis):
        cut = [lax.dynamic_slice_in_dim(x, (me ^ m) * width, width, axis) for m in masks]
        return jnp.concatenate(cut, axis=axis)

    rot_top = jnp.maximum(jnp.max(jnp.abs(rotation)), 1e-30)
    rot_unit = rot_top / code_top
    rot_scale = code_top / rot_top
    rot_round = lax.reduce_precision(rotation, 8, 7)
    code = half_code(rotation, rot_scale)
    inner = half_code(rot_round + 0.75 * (rotation - rot_round), rot_scale)
    kept = lax.reduce_precision(code * rot_unit, 8, 7) == rot_round
    rot_code = jnp.where(kept, code, inner).astype(F16)
    rot_units = gather_small(jnp.full((128,), rot_unit))[:, :1]
    rot_parts = [gather(rot_code[:, c * wide : (c + 1) * wide]) for c in range(chunks)]

    def decode(parts):
        return (parts.reshape(n, row_block, -1).astype(F32) * rot_units[:, :, None]).reshape(
            parts.shape
        )

    positions = jnp.arange(tok_rows, dtype=jnp.int32)
    slot_match = (positions // slot_len)[:, None] == jnp.arange(slot_count, dtype=jnp.int32)[
        None, :
    ]
    row_lengths = jnp.sum(jnp.where(slot_match, doc_lengths[None, :], 0), axis=1)
    live_rows = positions % slot_len < row_lengths
    masked = relative(cotangent * live_rows.astype(BF16)[:, None], out_block, 1)
    both = jnp.concatenate(
        [relative(tokens, row_block, 1), relative(proj_weight, row_block, 0).T], axis=0
    )

    share = tok_rows // loops
    own_share = lax.dynamic_slice_in_dim(masked, level * share, share, 0)
    cuts = [own_share[:, q * out_block : (q + 1) * out_block] for q in range(n)]
    cuts = jnp.stack([cuts[0]] + [swap(x, m) for x, m in zip(cuts[1:], masks[1:])])
    shares = jnp.stack(gather_loop(cuts))
    cot_owned = jnp.concatenate(
        [
            lax.dynamic_index_in_dim(shares, (a - level) % loops, 0, keepdims=False)
            for a in range(loops)
        ],
        axis=1,
    ).reshape(all_tokens, out_block)

    rotated = [dot(both, decode(p).astype(BF16), 1, 0) for p in rot_parts]
    power = sum_loop(sum(jnp.sum(r * r, axis=1) for r in rotated))
    limit = clip_ratio * jnp.sqrt(power / feat_width + eps_power)
    tok_top = jnp.max(jnp.abs(tokens), axis=1).astype(F32)
    weight_top = jnp.max(jnp.abs(proj_weight), axis=0).astype(F32)
    sizes = [
        jnp.sum(limit[tok_rows:] ** 2),
        jnp.sum(limit[:tok_rows] ** 2),
        jnp.sum(tok_top**2),
        jnp.sum(weight_top**2),
        jnp.max(jnp.sum(rotation**2, axis=0)),
    ]
    sizes = jnp.concatenate([jnp.stack(sizes), jnp.zeros((128 - len(sizes),), F32)])
    told = gather_small(jnp.concatenate([limit, sizes]))
    limits = told[:, : limit.shape[0]].astype(BF16)
    norms = jnp.sqrt(n * jnp.max(told[:, limit.shape[0] :], axis=0))
    bound = cot_limit * all_outs**0.5 * (norms[0] * norms[2] + norms[1] * norms[3])
    grad_scale = code_top / jnp.clip(1.02 * bound, 1e-30, 3e38)
    cross_scale = 0.9 / (feat_width**0.5 * jnp.maximum(norms[4], 1e-15))

    acts_limit = limits[:, :tok_rows].reshape(all_tokens, 1)
    mixed_limit = limits[:, tok_rows:].reshape(all_outs, 1)
    acts = [gather(r[:tok_rows].astype(BF16)) for r in rotated]
    mixed = [gather(r[tok_rows:].astype(BF16)) for r in rotated]
    acts_q = [jnp.clip(r, -acts_limit, acts_limit) for r in acts]
    mixed_q = [jnp.clip(r, -mixed_limit, mixed_limit) for r in mixed]
    grad_acts = [dot(masked, m, 1, 0).astype(BF16) for m in mixed_q]
    grad_mixed = [dot(cot_owned, a, 0, 0).astype(BF16) for a in acts_q]

    cols = jnp.arange(wide, dtype=jnp.int32)
    source = ((cols // sub) ^ place) * sub + cols % sub
    shuffle = (cols[:, None] == source[None, :]).astype(BF16)
    to_code = grad_scale / jnp.sqrt(F32(all_tokens))

    rot_high, rot_low = split(decode(jnp.concatenate(rot_parts, axis=1)))
    rows_units = jnp.stack(gather_loop(jnp.full((128,), rot_unit)))[:, :1, None]
    rows_code = jnp.stack(gather_loop(rot_code.T)).astype(F32) * rows_units
    rows_code = rows_code.reshape(loops, chunks, n, sub, row_block)
    rows_code = jnp.concatenate(
        [lax.dynamic_slice_in_dim(rows_code, place ^ q, 1, 2) for q in range(n)], axis=2
    )
    rows_code = rows_code.transpose(1, 2, 0, 3, 4).reshape(chunks, n * loops * sub, row_block)

    strips, correction = [], 0.0
    for c in range(chunks):
        pair = jnp.concatenate([grad_acts[c], grad_mixed[c]], axis=0)
        pair = jnp.dot(pair, shuffle, preferred_element_type=F32).astype(BF16)
        near = dot(pair[:, : wide // 2], both, 0, 0) * to_code
        away = dot(pair[:, wide // 2 :], both, 0, 0) * to_code
        strip = scatter(near, away).astype(F16)
        strips.append(strip)
        rows = jnp.concatenate(gather_loop(strip), axis=0)
        high, low = split(rows.astype(F32))
        stacked = dot(jnp.concatenate([high, low], axis=0), rot_high, 1, 0)
        cross = stacked[: rows.shape[0]] + stacked[rows.shape[0] :] + dot(high, rot_low, 1, 0)
        cross = gather((cross * cross_scale).astype(F16)).astype(F32)
        cross_high, cross_low = split(cross)
        rows_high, rows_low = split(rows_code[c])
        correction = correction + dot(
            jnp.concatenate([rows_high, rows_low, rows_high], axis=0),
            jnp.concatenate([cross_high, cross_high, cross_low], axis=0),
            0,
            0,
        )

    strip = jnp.concatenate(strips, axis=0)
    blocks = [strip[:, q * row_block : (q + 1) * row_block] for q in range(n)]
    blocks = jnp.stack([blocks[0]] + [swap(b, m) for b, m in zip(blocks[1:], masks[1:])])
    blocks = jnp.concatenate(
        [lax.dynamic_slice_in_dim(blocks, place ^ q, 1, 0) for q in range(n)], axis=0
    )
    gradient = blocks.reshape(n, chunks, sub, row_block).transpose(1, 0, 2, 3)
    gradient = gradient.reshape(panel, row_block).T.astype(F32)
    unit = 1.0 / grad_scale
    return gradient * unit - correction * (unit / cross_scale)


def solution(mesh):
    in_specs = (P("dp", None), P("dp", None), P(None, "dp"), P("dp", "loop"), P("dp"))
    out_specs = P("dp", "loop")
    return jax.shard_map(
        on_device, mesh=mesh, in_specs=in_specs, out_specs=out_specs, check_vma=False
    )
```

time: 963 us -> 655 us (0.68)
  the two profiles are of different devices: /device:TPU:0 before, /device:TPU:17 now
where the time goes in v1:
time: 655 us; the launch traced here: 644 us
  starting transfers between devices  245 us (37%)
  local copies, waits for them, and re-layouts  130 us (20%)
  waiting for transfers between devices  121 us (18%)
  matrix products  95 us (15%)
  other arithmetic  45.4 us (7%)
  between operations  7.74 us (1%)
    ppermute x128, starting transfers between devices, swap(): return lax.ppermute(x, 'dp', [(i, i ^ mask) for i in range(n)])  151 us
    ppermute x128, waiting for transfers between devices, swap(): return lax.ppermute(x, 'dp', [(i, i ^ mask) for i in range(n)])  108 us
    unnamed x334, local copies, waits for them, and re-layouts  94.3 us
    dot_general x32, matrix products, dot(): lax.dot_general(a, b, (((ca,), (cb,)), ((), ())), preferred_element_type=...  93.9 us
    ppermute x21, starting transfers between devices, gather_loop(): lax.ppermute(down[-1], 'loop', [(i, i + 1) for i in range(step - 1, n - 1)])  49.8 us
    ppermute x21, starting transfers between devices, gather_loop(): lax.ppermute(up[-1], 'loop', [(i, i - 1) for i in range(1, n - step + 1)])  42.4 us
  transfers between devices with their start and end apart: 172, of which 52 were waited for; matrix products, arithmetic and copies ran while one was open for 38% of the time, Pallas kernels for 0%

profile of v1, /device:TPU:17, one launch (start us, length us, event | category | flops | bytes accessed | tf_op | source)
XLA Modules:
  0.0 644.2 jit_solution(6684294538407795574)
XLA Ops:
  0.0 2.7 multiply_reduce_fusion
  11.9 2.7 fusion.61
  14.6 3.7 fusion.293
  83.3 3.2 collective-permute-start.123
  102.2 3.1 collective-permute-done.42
  107.1 2.8 collective-permute-done.43
  109.8 7.4 %collective-permute-start.44 = (bf16[96,512]{1,0:T(8,128)(2,1)}, bf16[96,512]{1,0:T(8,128)(2,1)S(1)}, u32[]{:S(2)}, u32[]{:S(2)}) collective-permute-start(bf16[96,512]{1,0:T(8,128)(2,1)} %get-tuple-element.18), channel_id=1, source_target_pairs={{0,4},{4,0},{8,12},{12,8},{16,20},{20,16},{24,28},{28,24},{1,5},{5... | collective-permute-start | bytes 294920 | tf_op jit(solution)/shard_map/ppermute | solution.py:17
  120.3 3.1 collective-permute-done.45
  124.6 3.8 collective-permute-done.46
  130.4 3.6 collective-permute-done.47
  143.5 8.0 %collective-permute-done.24 = f16[256,256]{0,1:T(8,128)(2,1)S(1)} collective-permute-done((f16[256,256]{0,1:T(8,128)(2,1)S(1)}, f16[256,256]{0,1:T(8,128)(2,1)S(1)}, u32[]{:S(2)}, u32[]{:S(2)}) %collective-permute-start.24) | collective-permute-done | bytes 131104 | tf_op jit(solution)/shard_map/ppermute | solution.py:17
  154.1 2.9 collective-permute-start.48
  174.1 2.8 collective-permute-start.49
  177.0 3.2 collective-permute-start.21
  180.5 4.3 fusion.270
  192.6 5.1 pad_maximum_fusion
  206.8 3.2 concatenate.319
  221.2 3.9 collective-permute-start.52
  229.8 3.2 collective-permute-done.54
  243.8 2.8 collective-permute-done.84
  248.2 3.8 collective-permute-done.69
  255.5 3.5 collective-permute-done.36
  264.7 3.0 collective-permute-done.117
  303.2 2.6 collective-permute-start.51
  306.4 18.2 %collective-permute-start.58 = (bf16[1536,256]{1,0:T(8,128)(2,1)S(1)}, bf16[1536,256]{1,0:T(8,128)(2,1)S(1)}, u32[]{:S(2)}, u32[]{:S(2)}) collective-permute-start(bf16[1536,256]{1,0:T(8,128)(2,1)S(1)} %get-tuple-element.301), channel_id=1, source_target_pairs={{0,4},{4,0},{8,12},{12,8},{16,20},{20,16},{24,28},{28,24},{1,5},{5... | collective-permute-start | bytes 2359304 | tf_op jit(solution)/shard_map/ppermute | solution.py:17
  327.5 6.1 collective-permute-start.40
  340.3 2.6 fusion.123
  343.7 2.7 fusion.120
  348.3 2.9 collective-permute-start.119
  354.7 3.7 fusion.25
  361.1 3.5 fusion.28
  365.8 3.2 fusion.132
  369.3 3.5 fusion.27
  375.3 3.5 fusion.26
  400.8 5.3 collective-permute-start.107
  422.6 13.8 %collective-permute-done.91 = f16[32,4096]{1,0:T(8,128)(2,1)S(1)} collective-permute-done((f16[32,4096]{1,0:T(8,128)(2,1)S(1)}, f16[32,4096]{1,0:T(8,128)(2,1)S(1)}, u32[]{:S(2)}, u32[]{:S(2)}) %collective-permute-start.91) | collective-permute-done | bytes 262176 | tf_op jit(solution)/shard_map/ppermute | solution.py:17
  437.0 5.6 collective-permute-done.93
  447.0 3.2 collective-permute-start.151
  452.6 3.2 collective-permute-start.129
  456.9 4.1 collective-permute-done.109
  461.0 4.1 collective-permute-done.110
  466.0 3.9 collective-permute-done.111
  469.9 7.9 %collective-permute-start.112 = (f16[128,512]{1,0:T(8,128)(2,1)S(1)}, f16[128,512]{1,0:T(8,128)(2,1)S(1)}, u32[]{:S(2)}, u32[]{:S(2)}) collective-permute-start(f16[128,512]{1,0:T(8,128)(2,1)S(1)} %get-tuple-element.65), channel_id=1, source_target_pairs={{0,4},{4,0},{8,12},{12,8},{16,20},{20,16},{24,28},{28,24},{1,5},{5... | collective-permute-start | bytes 393224 | tf_op jit(solution)/shard_map/ppermute | solution.py:17
  479.0 5.2 collective-permute-done.113
  484.5 5.2 collective-permute-done.114
  490.9 5.2 collective-permute-done.115
  498.4 2.6 collective-permute-start.154
  505.0 3.4 collective-permute-start.161
  510.3 3.4 collective-permute-start.132
  515.7 3.4 collective-permute-start.143
  521.1 3.4 collective-permute-start.165
  529.6 2.6 collective-permute-done.141
  535.3 2.6 collective-permute-done.163
  545.5 4.1 constant_dynamic-update-slice_fusion.270
  549.5 4.1 collective-permute-start.164
  556.8 4.1 constant_dynamic-update-slice_fusion.248
  565.5 4.5 constant_dynamic-update-slice_fusion.259
  574.6 4.3 constant_dynamic-update-slice_fusion.281
  588.3 3.4 collective-permute-done.158
  597.1 8.0 %collective-permute-start.160 = (f16[512,1024]{1,0:T(8,128)(2,1)}, f16[512,1024]{1,0:T(8,128)(2,1)S(1)}, u32[]{:S(2)}, u32[]{:S(2)}) collective-permute-start(f16[512,1024]{1,0:T(8,128)(2,1)} %get-tuple-element.237), channel_id=1, source_target_pairs={{0,4},{4,0},{8,12},{12,8},{16,20},{20,16},{24,28},{28,24},{1,5},{5... | collective-permute-start | bytes 3145736 | tf_op jit(solution)/shard_map/ppermute | solution.py:17
  628.7 3.4 fusion.13
  632.2 3.4 fusion.1
  635.6 3.4 fusion.7
  639.1 4.9 bitcast_subtract_fusion
  (847 shorter events, 363.0 us)
Async XLA Ops:
  3.9 72.9 %collective-permute-start.5 = (f32[128]{0:T(128)}, f32[128]{0:T(128)S(1)}, u32[]{:S(2)}, u32[]{:S(2)}) collective-permute-start(f32[128]{0:T(128)} %broadcast_in_dim.18), channel_id=1, source_target_pairs={{0,8},{4,12},{8,0},{12,4},{16,24},{20,28},{24,16},{28,20},{1,9},{5... | collective-permute-start | bytes 1544 | tf_op jit(solution)/shard_map/ppermute | solution.py:17
  5.1 73.3 %collective-permute-start.6 = (f32[128]{0:T(128)}, f32[128]{0:T(128)}, u32[]{:S(2)}, u32[]{:S(2)}) collective-permute-start(f32[128]{0:T(128)} %broadcast_in_dim.18), channel_id=1, source_target_pairs={{0,16},{4,20},{8,24},{12,28},{16,0},{20,4},{24,8},{28,12},{1,17},{... | collective-permute-start | bytes 1544 | tf_op jit(solution)/shard_map/ppermute | solution.py:17
  6.4 72.2 %collective-permute-start.7 = (f32[128]{0:T(128)}, f32[128]{0:T(128)}, u32[]{:S(2)}, u32[]{:S(2)}) collective-permute-start(f32[128]{0:T(128)} %broadcast_in_dim.18), channel_id=1, source_target_pairs={{0,24},{4,28},{8,16},{12,20},{16,8},{20,12},{24,0},{28,4},{1,25},{... | collective-permute-start | bytes 1544 | tf_op jit(solution)/shard_map/ppermute | solution.py:17
  6.6 73.2 %collective-permute-start.8 = (f32[128]{0:T(128)}, f32[128]{0:T(128)}, u32[]{:S(2)}, u32[]{:S(2)}) collective-permute-start(f32[128]{0:T(128)} %broadcast_in_dim.18), channel_id=1, source_target_pairs={{0,4},{4,0},{8,12},{12,8},{16,20},{20,16},{24,28},{28,24},{1,5},{5... | collective-permute-start | bytes 1544 | tf_op jit(solution)/shard_map/ppermute | solution.py:17
  8.1 72.9 %collective-permute-start.9 = (f32[128]{0:T(128)}, f32[128]{0:T(128)}, u32[]{:S(2)}, u32[]{:S(2)}) collective-permute-start(f32[128]{0:T(128)} %broadcast_in_dim.18), channel_id=1, source_target_pairs={{0,12},{4,8},{8,4},{12,0},{16,28},{20,24},{24,20},{28,16},{1,13},{... | collective-permute-start | bytes 1544 | tf_op jit(solution)/shard_map/ppermute | solution.py:17
  78.5 57.1 %collective-permute-start.22 = (f16[512,256]{0,1:T(8,128)(2,1)}, f16[512,256]{0,1:T(8,128)(2,1)S(1)}, u32[]{:S(2)}, u32[]{:S(2)}) collective-permute-start(f16[512,256]{0,1:T(8,128)(2,1)} %get-tuple-element.101), channel_id=1, source_target_pairs={{0,8},{4,12},{8,0},{12,4},{16,24},{20,28},{24,16},{28,20},{1,9},{5... | collective-permute-start | bytes 786440 | tf_op jit(solution)/shard_map/ppermute | solution.py:17
  79.8 57.3 %collective-permute-start.23 = (f16[512,256]{0,1:T(8,128)(2,1)}, f16[512,256]{0,1:T(8,128)(2,1)S(1)}, u32[]{:S(2)}, u32[]{:S(2)}) collective-permute-start(f16[512,256]{0,1:T(8,128)(2,1)} %get-tuple-element.101), channel_id=1, source_target_pairs={{0,16},{4,20},{8,24},{12,28},{16,0},{20,4},{24,8},{28,12},{1,17},{... | collective-permute-start | bytes 786440 | tf_op jit(solution)/shard_map/ppermute | solution.py:17
  86.5 51.8 %collective-permute-start.17 = (f16[512,256]{0,1:T(8,128)(2,1)S(1)}, f16[512,256]{0,1:T(8,128)(2,1)S(1)}, u32[]{:S(2)}, u32[]{:S(2)}) collective-permute-start(f16[512,256]{0,1:T(8,128)(2,1)S(1)} %copy-done.34), channel_id=1, source_target_pairs={{0,8},{4,12},{8,0},{12,4},{16,24},{20,28},{24,16},{28,20},{1,9},{5... | collective-permute-start | bytes 786440 | tf_op jit(solution)/shard_map/ppermute | solution.py:17
  91.7 48.6 %collective-permute-start.18 = (f16[512,256]{0,1:T(8,128)(2,1)S(1)}, f16[512,256]{0,1:T(8,128)(2,1)S(1)}, u32[]{:S(2)}, u32[]{:S(2)}) collective-permute-start(f16[512,256]{0,1:T(8,128)(2,1)S(1)} %copy-done.34), channel_id=1, source_target_pairs={{0,16},{4,20},{8,24},{12,28},{16,0},{20,4},{24,8},{28,12},{1,17},{... | collective-permute-start | bytes 786440 | tf_op jit(solution)/shard_map/ppermute | solution.py:17
  135.6 22.1 %collective-permute-start.1 = (f16[512,256]{0,1:T(8,128)(2,1)}, f16[512,256]{0,1:T(8,128)(2,1)S(1)}, u32[]{:S(2)}, u32[]{:S(2)}) collective-permute-start(f16[512,256]{0,1:T(8,128)(2,1)} %get-tuple-element.104), channel_id=1, source_target_pairs={{0,16},{4,20},{8,24},{12,28},{16,0},{20,4},{24,8},{28,12},{1,17},{... | collective-permute-start | bytes 786440 | tf_op jit(solution)/shard_map/ppermute | solution.py:17
  137.1 23.5 %collective-permute-start.12 = (f16[512,256]{0,1:T(8,128)(2,1)S(1)}, f16[512,256]{0,1:T(8,128)(2,1)S(1)}, u32[]{:S(2)}, u32[]{:S(2)}) collective-permute-start(f16[512,256]{0,1:T(8,128)(2,1)S(1)} %copy-done.33), channel_id=1, source_target_pairs={{0,8},{4,12},{8,0},{12,4},{16,24},{20,28},{24,16},{28,20},{1,9},{5... | collective-permute-start | bytes 786440 | tf_op jit(solution)/shard_map/ppermute | solution.py:17
  138.3 24.1 %collective-permute-start.13 = (f16[512,256]{0,1:T(8,128)(2,1)S(1)}, f16[512,256]{0,1:T(8,128)(2,1)S(1)}, u32[]{:S(2)}, u32[]{:S(2)}) collective-permute-start(f16[512,256]{0,1:T(8,128)(2,1)S(1)} %copy-done.33), channel_id=1, source_target_pairs={{0,16},{4,20},{8,24},{12,28},{16,0},{20,4},{24,8},{28,12},{1,17},{... | collective-permute-start | bytes 786440 | tf_op jit(solution)/shard_map/ppermute | solution.py:17
  151.5 77.3 %collective-permute-start.116 = (f16[1024,512]{1,0:T(8,128)(2,1)}, f16[1024,512]{1,0:T(8,128)(2,1)S(1)}, u32[]{:S(2)}, u32[]{:S(2)}) collective-permute-start(f16[1024,512]{1,0:T(8,128)(2,1)} %fusion.293), channel_id=1, source_target_pairs={{1,0},{2,1},{3,2},{5,4},{6,5},{7,6},{9,8},{10,9},{11,10},{13,12},{... | collective-permute-start | bytes 3145736 | tf_op jit(solution)/shard_map/ppermute | solution.py:83
  154.1 56.9 %collective-permute-start.48 = (bf16[8,96,512]{2,1,0:T(8,128)(2,1)}, bf16[8,96,512]{2,1,0:T(8,128)(2,1)}, u32[]{:S(2)}, u32[]{:S(2)}) collective-permute-start(bf16[8,96,512]{2,1,0:T(8,128)(2,1)} %constant_dynamic-update-slice_fusion.79), channel_id=1, source_target_pairs={{1,0},{2,1},{3,2},{5,4},{6,5},{7,6},{9,8},{10,9},{11,10},{13,12},{... | collective-permute-start | bytes 2359304 | tf_op jit(solution)/shard_map/ppermute | solution.py:83
  157.8 22.4 %collective-permute-start.26 = (f16[2048,256]{0,1:T(8,128)(2,1)}, f16[2048,256]{0,1:T(8,128)(2,1)S(1)}, u32[]{:S(2)}, u32[]{:S(2)}) collective-permute-start(f16[2048,256]{0,1:T(8,128)(2,1)} %get-tuple-element.285), channel_id=1, source_target_pairs={{0,4},{4,0},{8,12},{12,8},{16,20},{20,16},{24,28},{28,24},{1,5},{5... | collective-permute-start | bytes 3145736 | tf_op jit(solution)/shard_map/ppermute | solution.py:17
  174.1 40.5 %collective-permute-start.49 = (bf16[8,96,512]{2,1,0:T(8,128)(2,1)}, bf16[8,96,512]{2,1,0:T(8,128)(2,1)}, u32[]{:S(2)}, u32[]{:S(2)}) collective-permute-start(bf16[8,96,512]{2,1,0:T(8,128)(2,1)} %constant_dynamic-update-slice_fusion.79), channel_id=1, source_target_pairs={{0,1},{1,2},{2,3},{4,5},{5,6},{6,7},{8,9},{9,10},{10,11},{12,13},{... | collective-permute-start | bytes 2359304 | tf_op jit(solution)/shard_map/ppermute | solution.py:84
  221.2 31.9 %collective-permute-start.52 = (bf16[8,96,512]{2,1,0:T(8,128)(2,1)}, bf16[8,96,512]{2,1,0:T(8,128)(2,1)}, u32[]{:S(2)}, u32[]{:S(2)}) collective-permute-start(bf16[8,96,512]{2,1,0:T(8,128)(2,1)} %collective-permute-done.48), channel_id=1, source_target_pairs={{1,0},{2,1},{5,4},{6,5},{9,8},{10,9},{13,12},{14,13},{17,16},{18,1... | collective-permute-start | bytes 2359304 | tf_op jit(solution)/shard_map/ppermute | solution.py:83
  225.1 29.2 %collective-permute-start.50 = (bf16[8,96,512]{2,1,0:T(8,128)(2,1)}, bf16[8,96,512]{2,1,0:T(8,128)(2,1)}, u32[]{:S(2)}, u32[]{:S(2)}) collective-permute-start(bf16[8,96,512]{2,1,0:T(8,128)(2,1)} %collective-permute-done.49), channel_id=1, source_target_pairs={{1,2},{2,3},{5,6},{6,7},{9,10},{10,11},{13,14},{14,15},{17,18},{18... | collective-permute-start | bytes 2359304 | tf_op jit(solution)/shard_map/ppermute | solution.py:84
  239.5 28.2 %collective-permute-start.117 = (f16[1024,512]{1,0:T(8,128)(2,1)S(1)}, f16[1024,512]{1,0:T(8,128)(2,1)S(1)}, u32[]{:S(2)}, u32[]{:S(2)}) collective-permute-start(f16[1024,512]{1,0:T(8,128)(2,1)S(1)} %copy-done.21), channel_id=1, source_target_pairs={{0,1},{1,2},{2,3},{4,5},{5,6},{6,7},{8,9},{9,10},{10,11},{12,13},{... | collective-permute-start | bytes 3145736 | tf_op jit(solution)/shard_map/ppermute | solution.py:84
  267.6 57.6 %collective-permute-start.120 = (f16[1024,512]{1,0:T(8,128)(2,1)S(1)}, f16[1024,512]{1,0:T(8,128)(2,1)S(1)}, u32[]{:S(2)}, u32[]{:S(2)}) collective-permute-start(f16[1024,512]{1,0:T(8,128)(2,1)S(1)} %collective-permute-done.116), channel_id=1, source_target_pairs={{1,0},{2,1},{5,4},{6,5},{9,8},{10,9},{13,12},{14,13},{17,16},{18,1... | collective-permute-start | bytes 3145736 | tf_op jit(solution)/shard_map/ppermute | solution.py:83
  269.8 55.5 %collective-permute-start.118 = (f16[1024,512]{1,0:T(8,128)(2,1)S(1)}, f16[1024,512]{1,0:T(8,128)(2,1)S(1)}, u32[]{:S(2)}, u32[]{:S(2)}) collective-permute-start(f16[1024,512]{1,0:T(8,128)(2,1)S(1)} %collective-permute-done.117), channel_id=1, source_target_pairs={{1,2},{2,3},{5,6},{6,7},{9,10},{10,11},{13,14},{14,15},{17,18},{18... | collective-permute-start | bytes 3145736 | tf_op jit(solution)/shard_map/ppermute | solution.py:84
  284.9 41.2 %collective-permute-start.53 = (bf16[8,96,512]{2,1,0:T(8,128)(2,1)}, bf16[8,96,512]{2,1,0:T(8,128)(2,1)S(1)}, u32[]{:S(2)}, u32[]{:S(2)}) collective-permute-start(bf16[8,96,512]{2,1,0:T(8,128)(2,1)} %collective-permute-done.52), channel_id=1, source_target_pairs={{1,0},{5,4},{9,8},{13,12},{17,16},{21,20},{25,24},{29,28}} | collective-permute-start | bytes 2359304 | tf_op jit(solution)/shard_map/ppermute | solution.py:83
  303.2 24.3 %collective-permute-start.51 = (bf16[8,96,512]{2,1,0:T(8,128)(2,1)}, bf16[8,96,512]{2,1,0:T(8,128)(2,1)S(1)}, u32[]{:S(2)}, u32[]{:S(2)}) collective-permute-start(bf16[8,96,512]{2,1,0:T(8,128)(2,1)} %collective-permute-done.50), channel_id=1, source_target_pairs={{2,3},{6,7},{10,11},{14,15},{18,19},{22,23},{26,27},{30,31}} | collective-permute-start | bytes 2359304 | tf_op jit(solution)/shard_map/ppermute | solution.py:84
  306.4 31.0 %collective-permute-start.58 = (bf16[1536,256]{1,0:T(8,128)(2,1)S(1)}, bf16[1536,256]{1,0:T(8,128)(2,1)S(1)}, u32[]{:S(2)}, u32[]{:S(2)}) collective-permute-start(bf16[1536,256]{1,0:T(8,128)(2,1)S(1)} %get-tuple-element.301), channel_id=1, source_target_pairs={{0,4},{4,0},{8,12},{12,8},{16,20},{20,16},{24,28},{28,24},{1,5},{5... | collective-permute-start | bytes 2359304 | tf_op jit(solution)/shard_map/ppermute | solution.py:17
  325.3 14.2 %collective-permute-start.103 = (bf16[1536,256]{1,0:T(8,128)(2,1)S(1)}, bf16[1536,256]{1,0:T(8,128)(2,1)S(1)}, u32[]{:S(2)}, u32[]{:S(2)}) collective-permute-start(bf16[1536,256]{1,0:T(8,128)(2,1)S(1)} %get-tuple-element.297), channel_id=1, source_target_pairs={{0,4},{4,0},{8,12},{12,8},{16,20},{20,16},{24,28},{28,24},{1,5},{5... | collective-permute-start | bytes 2359304 | tf_op jit(solution)/shard_map/ppermute | solution.py:17
  325.3 14.9 %collective-permute-start.88 = (bf16[1536,256]{1,0:T(8,128)(2,1)S(1)}, bf16[1536,256]{1,0:T(8,128)(2,1)S(1)}, u32[]{:S(2)}, u32[]{:S(2)}) collective-permute-start(bf16[1536,256]{1,0:T(8,128)(2,1)S(1)} %get-tuple-element.293), channel_id=1, source_target_pairs={{0,4},{4,0},{8,12},{12,8},{16,20},{20,16},{24,28},{28,24},{1,5},{5... | collective-permute-start | bytes 2359304 | tf_op jit(solution)/shard_map/ppermute | solution.py:17
  326.1 16.8 %collective-permute-start.73 = (bf16[1536,256]{1,0:T(8,128)(2,1)S(1)}, bf16[1536,256]{1,0:T(8,128)(2,1)S(1)}, u32[]{:S(2)}, u32[]{:S(2)}) collective-permute-start(bf16[1536,256]{1,0:T(8,128)(2,1)S(1)} %get-tuple-element.289), channel_id=1, source_target_pairs={{0,4},{4,0},{8,12},{12,8},{16,20},{20,16},{24,28},{28,24},{1,5},{5... | collective-permute-start | bytes 2359304 | tf_op jit(solution)/shard_map/ppermute | solution.py:17
  327.5 20.8 %collective-permute-start.40 = (bf16[2048,256]{1,0:T(8,128)(2,1)S(1)}, bf16[2048,256]{1,0:T(8,128)(2,1)S(1)}, u32[]{:S(2)}, u32[]{:S(2)}) collective-permute-start(bf16[2048,256]{1,0:T(8,128)(2,1)S(1)} %get-tuple-element.269), channel_id=1, source_target_pairs={{0,4},{4,0},{8,12},{12,8},{16,20},{20,16},{24,28},{28,24},{1,5},{5... | collective-permute-start | bytes 3145736 | tf_op jit(solution)/shard_map/ppermute | solution.py:17
  337.4 21.0 %collective-permute-start.98 = (bf16[2048,256]{1,0:T(8,128)(2,1)S(1)}, bf16[2048,256]{1,0:T(8,128)(2,1)S(1)}, u32[]{:S(2)}, u32[]{:S(2)}) collective-permute-start(bf16[2048,256]{1,0:T(8,128)(2,1)S(1)} %get-tuple-element.261), channel_id=1, source_target_pairs={{0,4},{4,0},{8,12},{12,8},{16,20},{20,16},{24,28},{28,24},{1,5},{5... | collective-permute-start | bytes 3145736 | tf_op jit(solution)/shard_map/ppermute | solution.py:17
  339.5 25.2 %collective-permute-start.83 = (bf16[2048,256]{1,0:T(8,128)(2,1)S(1)}, bf16[2048,256]{1,0:T(8,128)(2,1)S(1)}, u32[]{:S(2)}, u32[]{:S(2)}) collective-permute-start(bf16[2048,256]{1,0:T(8,128)(2,1)S(1)} %get-tuple-element.253), channel_id=1, source_target_pairs={{0,4},{4,0},{8,12},{12,8},{16,20},{20,16},{24,28},{28,24},{1,5},{5... | collective-permute-start | bytes 3145736 | tf_op jit(solution)/shard_map/ppermute | solution.py:17
  340.1 32.7 %collective-permute-start.68 = (bf16[2048,256]{1,0:T(8,128)(2,1)S(1)}, bf16[2048,256]{1,0:T(8,128)(2,1)S(1)}, u32[]{:S(2)}, u32[]{:S(2)}) collective-permute-start(bf16[2048,256]{1,0:T(8,128)(2,1)S(1)} %get-tuple-element.245), channel_id=1, source_target_pairs={{0,4},{4,0},{8,12},{12,8},{16,20},{20,16},{24,28},{28,24},{1,5},{5... | collective-permute-start | bytes 3145736 | tf_op jit(solution)/shard_map/ppermute | solution.py:17
  342.9 35.9 %collective-permute-start.121 = (f16[1024,512]{1,0:T(8,128)(2,1)S(1)}, f16[1024,512]{1,0:T(8,128)(2,1)S(1)}, u32[]{:S(2)}, u32[]{:S(2)}) collective-permute-start(f16[1024,512]{1,0:T(8,128)(2,1)S(1)} %collective-permute-done.120), channel_id=1, source_target_pairs={{1,0},{5,4},{9,8},{13,12},{17,16},{21,20},{25,24},{29,28}} | collective-permute-start | bytes 3145736 | tf_op jit(solution)/shard_map/ppermute | solution.py:83
  348.3 30.8 %collective-permute-start.119 = (f16[1024,512]{1,0:T(8,128)(2,1)S(1)}, f16[1024,512]{1,0:T(8,128)(2,1)S(1)}, u32[]{:S(2)}, u32[]{:S(2)}) collective-permute-start(f16[1024,512]{1,0:T(8,128)(2,1)S(1)} %collective-permute-done.118), channel_id=1, source_target_pairs={{2,3},{6,7},{10,11},{14,15},{18,19},{22,23},{26,27},{30,31}} | collective-permute-start | bytes 3145736 | tf_op jit(solution)/shard_map/ppermute | solution.py:84
  358.4 33.8 %collective-permute-start.59 = (f16[128,4096]{1,0:T(8,128)(2,1)}, f16[128,4096]{1,0:T(8,128)(2,1)}, u32[]{:S(2)}, u32[]{:S(2)}) collective-permute-start(f16[128,4096]{1,0:T(8,128)(2,1)} %fusion.25), channel_id=1, source_target_pairs={{0,4},{4,0},{8,12},{12,8},{16,20},{20,16},{24,28},{28,24},{1,5},{5... | collective-permute-start | bytes 3145736 | tf_op jit(solution)/shard_map/ppermute | solution.py:17
  364.7 33.2 %collective-permute-start.104 = (f16[128,4096]{1,0:T(8,128)(2,1)}, f16[128,4096]{1,0:T(8,128)(2,1)S(1)}, u32[]{:S(2)}, u32[]{:S(2)}) collective-permute-start(f16[128,4096]{1,0:T(8,128)(2,1)} %fusion.28), channel_id=1, source_target_pairs={{0,4},{4,0},{8,12},{12,8},{16,20},{20,16},{24,28},{28,24},{1,5},{5... | collective-permute-start | bytes 3145736 | tf_op jit(solution)/shard_map/ppermute | solution.py:17
  372.8 33.2 %collective-permute-start.89 = (f16[128,4096]{1,0:T(8,128)(2,1)}, f16[128,4096]{1,0:T(8,128)(2,1)S(1)}, u32[]{:S(2)}, u32[]{:S(2)}) collective-permute-start(f16[128,4096]{1,0:T(8,128)(2,1)} %fusion.27), channel_id=1, source_target_pairs={{0,4},{4,0},{8,12},{12,8},{16,20},{20,16},{24,28},{28,24},{1,5},{5... | collective-permute-start | bytes 3145736 | tf_op jit(solution)/shard_map/ppermute | solution.py:17
  378.8 31.5 %collective-permute-start.74 = (f16[128,4096]{1,0:T(8,128)(2,1)}, f16[128,4096]{1,0:T(8,128)(2,1)S(1)}, u32[]{:S(2)}, u32[]{:S(2)}) collective-permute-start(f16[128,4096]{1,0:T(8,128)(2,1)} %fusion.26), channel_id=1, source_target_pairs={{0,4},{4,0},{8,12},{12,8},{16,20},{20,16},{24,28},{28,24},{1,5},{5... | collective-permute-start | bytes 3145736 | tf_op jit(solution)/shard_map/ppermute | solution.py:17
  396.6 17.8 %collective-permute-start.62 = (f16[16,4096]{1,0:T(8,128)(2,1)S(1)}, f16[16,4096]{1,0:T(8,128)(2,1)S(1)}, u32[]{:S(2)}, u32[]{:S(2)}) collective-permute-start(f16[16,4096]{1,0:T(8,128)(2,1)S(1)} %get-tuple-element.87), channel_id=1, source_target_pairs={{0,8},{4,12},{8,0},{12,4},{16,24},{20,28},{24,16},{28,20},{1,9},{5... | collective-permute-start | bytes 393224 | tf_op jit(solution)/shard_map/ppermute | solution.py:17
  396.7 18.2 %collective-permute-start.60 = (f16[16,4096]{1,0:T(8,128)(2,1)S(1)}, f16[16,4096]{1,0:T(8,128)(2,1)S(1)}, u32[]{:S(2)}, u32[]{:S(2)}) collective-permute-start(f16[16,4096]{1,0:T(8,128)(2,1)S(1)} %get-tuple-element.89), channel_id=1, source_target_pairs={{0,16},{4,20},{8,24},{12,28},{16,0},{20,4},{24,8},{28,12},{1,17},{... | collective-permute-start | bytes 393224 | tf_op jit(solution)/shard_map/ppermute | solution.py:17
  400.8 15.0 %collective-permute-start.107 = (f16[16,4096]{1,0:T(8,128)(2,1)S(1)}, f16[16,4096]{1,0:T(8,128)(2,1)S(1)}, u32[]{:S(2)}, u32[]{:S(2)}) collective-permute-start(f16[16,4096]{1,0:T(8,128)(2,1)S(1)} %get-tuple-element.81), channel_id=1, source_target_pairs={{0,8},{4,12},{8,0},{12,4},{16,24},{20,28},{24,16},{28,20},{1,9},{5... | collective-permute-start | bytes 393224 | tf_op jit(solution)/shard_map/ppermute | solution.py:17
  417.2 25.5 %collective-permute-start.61 = (f16[32,4096]{1,0:T(8,128)(2,1)S(1)}, f16[32,4096]{1,0:T(8,128)(2,1)S(1)}, u32[]{:S(2)}, u32[]{:S(2)}) collective-permute-start(f16[32,4096]{1,0:T(8,128)(2,1)S(1)} %pad_maximum_fusion.9), channel_id=1, source_target_pairs={{0,8},{4,12},{8,0},{12,4},{16,24},{20,28},{24,16},{28,20},{1,9},{5... | collective-permute-start | bytes 786440 | tf_op jit(solution)/shard_map/ppermute | solution.py:17
  418.4 26.2 %collective-permute-start.63 = (f16[32,4096]{1,0:T(8,128)(2,1)S(1)}, f16[32,4096]{1,0:T(8,128)(2,1)S(1)}, u32[]{:S(2)}, u32[]{:S(2)}) collective-permute-start(f16[32,4096]{1,0:T(8,128)(2,1)S(1)} %pad_maximum_fusion.10), channel_id=1, source_target_pairs={{0,16},{4,20},{8,24},{12,28},{16,0},{20,4},{24,8},{28,12},{1,17},{... | collective-permute-start | bytes 786440 | tf_op jit(solution)/shard_map/ppermute | solution.py:17
  418.9 28.1 %collective-permute-start.106 = (f16[32,4096]{1,0:T(8,128)(2,1)S(1)}, f16[32,4096]{1,0:T(8,128)(2,1)S(1)}, u32[]{:S(2)}, u32[]{:S(2)}) collective-permute-start(f16[32,4096]{1,0:T(8,128)(2,1)S(1)} %pad_maximum_fusion.15), channel_id=1, source_target_pairs={{0,8},{4,12},{8,0},{12,4},{16,24},{20,28},{24,16},{28,20},{1,9},{5... | collective-permute-start | bytes 786440 | tf_op jit(solution)/shard_map/ppermute | solution.py:17
  419.8 30.5 %collective-permute-start.108 = (f16[32,4096]{1,0:T(8,128)(2,1)S(1)}, f16[32,4096]{1,0:T(8,128)(2,1)S(1)}, u32[]{:S(2)}, u32[]{:S(2)}) collective-permute-start(f16[32,4096]{1,0:T(8,128)(2,1)S(1)} %pad_maximum_fusion.16), channel_id=1, source_target_pairs={{0,16},{4,20},{8,24},{12,28},{16,0},{20,4},{24,8},{28,12},{1,17},{... | collective-permute-start | bytes 786440 | tf_op jit(solution)/shard_map/ppermute | solution.py:17
  421.4 15.0 %collective-permute-start.91 = (f16[32,4096]{1,0:T(8,128)(2,1)S(1)}, f16[32,4096]{1,0:T(8,128)(2,1)S(1)}, u32[]{:S(2)}, u32[]{:S(2)}) collective-permute-start(f16[32,4096]{1,0:T(8,128)(2,1)S(1)} %pad_maximum_fusion.13), channel_id=1, source_target_pairs={{0,8},{4,12},{8,0},{12,4},{16,24},{20,28},{24,16},{28,20},{1,9},{5... | collective-permute-start | bytes 786440 | tf_op jit(solution)/shard_map/ppermute | solution.py:17
  444.7 53.7 %collective-permute-start.150 = (f16[32,4096]{1,0:T(8,128)(2,1)S(1)}, f16[32,4096]{1,0:T(8,128)(2,1)S(1)}, u32[]{:S(2)}, u32[]{:S(2)}) collective-permute-start(f16[32,4096]{1,0:T(8,128)(2,1)S(1)} %fusion.173), channel_id=1, source_target_pairs={{1,0},{2,1},{3,2},{5,4},{6,5},{7,6},{9,8},{10,9},{11,10},{13,12},{... | collective-permute-start | bytes 786440 | tf_op jit(solution)/shard_map/ppermute | solution.py:83
  447.0 54.0 %collective-permute-start.151 = (f16[32,4096]{1,0:T(8,128)(2,1)S(1)}, f16[32,4096]{1,0:T(8,128)(2,1)S(1)}, u32[]{:S(2)}, u32[]{:S(2)}) collective-permute-start(f16[32,4096]{1,0:T(8,128)(2,1)S(1)} %fusion.173), channel_id=1, source_target_pairs={{0,1},{1,2},{2,3},{4,5},{5,6},{6,7},{8,9},{9,10},{10,11},{12,13},{... | collective-permute-start | bytes 786440 | tf_op jit(solution)/shard_map/ppermute | solution.py:84
  450.3 52.7 %collective-permute-start.128 = (f16[32,4096]{1,0:T(8,128)(2,1)S(1)}, f16[32,4096]{1,0:T(8,128)(2,1)S(1)}, u32[]{:S(2)}, u32[]{:S(2)}) collective-permute-start(f16[32,4096]{1,0:T(8,128)(2,1)S(1)} %fusion.177), channel_id=1, source_target_pairs={{1,0},{2,1},{3,2},{5,4},{6,5},{7,6},{9,8},{10,9},{11,10},{13,12},{... | collective-permute-start | bytes 786440 | tf_op jit(solution)/shard_map/ppermute | solution.py:83
  452.6 52.3 %collective-permute-start.129 = (f16[32,4096]{1,0:T(8,128)(2,1)S(1)}, f16[32,4096]{1,0:T(8,128)(2,1)S(1)}, u32[]{:S(2)}, u32[]{:S(2)}) collective-permute-start(f16[32,4096]{1,0:T(8,128)(2,1)S(1)} %fusion.177), channel_id=1, source_target_pairs={{0,1},{1,2},{2,3},{4,5},{5,6},{6,7},{8,9},{9,10},{10,11},{12,13},{... | collective-permute-start | bytes 786440 | tf_op jit(solution)/shard_map/ppermute | solution.py:84
  527.4 14.2 %collective-permute-start.153 = (f16[32,4096]{1,0:T(8,128)(2,1)S(1)}, f16[32,4096]{1,0:T(8,128)(2,1)S(1)}, u32[]{:S(2)}, u32[]{:S(2)}) collective-permute-start(f16[32,4096]{1,0:T(8,128)(2,1)S(1)} %collective-permute-done.152), channel_id=1, source_target_pairs={{2,3},{6,7},{10,11},{14,15},{18,19},{22,23},{26,27},{30,31}} | collective-permute-start | bytes 786440 | tf_op jit(solution)/shard_map/ppermute | solution.py:84
  532.2 17.3 %collective-permute-start.133 = (f16[32,4096]{1,0:T(8,128)(2,1)S(1)}, f16[32,4096]{1,0:T(8,128)(2,1)S(1)}, u32[]{:S(2)}, u32[]{:S(2)}) collective-permute-start(f16[32,4096]{1,0:T(8,128)(2,1)S(1)} %collective-permute-done.132), channel_id=1, source_target_pairs={{1,0},{5,4},{9,8},{13,12},{17,16},{21,20},{25,24},{29,28}} | collective-permute-start | bytes 786440 | tf_op jit(solution)/shard_map/ppermute | solution.py:83
  533.0 20.7 %collective-permute-start.131 = (f16[32,4096]{1,0:T(8,128)(2,1)S(1)}, f16[32,4096]{1,0:T(8,128)(2,1)S(1)}, u32[]{:S(2)}, u32[]{:S(2)}) collective-permute-start(f16[32,4096]{1,0:T(8,128)(2,1)S(1)} %collective-permute-done.130), channel_id=1, source_target_pairs={{2,3},{6,7},{10,11},{14,15},{18,19},{22,23},{26,27},{30,31}} | collective-permute-start | bytes 786440 | tf_op jit(solution)/shard_map/ppermute | solution.py:84
  537.8 23.1 %collective-permute-start.144 = (f16[32,4096]{1,0:T(8,128)(2,1)S(1)}, f16[32,4096]{1,0:T(8,128)(2,1)S(1)}, u32[]{:S(2)}, u32[]{:S(2)}) collective-permute-start(f16[32,4096]{1,0:T(8,128)(2,1)S(1)} %collective-permute-done.143), channel_id=1, source_target_pairs={{1,0},{5,4},{9,8},{13,12},{17,16},{21,20},{25,24},{29,28}} | collective-permute-start | bytes 786440 | tf_op jit(solution)/shard_map/ppermute | solution.py:83
  538.6 23.5 %collective-permute-start.142 = (f16[32,4096]{1,0:T(8,128)(2,1)S(1)}, f16[32,4096]{1,0:T(8,128)(2,1)S(1)}, u32[]{:S(2)}, u32[]{:S(2)}) collective-permute-start(f16[32,4096]{1,0:T(8,128)(2,1)S(1)} %collective-permute-done.141), channel_id=1, source_target_pairs={{2,3},{6,7},{10,11},{14,15},{18,19},{22,23},{26,27},{30,31}} | collective-permute-start | bytes 786440 | tf_op jit(solution)/shard_map/ppermute | solution.py:84
  541.6 28.4 %collective-permute-start.166 = (f16[32,4096]{1,0:T(8,128)(2,1)S(1)}, f16[32,4096]{1,0:T(8,128)(2,1)S(1)}, u32[]{:S(2)}, u32[]{:S(2)}) collective-permute-start(f16[32,4096]{1,0:T(8,128)(2,1)S(1)} %collective-permute-done.165), channel_id=1, source_target_pairs={{1,0},{5,4},{9,8},{13,12},{17,16},{21,20},{25,24},{29,28}} | collective-permute-start | bytes 786440 | tf_op jit(solution)/shard_map/ppermute | solution.py:83
  549.5 22.0 %collective-permute-start.164 = (f16[32,4096]{1,0:T(8,128)(2,1)S(1)}, f16[32,4096]{1,0:T(8,128)(2,1)S(1)}, u32[]{:S(2)}, u32[]{:S(2)}) collective-permute-start(f16[32,4096]{1,0:T(8,128)(2,1)S(1)} %collective-permute-done.163), channel_id=1, source_target_pairs={{2,3},{6,7},{10,11},{14,15},{18,19},{22,23},{26,27},{30,31}} | collective-permute-start | bytes 786440 | tf_op jit(solution)/shard_map/ppermute | solution.py:84
  553.8 25.1 %collective-permute-start.156 = (f16[128,1024]{1,0:T(8,128)(2,1)S(1)}, f16[128,1024]{1,0:T(8,128)(2,1)S(1)}, u32[]{:S(2)}, u32[]{:S(2)}) collective-permute-start(f16[128,1024]{1,0:T(8,128)(2,1)S(1)} %get-tuple-element.318), channel_id=1, source_target_pairs={{0,8},{4,12},{8,0},{12,4},{16,24},{20,28},{24,16},{28,20},{1,9},{5... | collective-permute-start | bytes 786440 | tf_op jit(solution)/shard_map/ppermute | solution.py:17
  560.9 19.9 %collective-permute-start.157 = (f16[128,1024]{1,0:T(8,128)(2,1)S(1)}, f16[128,1024]{1,0:T(8,128)(2,1)S(1)}, u32[]{:S(2)}, u32[]{:S(2)}) collective-permute-start(f16[128,1024]{1,0:T(8,128)(2,1)S(1)} %get-tuple-element.318), channel_id=1, source_target_pairs={{0,16},{4,20},{8,24},{12,28},{16,0},{20,4},{24,8},{28,12},{1,17},{... | collective-permute-start | bytes 786440 | tf_op jit(solution)/shard_map/ppermute | solution.py:17
  562.2 19.7 %collective-permute-start.134 = (f16[128,1024]{1,0:T(8,128)(2,1)S(1)}, f16[128,1024]{1,0:T(8,128)(2,1)S(1)}, u32[]{:S(2)}, u32[]{:S(2)}) collective-permute-start(f16[128,1024]{1,0:T(8,128)(2,1)S(1)} %get-tuple-element.319), channel_id=1, source_target_pairs={{0,8},{4,12},{8,0},{12,4},{16,24},{20,28},{24,16},{28,20},{1,9},{5... | collective-permute-start | bytes 786440 | tf_op jit(solution)/shard_map/ppermute | solution.py:17
  570.0 14.2 %collective-permute-start.135 = (f16[128,1024]{1,0:T(8,128)(2,1)S(1)}, f16[128,1024]{1,0:T(8,128)(2,1)S(1)}, u32[]{:S(2)}, u32[]{:S(2)}) collective-permute-start(f16[128,1024]{1,0:T(8,128)(2,1)S(1)} %get-tuple-element.319), channel_id=1, source_target_pairs={{0,16},{4,20},{8,24},{12,28},{16,0},{20,4},{24,8},{28,12},{1,17},{... | collective-permute-start | bytes 786440 | tf_op jit(solution)/shard_map/ppermute | solution.py:17
  580.8 30.4 %collective-permute-start.167 = (f16[128,1024]{1,0:T(8,128)(2,1)}, f16[128,1024]{1,0:T(8,128)(2,1)S(1)}, u32[]{:S(2)}, u32[]{:S(2)}) collective-permute-start(f16[128,1024]{1,0:T(8,128)(2,1)} %get-tuple-element.321), channel_id=1, source_target_pairs={{0,8},{4,12},{8,0},{12,4},{16,24},{20,28},{24,16},{28,20},{1,9},{5... | collective-permute-start | bytes 786440 | tf_op jit(solution)/shard_map/ppermute | solution.py:17
  581.9 30.2 %collective-permute-start.168 = (f16[128,1024]{1,0:T(8,128)(2,1)}, f16[128,1024]{1,0:T(8,128)(2,1)}, u32[]{:S(2)}, u32[]{:S(2)}) collective-permute-start(f16[128,1024]{1,0:T(8,128)(2,1)} %get-tuple-element.321), channel_id=1, source_target_pairs={{0,16},{4,20},{8,24},{12,28},{16,0},{20,4},{24,8},{28,12},{1,17},{... | collective-permute-start | bytes 786440 | tf_op jit(solution)/shard_map/ppermute | solution.py:17
  597.1 22.9 %collective-permute-start.160 = (f16[512,1024]{1,0:T(8,128)(2,1)}, f16[512,1024]{1,0:T(8,128)(2,1)S(1)}, u32[]{:S(2)}, u32[]{:S(2)}) collective-permute-start(f16[512,1024]{1,0:T(8,128)(2,1)} %get-tuple-element.237), channel_id=1, source_target_pairs={{0,4},{4,0},{8,12},{12,8},{16,20},{20,16},{24,28},{28,24},{1,5},{5... | collective-permute-start | bytes 3145736 | tf_op jit(solution)/shard_map/ppermute | solution.py:17
  605.8 14.5 %collective-permute-start.138 = (f16[512,1024]{1,0:T(8,128)(2,1)}, f16[512,1024]{1,0:T(8,128)(2,1)}, u32[]{:S(2)}, u32[]{:S(2)}) collective-permute-start(f16[512,1024]{1,0:T(8,128)(2,1)} %get-tuple-element.233), channel_id=1, source_target_pairs={{0,4},{4,0},{8,12},{12,8},{16,20},{20,16},{24,28},{28,24},{1,5},{5... | collective-permute-start | bytes 3145736 | tf_op jit(solution)/shard_map/ppermute | solution.py:17
  (188 other events, 1697.4 us)

commit v2 on v1

v2 whole, which is shorter than its diff:
```python
import jax
import jax.numpy as jnp
from jax import lax
from jax.experimental import pallas as pl
from jax.experimental.pallas import tpu as pltpu
from jax.sharding import PartitionSpec as P

clip_ratio = 2.0
eps_power = 1e-06
cot_limit = 6.0
code_top = 30000.0
BF16 = jnp.bfloat16
F16 = jnp.float16
F32 = jnp.float32


def swap(x, mask):
    n = lax.axis_size("dp")
    return lax.ppermute(x, "dp", [(i, i ^ mask) for i in range(n)])


def relative_masks():
    half = lax.axis_size("dp") // 2
    return [(q % half) * 2 + q // half for q in range(2 * half)]


def gather_small(x):
    bit = 1
    while bit < lax.axis_size("dp") // 2:
        x = jnp.concatenate([x, swap(x, 2 * bit)], axis=0)
        bit *= 2
    return jnp.concatenate([x, swap(x, 1)], axis=0)


def after(x, *earlier):
    return lax.optimization_barrier((x,) + earlier)[0]


def first_step(x):
    return (swap(x, 2), swap(x, 4)) if lax.axis_size("dp") == 8 else ()


def second_step(x, came):
    if lax.axis_size("dp") != 8:
        bit = 1
        while bit < lax.axis_size("dp") // 2:
            x = jnp.concatenate([x, swap(x, 2 * bit)], axis=0)
            bit *= 2
        return x
    half = x.shape[0] // 2
    from_x, from_y = came
    far = [swap(from_x[:half], 4), swap(from_y[half:], 2)]
    return jnp.concatenate([x, from_x, from_y] + far, axis=0)


def trade(x, mask):
    return swap(x.astype(F16), mask).astype(F32)


def scatter_first(total):
    size = total.shape[0] // (lax.axis_size("dp") // 2)
    far = total[3 * size :]
    half = size // 2
    return trade(far[:half], 2), trade(far[half:], 4)


def scatter_last(total, came):
    chips = lax.axis_size("dp") // 2
    if chips != 4:
        bit = chips // 2
        while bit:
            half = total.shape[0] // 2
            total = total[:half] + trade(total[half:], 2 * bit)
            bit //= 2
        return total
    via_x, via_y = came
    size = total.shape[0] // chips
    half = size // 2
    own, to_x, to_y = (total[i * size : (i + 1) * size] for i in range(3))
    to_y = jnp.concatenate([to_y[:half] + via_x, to_y[half:]], axis=0)
    to_x = jnp.concatenate([to_x[:half], to_x[half:] + via_y], axis=0)
    return own + trade(to_x, 2) + trade(to_y, 4)


def exchange_steps(x):
    shape = x.shape
    n = shape[0]
    bits = n.bit_length() - 1

    def halve(x, axis):
        stay, go = jnp.split(x, 2, axis=axis)
        return jnp.concatenate([stay, swap(go, 1 if axis == 0 else n >> axis)], axis=axis)

    x = yield halve(x.reshape((2,) * bits + shape[1:]), 0)
    if bits != 3:
        x = yield halve(x, 1)
        for axis in range(2, bits):
            x = halve(x, axis)
        yield x.reshape(shape)
        return
    upper, lower = jnp.split(x, 2, axis=3)
    upper, lower = yield (halve(upper, 1), halve(lower, 2))
    yield jnp.concatenate([halve(upper, 2), halve(lower, 1)], axis=3).reshape(shape)


def gather_loop(x):
    n = lax.axis_size("loop")

    def turn(r):
        return lax.ppermute(x, "loop", [(i, (i - r) % n) for i in range(n)])

    if n != 4:
        return [x] + [turn(r) for r in range(1, n)]
    me = lax.axis_index("loop")
    after_me, before_me = turn(1), turn(3)
    across = jnp.where(me == 1, after_me, jnp.where(me == 2, before_me, x))
    across = lax.ppermute(across, "loop", [(3, 1), (0, 2), (1, 0), (2, 3)])
    return [x, after_me, across, before_me]


def sum_loop(x):
    n = lax.axis_size("loop")
    bit = 1
    while bit < n:
        x = x + lax.ppermute(x, "loop", [(i, i ^ bit) for i in range(n)])
        bit *= 2
    return x


def dot(a, b, ca, cb):
    return lax.dot_general(a, b, (((ca,), (cb,)), ((), ())), preferred_element_type=F32)


def split(x):
    high = lax.reduce_precision(x, 8, 7)
    return high.astype(BF16), (x - high).astype(BF16)


def half_code(x, scale):
    return lax.reduce_precision(x * scale, 5, 10)


def ordered_call(body, order, grid, ins, in_specs, outs, out_specs):
    return pl.pallas_call(
        body,
        out_shape=outs,
        grid_spec=pltpu.PrefetchScalarGridSpec(
            num_scalar_prefetch=1, grid=grid, in_specs=in_specs, out_specs=out_specs
        ),
        compiler_params=pltpu.CompilerParams(vmem_limit_bytes=32 * 1024 * 1024),
    )(order, *ins)


def lay_both(order, tokens, proj_weight, row_block):
    tok_rows, feat_width = tokens.shape
    outs = proj_weight.shape[1]

    def body(order_ref, tok_ref, weight_ref, placed_ref, plain_ref):
        turned = weight_ref[...].T
        for ref in (placed_ref, plain_ref):
            ref[:tok_rows] = tok_ref[...]
            ref[tok_rows:] = turned

    shape = (tok_rows + outs, feat_width)
    block = (tok_rows + outs, row_block)
    return ordered_call(
        body,
        order,
        (feat_width // row_block,),
        (tokens, proj_weight),
        [
            pl.BlockSpec((tok_rows, row_block), lambda q, o: (0, o[q])),
            pl.BlockSpec((row_block, outs), lambda q, o: (o[q], 0)),
        ],
        [jax.ShapeDtypeStruct(shape, BF16)] * 2,
        [pl.BlockSpec(block, lambda q, o: (0, q)), pl.BlockSpec(block, lambda q, o: (0, o[q]))],
    )


def lay_columns(order, x, live, width):
    def body(order_ref, x_ref, live_ref, out_ref):
        out_ref[...] = (x_ref[...].astype(F32) * live_ref[...]).astype(out_ref.dtype)

    rows, cols = x.shape
    return ordered_call(
        body,
        order,
        (cols // width,),
        (x, live),
        [
            pl.BlockSpec((rows, width), lambda q, o: (0, o[q])),
            pl.BlockSpec((rows, 1), lambda q, o: (0, 0)),
        ],
        jax.ShapeDtypeStruct(x.shape, x.dtype),
        pl.BlockSpec((rows, width), lambda q, o: (0, q)),
    )


def plain_call(body, grid, ins, in_specs, out, out_spec, flops, scratch=()):
    size = sum(x.size * x.dtype.itemsize for x in ins) + out.size * out.dtype.itemsize
    return pl.pallas_call(
        body,
        out_shape=out,
        grid=grid,
        in_specs=in_specs,
        out_specs=out_spec,
        scratch_shapes=scratch,
        compiler_params=pltpu.CompilerParams(vmem_limit_bytes=30 * 1024 * 1024),
        cost_estimate=pl.CostEstimate(flops=flops, bytes_accessed=size, transcendentals=0),
    )(*ins)


def cross_rows(scale, stacked, terms):
    (near_high, near_low), (away_high, away_low) = terms
    rows, depth = stacked.shape[0] // 2, stacked.shape[1]
    cols = near_high.shape[1]
    wide = min(cols, 256)
    half = depth // 2

    def body(scale_ref, rows_ref, nh_ref, nl_ref, ah_ref, al_ref, out_ref):
        wide_part = dot(rows_ref[:, :half], nh_ref[...], 1, 0)
        wide_part += dot(rows_ref[:, half:], ah_ref[...], 1, 0)
        total = wide_part[:rows] + wide_part[rows:]
        total += dot(rows_ref[:rows, :half], nl_ref[...], 1, 0)
        total += dot(rows_ref[:rows, half:], al_ref[...], 1, 0)
        out_ref[...] = total * scale_ref[0, 0]

    panel = pl.BlockSpec((half, wide), lambda j: (0, j))
    return plain_call(
        body,
        (cols // wide,),
        (scale, stacked, near_high, near_low, away_high, away_low),
        [
            pl.BlockSpec(memory_space=pltpu.SMEM),
            pl.BlockSpec((2 * rows, depth), lambda j: (0, 0)),
        ]
        + [panel] * 4,
        jax.ShapeDtypeStruct((rows, cols), F32),
        pl.BlockSpec((rows, wide), lambda j: (0, j)),
        6 * rows * depth * cols,
    )


def add_product(base, factor, levels, chunk, rows, terms):
    (near_high, near_low), (away_high, away_low) = terms
    depth, cols = near_high.shape
    height = base.shape[0]
    loops = rows[0].shape[0]
    wide = min(cols, 256)
    places = lax.axis_size("dp") // 2
    part = depth // loops

    def body(factor_ref, level_ref, base_ref, rh_ref, rl_ref, nh_ref, nl_ref, ah_ref, al_ref, out_ref, kept):
        @pl.when(pl.program_id(0) == 0)
        def _():
            for term, ref in enumerate((rh_ref, rl_ref)):
                for r in range(loops):
                    for h in range(2):
                        kept[term, h, :, r * part : (r + 1) * part] = ref[
                            level_ref[r], :, h * part : (h + 1) * part
                        ]

        def by_level(ref):
            x = ref[...].reshape(places, loops, part // places, wide)
            return jnp.concatenate([x[q, r] for r in range(loops) for q in range(places)], axis=0)

        total = 0.0
        for h, (high_ref, low_ref) in enumerate(((nh_ref, nl_ref), (ah_ref, al_ref))):
            high, low = by_level(high_ref), by_level(low_ref)
            total += dot(kept[0, h], high, 1, 0)
            total += dot(kept[1, h], high, 1, 0)
            total += dot(kept[0, h], low, 1, 0)
        out_ref[...] = base_ref[...] + total * factor_ref[0, 0]

    flat = pl.BlockSpec((height, wide), lambda j: (0, j))
    panel = pl.BlockSpec((depth, wide), lambda j: (0, j))
    strip = pl.BlockSpec((loops, height, 2 * part), lambda j: (0, 0, chunk))
    scalars = pl.BlockSpec(memory_space=pltpu.SMEM)
    return plain_call(
        body,
        (cols // wide,),
        (factor, levels, base, *rows, near_high, near_low, away_high, away_low),
        [scalars, scalars, flat, strip, strip] + [panel] * 4,
        jax.ShapeDtypeStruct(base.shape, F32),
        flat,
        12 * height * depth * cols,
        [pltpu.VMEM((2, 2, height, depth), BF16)],
    )


def on_device(tokens, cotangent, proj_weight, rotation, doc_lengths):
    tok_rows, feat_width = tokens.shape
    slot_count = doc_lengths.shape[0]
    slot_len = tok_rows // slot_count
    n, loops = lax.axis_size("dp"), lax.axis_size("loop")
    half = n // 2
    me, level = lax.axis_index("dp"), lax.axis_index("loop")
    place = (me & 1) * half + (me >> 1)
    masks = relative_masks()
    order = jnp.bitwise_xor(me, jnp.array(masks, jnp.int32))
    places = jnp.bitwise_xor(place, jnp.arange(n, dtype=jnp.int32))
    row_block, panel = rotation.shape
    out_block = proj_weight.shape[1]
    all_tokens, all_outs = tok_rows * n, out_block * n
    chunks = max(1, panel // (n * 64))
    wide = panel // chunks
    sub = wide // n

    rot_top = jnp.maximum(jnp.max(jnp.abs(rotation)), 1e-30)
    rot_power = jnp.floor(14.5 - jnp.log2(rot_top))
    rot_scale, rot_unit = jnp.exp2(rot_power), jnp.exp2(-rot_power)
    rot_round = lax.reduce_precision(rotation, 8, 7)
    code = half_code(rotation, rot_scale)
    inner = half_code(rot_round + 0.75 * (rotation - rot_round), rot_scale)
    read = code * rot_unit
    kept = (lax.reduce_precision(read * (1 + 1e-6), 8, 7) == rot_round) & (
        lax.reduce_precision(read * (1 - 1e-6), 8, 7) == rot_round
    )
    rot_code = jnp.where(kept, code, inner).astype(F16)
    rot_units = jnp.full((128,), rot_unit)
    bit = 1
    while bit < half:
        rot_units = jnp.concatenate([rot_units, swap(rot_units, 2 * bit)], axis=0)
        bit *= 2
    rot_code = after(rot_code, rot_units)
    rot_units = jnp.concatenate([rot_units, swap(rot_units, 1)], axis=0)
    rot_units = rot_units.reshape(2, half, 1, 128)[:, :, :, :1]
    tokens, cotangent, proj_weight = after((tokens, cotangent, proj_weight), rot_code)
    rot_came = first_step(rot_code)

    def decode(part, units):
        part = part.reshape(half, row_block, panel).astype(F32) * units
        return split(part.reshape(half * row_block, panel))

    positions = jnp.arange(tok_rows, dtype=jnp.int32)
    slot_match = (positions // slot_len)[:, None] == jnp.arange(slot_count, dtype=jnp.int32)[
        None, :
    ]
    row_lengths = jnp.sum(jnp.where(slot_match, doc_lengths[None, :], 0), axis=1)
    live_rows = positions % slot_len < row_lengths
    masked = lay_columns(order, cotangent, live_rows.astype(F32)[:, None], out_block)
    both, both_plain = lay_both(order, tokens, proj_weight, row_block)
    cuts = masked.reshape(tok_rows, n, out_block).transpose(1, 0, 2)
    cols = jnp.arange(panel, dtype=jnp.int32)
    source = cols - cols % wide + (((cols % wide) // sub) ^ place) * sub + cols % sub
    shuffle = (cols[:, None] == source[None, :]).astype(BF16)
    rows_terms = [
        dot(x, shuffle, 1, 0).astype(BF16) for x in split(after(rotation, tokens))
    ]
    cuts_way = exchange_steps(cuts)
    cuts = next(cuts_way)
    rot_came = after(rot_came, both, cuts, *rows_terms)
    rows_terms = [lax.all_gather(x, "loop", axis=0) for x in rows_terms]
    rot_near = second_step(rot_code, rot_came)
    rot_away = swap(rot_near, 1)
    rot_terms = [decode(rot_near, rot_units[0])]
    near_part = dot(both[:, : feat_width // 2], rot_terms[0][0], 1, 0)
    cuts = cuts_way.send(after(cuts, *rot_came))

    half_feat, half_out = feat_width // 2, all_outs // 2
    rot_terms.append(decode(after(rot_away, near_part, cuts), rot_units[1]))
    cuts = cuts_way.send(cuts)
    cot_owned = cuts.reshape(2, half * tok_rows, out_block)
    rotated = near_part + dot(both[:, half_feat:], rot_terms[1][0], 1, 0)
    acts_raw, mixed_raw = rotated[:tok_rows].astype(BF16), rotated[tok_rows:].astype(BF16)
    acts_came, mixed_came = first_step(acts_raw), first_step(mixed_raw)
    power = after(jnp.sum(rotated * rotated, axis=1), acts_raw, mixed_raw)
    power = sum_loop(power)
    tokens, proj_weight, rotation = after((tokens, proj_weight, rotation), acts_raw, mixed_raw)
    limit = clip_ratio * jnp.sqrt(power / feat_width + eps_power)
    tok_top = jnp.max(jnp.abs(tokens), axis=1).astype(F32)
    weight_top = jnp.max(jnp.abs(proj_weight), axis=0).astype(F32)
    sizes = [
        jnp.sum(limit[tok_rows:] ** 2),
        jnp.sum(limit[:tok_rows] ** 2),
        jnp.sum(tok_top**2),
        jnp.sum(weight_top**2),
        jnp.max(jnp.sum(rotation**2, axis=0)),
    ]
    sizes = jnp.concatenate([jnp.stack(sizes), jnp.zeros((128 - len(sizes),), F32)])
    told = gather_small(after(jnp.concatenate([limit, sizes]), *acts_came)).reshape(2, half, -1)
    limits = told[:, :, : limit.shape[0]].astype(BF16)
    acts_came = after(acts_came, cuts, rows_terms[0])
    acts_near = second_step(acts_raw, acts_came)
    acts_away = swap(acts_near, 1)
    mixed_came = after(mixed_came, acts_near, told)
    mixed_near = second_step(mixed_raw, mixed_came)
    mixed_away = swap(mixed_near, 1)
    norms = jnp.sqrt(n * jnp.max(told[:, :, limit.shape[0] :], axis=(0, 1)))
    bound = cot_limit * all_outs**0.5 * (norms[0] * norms[2] + norms[1] * norms[3])
    grad_scale = code_top / jnp.clip(1.02 * bound, 1e-30, 3e38)
    cross_scale = 0.9 / (feat_width**0.5 * jnp.maximum(norms[4], 1e-15))

    shuffle = shuffle[:wide, :wide]
    to_code = grad_scale / jnp.sqrt(F32(all_tokens))

    acts_limit = limits[:, :, :tok_rows].reshape(2, half * tok_rows, 1)
    mixed_limit = limits[:, :, tok_rows:].reshape(2, half * out_block, 1)

    def clip(x, top):
        return jnp.clip(x, -top, top)

    acts_q = [clip(x, top) for x, top in zip((acts_near, acts_away), acts_limit)]
    grad_mixed = sum(dot(x, y, 0, 0) for x, y in zip(cot_owned, acts_q)).astype(BF16)
    mixed_near, mixed_away = after((mixed_near, mixed_away), grad_mixed, rows_terms[1])
    mixed_q = [clip(x, top) for x, top in zip((mixed_near, mixed_away), mixed_limit)]
    grad_acts = sum(
        dot(masked[:, h * half_out : (h + 1) * half_out], mixed_q[h], 1, 0) for h in range(2)
    ).astype(BF16)
    pairs = jnp.concatenate([grad_acts, grad_mixed], axis=0)

    totals, strips = [], []
    for c in range(chunks):
        pair = pairs[:, c * wide : (c + 1) * wide]
        pair = jnp.dot(pair, shuffle, preferred_element_type=F32).astype(BF16)
        away = (dot(pair[:, wide // 2 :], both_plain, 0, 0) * to_code).astype(F16)
        near = dot(pair[:, : wide // 2], both_plain, 0, 0) * to_code
        totals.append(near + swap(away, 1).astype(F32))
    for c in range(chunks):
        total = after(totals[c], *came) if c else totals[c]
        came = scatter_first(total) if n == 8 else ()
        strip = scatter_last(total, came)
        strip = lay_columns(order, strip, jnp.ones((sub, 1), F32), row_block).astype(F16)
        strips.append(strip)

    strip = jnp.concatenate(strips, axis=0)
    blocks = strip.reshape(chunks * sub, n, row_block).transpose(1, 0, 2)
    blocks_way = exchange_steps(blocks)
    blocks = blocks_way.send(blocks_way.send(next(blocks_way)))
    blocks = jnp.concatenate(
        [lax.dynamic_slice_in_dim(blocks, place ^ q, 1, 0) for q in range(n)], axis=0
    )
    gradient = blocks.reshape(n, chunks, sub, row_block).transpose(1, 0, 2, 3)
    unit = 1.0 / grad_scale
    result = after(gradient.reshape(panel, row_block).astype(F32) * unit, strip).T
    factor = -(unit / cross_scale).reshape(1, 1)

    levels = (level + jnp.arange(loops, dtype=jnp.int32)) % loops

    cross_pairs = []
    for c in range(chunks):
        strip = after(strips[c], gradient) if c else strips[c]
        rows = jnp.concatenate(gather_loop(strip), axis=0)
        if c == 0:
            rows, result = after((rows, result), gradient)
        else:
            rows = after(rows, cross_near)
        stacked = jnp.concatenate(split(rows.astype(F32)), axis=0)
        cross = cross_rows(cross_scale.reshape(1, 1), stacked, rot_terms).astype(F16)
        cross_near = second_step(cross, first_step(cross))
        cross_pairs.append((cross_near, swap(cross_near, 1)))
    for c, pair in enumerate(cross_pairs):
        if c:
            pair = after(pair, result)
        terms = [split(x.astype(F32)) for x in pair]
        result = add_product(result, factor, levels, c, rows_terms, terms)
    return result


def solution(mesh):
    in_specs = (P("dp", None), P("dp", None), P(None, "dp"), P("dp", "loop"), P("dp"))
    out_specs = P("dp", "loop")
    return jax.shard_map(
        on_device, mesh=mesh, in_specs=in_specs, out_specs=out_specs, check_vma=False
    )
```

time: 655 us -> 444 us (0.68)
  the two profiles are of different devices: /device:TPU:17 before, /device:TPU:0 now
where the time goes in v2:
time: 444 us; the launch traced here: 437 us
  waiting for transfers between devices  149 us (34%)
  local copies, waits for them, and re-layouts  73.7 us (17%)
  starting transfers between devices  59.5 us (13%)
  Pallas kernels  48.2 us (11%)
  other arithmetic  45.8 us (10%)
  matrix products  41.9 us (9%)
  between operations  18.8 us (4%)
    ppermute x51, waiting for transfers between devices, swap(): return lax.ppermute(x, 'dp', [(i, i ^ mask) for i in range(n)])  126 us
    ppermute x51, starting transfers between devices, swap(): return lax.ppermute(x, 'dp', [(i, i ^ mask) for i in range(n)])  45.5 us
    unnamed x113, local copies, waits for them, and re-layouts  42.1 us
    dot_general x12, matrix products, dot(): lax.dot_general(a, b, (((ca,), (cb,)), ((), ())), preferred_element_type=...  40.5 us
    pallas_call x4, Pallas kernels, plain_call(): pl.pallas_call(body, out_shape=out, grid=grid, in_specs=in_specs, out_spe...  39.2 us
    ppermute x4, waiting for transfers between devices, turn(): return lax.ppermute(x, 'loop', [(i, (i - r) % n) for i in range(n)])  15.3 us
    convert_element_type x8, other arithmetic, split(): return (high.astype(BF16), (x - high).astype(BF16))  14.7 us
    pallas_call x4, Pallas kernels, ordered_call(): pl.pallas_call(body, out_shape=outs, grid_spec=pltpu.PrefetchScalarGridSp...  8.98 us
  transfers between devices with their start and end apart: 61, of which 37 were waited for; matrix products, arithmetic and copies ran while one was open for 28% of the time, Pallas kernels for 6%

profile of v2, /device:TPU:0, one launch (start us, length us, event | category | flops | bytes accessed | tf_op | source)
XLA Modules:
  0.0 437.3 jit_solution(2712719719046470038)
XLA Ops:
  6.5 2.5 abs_reduce_fusion.2
  9.8 3.0 collective-permute-start
  12.8 4.0 fusion.32
  18.4 2.0 collective-permute-done.1
  20.5 2.3 fusion.50
  25.4 2.2 shard_map.65
  31.6 2.0 collective-permute-start.3
  35.1 3.8 shard_map.64
  39.0 2.9 copy-done
  41.9 2.9 copy-done.14
  44.9 2.3 fusion.51
  47.2 3.9 pad_maximum_fusion.2
  51.0 6.4 %collective-permute-done.2 = f16[512,1024]{1,0:T(8,128)(2,1)} collective-permute-done((f16[512,1024]{1,0:T(8,128)(2,1)}, f16[512,1024]{1,0:T(8,128)(2,1)}, u32[]{:S(2)}, u32[]{:S(2)}) %collective-permute-start.2) | collective-permute-done | bytes 1048608 | tf_op jit(solution)/shard_map/ppermute | solution.py:19
  63.1 2.6 constant_dynamic-update-slice_fusion.4
  65.7 2.5 constant_dynamic-update-slice_fusion.3
  68.2 2.5 constant_dynamic-update-slice_fusion.2
  76.1 5.3 %collective-permute-done.7 = f32[512]{0:T(512)S(1)} collective-permute-done((f32[512]{0:T(512)S(1)}, f32[512]{0:T(512)S(1)}, u32[]{:S(2)}, u32[]{:S(2)}) %collective-permute-start.7) | collective-permute-done | bytes 2080 | tf_op jit(solution)/shard_map/ppermute | solution.py:19
  81.7 4.6 %fusion = (bf16[2048,1024]{1,0:T(8,128)(2,1)}, bf16[2048,1024]{1,0:T(8,128)(2,1)S(1)}) fusion(f16[2048,1024]{1,0:T(8,128)(2,1)} %constant_dynamic-update-slice_fusion, f32[2048]{0:T(1024)S(1)} %bitcast.82), kind=kLoop, calls=%fused_computation.4 | loop fusion | flops 12582912 | bytes 12591104 | tf_op jit(solution)/shard_map/convert_element_type | solution.py:136
  86.2 7.6 %fusion.18 = f32[896,1024]{1,0:T(8,128)S(1)} fusion(bf16[2048,1024]{1,0:T(8,128)(2,1)S(1)} %get-tuple-element.74.nh_ref, bf16[896,4096]{1,0:T(8,128)(2,1)} %copy-done.14), kind=kOutput, calls=%fused_computation.47 | convolution fusion | flops 3758096384 | bytes 11534336 | tf_op jit(solution)/shard_map/dot_general | solution.py:131
  93.9 4.9 %fusion.1 = (bf16[2048,1024]{1,0:T(8,128)(2,1)}, bf16[2048,1024]{1,0:T(8,128)(2,1)S(1)}) fusion(f16[2048,1024]{1,0:T(8,128)(2,1)} %collective-permute-done.8, f32[2048]{0:T(1024)S(1)} %bitcast.81), kind=kLoop, calls=%fused_computation.5 | loop fusion | flops 12582912 | bytes 12591104 | tf_op jit(solution)/shard_map/convert_element_type | solution.py:136
  98.8 4.0 fusion.102
  114.8 2.6 collective-permute-start.12
  121.4 3.2 concatenate.120
  127.1 2.6 fusion.104
  132.0 15.0 %collective-permute-done.15 = f32[1024]{0:T(1024)S(1)} collective-permute-done((f32[1024]{0:T(1024)S(1)}, f32[1024]{0:T(1024)S(1)}, u32[]{:S(2)}, u32[]{:S(2)}) %collective-permute-start.15) | collective-permute-done | bytes 4128 | tf_op jit(solution)/shard_map/ppermute | solution.py:19
  147.5 2.1 constant_dynamic-update-slice_fusion.8
  152.7 3.8 collective-permute-done.16
  156.6 2.1 constant_dynamic-update-slice_fusion.7
  170.3 2.4 constant_dynamic-update-slice_fusion.13
  172.7 2.3 constant_dynamic-update-slice_fusion.12
  175.0 4.7 %collective-permute-done.22 = bf16[256,1024]{1,0:T(8,128)(2,1)S(1)} collective-permute-done((bf16[256,1024]{1,0:T(8,128)(2,1)S(1)}, bf16[256,1024]{1,0:T(8,128)(2,1)S(1)}, u32[]{:S(2)}, u32[]{:S(2)}) %collective-permute-start.22) | collective-permute-done | bytes 524320 | tf_op jit(solution)/shard_map/ppermute | solution.py:19
  183.3 12.6 %collective-permute-done.9 = bf16[2,1,2,192,512]{4,3,2,1,0:T(8,128)(2,1)S(1)} collective-permute-done((bf16[2,1,2,192,512]{4,3,2,1,0:T(8,128)(2,1)S(1)}, bf16[2,1,2,192,512]{4,3,2,1,0:T(8,128)(2,1)S(1)}, u32[]{:S(2)}, u32[]{:S(2)}) %collective-permute-start.9) | collective-permute-done | bytes 786464 | tf_op jit(solution)/shard_map/ppermute | solution.py:19
  197.4 2.6 collective-permute-start.26
  201.8 13.2 %collective-permute-done.25 = bf16[2,2,1,192,512]{4,3,2,1,0:T(8,128)(2,1)S(1)} collective-permute-done((bf16[2,2,1,192,512]{4,3,2,1,0:T(8,128)(2,1)S(1)}, bf16[2,2,1,192,512]{4,3,2,1,0:T(8,128)(2,1)S(1)}, u32[]{:S(2)}, u32[]{:S(2)}) %collective-permute-start.25) | collective-permute-done | bytes 786464 | tf_op jit(solution)/shard_map/ppermute | solution.py:19
  221.6 4.4 %fusion.20 = f32[512,1024]{1,0:T(8,128)S(1)} fusion(bf16[1536,512]{1,0:T(8,128)(2,1)} %bitcast.78, bf16[1536,1024]{1,0:T(8,128)(2,1)} %collective-permute-done.27, bf16[1536]{0:T(1024)(128)(2,1)S(1)} %neg.45, bf16[1536]{0:T(1024)(128)(2,1)S(1)} %min.58), kind=kOutput, calls=%fused_computation.51 | convolution fusion | flops 1613758464 | bytes 6821888 | tf_op jit(solution)/shard_map/dot_general | solution.py:131
  226.1 2.9 add_convert_fusion
  229.0 4.3 fusion.10
  233.3 2.0 add_convert_fusion.1
  236.1 2.5 fusion.3
  239.4 2.7 fusion.2
  242.8 2.6 convert_add_fusion
  247.7 2.8 fusion.112
  258.1 2.7 collective-permute-done.29
  264.6 9.1 %collective-permute-done.38 = f16[64,4096]{1,0:T(8,128)(2,1)S(1)} collective-permute-done((f16[64,4096]{1,0:T(8,128)(2,1)S(1)}, f16[64,4096]{1,0:T(8,128)(2,1)S(1)}, u32[]{:S(2)}, u32[]{:S(2)}) %collective-permute-start.38) | collective-permute-done | bytes 524320 | tf_op jit(solution)/shard_map/ppermute | solution.py:19
  275.5 8.4 %collective-permute-done.30 = f16[64,4096]{1,0:T(8,128)(2,1)S(1)} collective-permute-done((f16[64,4096]{1,0:T(8,128)(2,1)S(1)}, f16[64,4096]{1,0:T(8,128)(2,1)S(1)}, u32[]{:S(2)}, u32[]{:S(2)}) %collective-permute-start.30) | collective-permute-done | bytes 524320 | tf_op jit(solution)/shard_map/ppermute | solution.py:19
  287.1 3.6 collective-permute-start.33
  294.7 5.8 %collective-permute-done.42 = f16[2,1,2,64,512]{4,3,2,1,0:T(8,128)(2,1)} collective-permute-done((f16[2,1,2,64,512]{4,3,2,1,0:T(8,128)(2,1)}, f16[2,1,2,64,512]{4,3,2,1,0:T(8,128)(2,1)}, u32[]{:S(2)}, u32[]{:S(2)}) %collective-permute-start.42) | collective-permute-done | bytes 262176 | tf_op jit(solution)/shard_map/ppermute | solution.py:19
  305.0 9.8 %collective-permute-done.34 = f16[64,4096]{1,0:T(8,128)(2,1)} collective-permute-done((f16[64,4096]{1,0:T(8,128)(2,1)S(1)}, f16[64,4096]{1,0:T(8,128)(2,1)}, u32[]{:S(2)}, u32[]{:S(2)}) %collective-permute-start.34) | collective-permute-done | bytes 524320 | tf_op jit(solution)/shard_map/ppermute | solution.py:110
  318.3 3.3 collective-permute-start.51
  323.8 3.0 copy.34
  326.8 4.9 %collective-permute-done.35 = f16[64,4096]{1,0:T(8,128)(2,1)} collective-permute-done((f16[64,4096]{1,0:T(8,128)(2,1)}, f16[64,4096]{1,0:T(8,128)(2,1)}, u32[]{:S(2)}, u32[]{:S(2)}) %collective-permute-start.35) | collective-permute-done | bytes 524320 | tf_op jit(solution)/shard_map/ppermute | solution.py:117
  331.6 2.2 pad_maximum_fusion.3
  338.6 9.6 %shard_map.68 = f32[256,1024]{1,0:T(8,128)S(1)} custom-call(f32[1,1]{1,0:T(1,128)} %bitcast.24.scale_ref, bf16[512,4096]{1,0:T(8,128)(2,1)S(1)} %pad_maximum_fusion.rows_ref, bf16[2048,1024]{1,0:T(8,128)(2,1)S(1)} %copy-done.7, bf16[2048,1024]{1,0:T(8,128)(2,1)S(1)} %copy-done.5, bf16[2048,1024]{1,0:T(8,128)(2,1)S(1)} %copy-done.11, ...), custom_call_target="tpu_custom_call" | custom-call | flops 6442450944 | bytes 22020100 | tf_op jit(solution)/shard_map/pallas_call | solution.py:201
  349.7 5.4 %collective-permute-done.52 = f16[64,4096]{1,0:T(8,128)(2,1)} collective-permute-done((f16[64,4096]{1,0:T(8,128)(2,1)S(1)}, f16[64,4096]{1,0:T(8,128)(2,1)}, u32[]{:S(2)}, u32[]{:S(2)}) %collective-permute-start.52) | collective-permute-done | bytes 524320 | tf_op jit(solution)/shard_map/ppermute | solution.py:110
  355.9 4.3 collective-permute-done.46
  360.7 2.9 collective-permute-start.49
  363.8 2.9 collective-permute-done.48
  374.1 9.8 %shard_map.70 = f32[256,1024]{1,0:T(8,128)S(1)} custom-call(f32[1,1]{1,0:T(1,128)} %bitcast.24.scale_ref, bf16[512,4096]{1,0:T(8,128)(2,1)S(1)} %pad_maximum_fusion.1.rows_ref, bf16[2048,1024]{1,0:T(8,128)(2,1)S(1)} %copy-done.7, bf16[2048,1024]{1,0:T(8,128)(2,1)S(1)} %copy-done.5, bf16[2048,1024]{1,0:T(8,128)(2,1)S(1)} %copy-done.11, ...), custom_call_target="tpu_custom_call" | custom-call | flops 6442450944 | bytes 22020100 | tf_op jit(solution)/shard_map/pallas_call | solution.py:201
  384.0 2.1 collective-permute-start.54
  386.1 9.8 %collective-permute-done.54 = f16[256,1024]{1,0:T(8,128)(2,1)S(1)} collective-permute-done((f16[256,1024]{1,0:T(8,128)(2,1)S(1)}, f16[256,1024]{1,0:T(8,128)(2,1)S(1)}, u32[]{:S(2)}, u32[]{:S(2)}) %collective-permute-start.54) | collective-permute-done | bytes 524320 | tf_op jit(solution)/shard_map/ppermute | solution.py:19
  396.6 3.1 collective-permute-start.57
  399.9 2.5 collective-permute-done.56
  408.5 9.5 %shard_map.69.base_ref = f32[512,1024]{1,0:T(8,128)S(1)} custom-call(f32[1,1]{1,0:T(1,128)} %bitcast.9.factor_ref, s32[4]{0:T(128)S(1)} %and_select_fusion.1.level_ref, f32[512,1024]{1,0:T(8,128)S(1)} %bitcast.55, bf16[4,512,1024]{2,1,0:T(8,128)(2,1)S(1)} %bitcast.58, bf16[4,512,1024]{2,1,0:T(8,128)(2,1)S(1)} %bitcast.60, ...), custom_call_target="tpu_custom_call" | custom-call | flops 6442450944 | bytes 20971540 | tf_op jit(solution)/shard_map/pallas_call | solution.py:201
  420.0 10.2 %shard_map.71 = f32[512,1024]{1,0:T(8,128)} custom-call(f32[1,1]{1,0:T(1,128)} %bitcast.9.factor_ref, s32[4]{0:T(128)S(1)} %and_select_fusion.1.level_ref, f32[512,1024]{1,0:T(8,128)S(1)} %shard_map.69.base_ref, bf16[4,512,1024]{2,1,0:T(8,128)(2,1)S(1)} %bitcast.59, bf16[4,512,1024]{2,1,0:T(8,128)(2,1)S(1)} %bitcast.61, ...), custom_call_target="tpu_custom_call" | custom-call | flops 6442450944 | bytes 20971540 | tf_op jit(solution)/shard_map/pallas_call | solution.py:201
  (308 shorter events, 125.8 us)
Async XLA Ops:
  6.5 123.1 %all-gather.5.cloned.1.call-start = ((), (), s32[]{:S(2)}) async-start(), calls=%async_computation | async-start | bytes 5242880 | tf_op jit(solution)/shard_map/all_gather | solution.py:353
  9.8 7.0 %collective-permute-start = (f32[128]{0:T(128)S(1)}, f32[128]{0:T(128)S(1)}, u32[]{:S(2)}, u32[]{:S(2)}) collective-permute-start(f32[128]{0:T(128)S(1)} %broadcast_in_dim.24), channel_id=1, source_target_pairs={{0,8},{4,12},{8,0},{12,4},{16,24},{20,28},{24,16},{28,20},{1,9},{5... | collective-permute-start | bytes 1544 | tf_op jit(solution)/shard_map/ppermute | solution.py:19
  16.8 3.6 collective-permute-start.1
  22.8 206.2 %all-gather.7.cloned.1.call-start = ((), (), s32[]{:S(2)}) async-start(), calls=%async_computation.1 | async-start | bytes 5242880 | tf_op jit(solution)/shard_map/all_gather | solution.py:353
  31.5 15.6 %collective-permute-start.4 = (bf16[1,2,2,384,512]{4,3,2,1,0:T(8,128)(2,1)}, bf16[1,2,2,384,512]{4,3,2,1,0:T(8,128)(2,1)}, u32[]{:S(2)}, u32[]{:S(2)}) collective-permute-start(bf16[1,2,2,384,512]{4,3,2,1,0:T(8,128)(2,1)} %bitcast.2), channel_id=1, source_target_pairs={{0,4},{4,0},{8,12},{12,8},{16,20},{20,16},{24,28},{28,24},{1,5},{5... | collective-permute-start | bytes 4718600 | tf_op jit(solution)/shard_map/ppermute | solution.py:19
  31.5 25.9 %collective-permute-start.2 = (f16[512,1024]{1,0:T(8,128)(2,1)}, f16[512,1024]{1,0:T(8,128)(2,1)}, u32[]{:S(2)}, u32[]{:S(2)}) collective-permute-start(f16[512,1024]{1,0:T(8,128)(2,1)} %fusion.32), channel_id=1, source_target_pairs={{0,8},{4,12},{8,0},{12,4},{16,24},{20,28},{24,16},{28,20},{1,9},{5... | collective-permute-start | bytes 3145736 | tf_op jit(solution)/shard_map/ppermute | solution.py:19
  31.6 25.9 %collective-permute-start.3 = (f16[512,1024]{1,0:T(8,128)(2,1)}, f16[512,1024]{1,0:T(8,128)(2,1)}, u32[]{:S(2)}, u32[]{:S(2)}) collective-permute-start(f16[512,1024]{1,0:T(8,128)(2,1)} %fusion.32), channel_id=1, source_target_pairs={{0,16},{4,20},{8,24},{12,28},{16,0},{20,4},{24,8},{28,12},{1,17},{... | collective-permute-start | bytes 3145736 | tf_op jit(solution)/shard_map/ppermute | solution.py:19
  58.6 13.6 %collective-permute-start.5 = (f16[256,1024]{1,0:T(8,128)(2,1)S(1)}, f16[256,1024]{1,0:T(8,128)(2,1)S(1)}, u32[]{:S(2)}, u32[]{:S(2)}) collective-permute-start(f16[256,1024]{1,0:T(8,128)(2,1)S(1)} %slice.203), channel_id=1, source_target_pairs={{0,16},{4,20},{8,24},{12,28},{16,0},{20,4},{24,8},{28,12},{1,17},{... | collective-permute-start | bytes 1572872 | tf_op jit(solution)/shard_map/ppermute | solution.py:19
  61.6 13.1 %collective-permute-start.6 = (f16[256,1024]{1,0:T(8,128)(2,1)S(1)}, f16[256,1024]{1,0:T(8,128)(2,1)S(1)}, u32[]{:S(2)}, u32[]{:S(2)}) collective-permute-start(f16[256,1024]{1,0:T(8,128)(2,1)S(1)} %slice.204), channel_id=1, source_target_pairs={{0,8},{4,12},{8,0},{12,4},{16,24},{20,28},{24,16},{28,20},{1,9},{5... | collective-permute-start | bytes 1572872 | tf_op jit(solution)/shard_map/ppermute | solution.py:19
  75.5 18.4 %collective-permute-start.8 = (f16[2048,1024]{1,0:T(8,128)(2,1)}, f16[2048,1024]{1,0:T(8,128)(2,1)}, u32[]{:S(2)}, u32[]{:S(2)}) collective-permute-start(f16[2048,1024]{1,0:T(8,128)(2,1)} %constant_dynamic-update-slice_fusion), channel_id=1, source_target_pairs={{0,4},{4,0},{8,12},{12,8},{16,20},{20,16},{24,28},{28,24},{1,5},{5... | collective-permute-start | bytes 12582920 | tf_op jit(solution)/shard_map/ppermute | solution.py:19
  75.5 5.9 %collective-permute-start.7 = (f32[512]{0:T(512)S(1)}, f32[512]{0:T(512)S(1)}, u32[]{:S(2)}, u32[]{:S(2)}) collective-permute-start(f32[512]{0:T(512)S(1)} %pad_maximum_fusion.21), channel_id=1, source_target_pairs={{0,4},{4,0},{8,12},{12,8},{16,20},{20,16},{24,28},{28,24},{1,5},{5... | collective-permute-start | bytes 6152 | tf_op jit(solution)/shard_map/ppermute | solution.py:19
  81.6 17.2 %slice-start.2 = ((s8[7340032]{0:T(1024)(128)(4,1)}), s8[4194304]{0:T(1024)(128)(4,1)S(1)}, s32[]{:S(2)}) async-start(s8[7340032]{0:T(1024)(128)(4,1)} %bitcast.56), calls=%async_computation.4 | async-start | bytes 8388608
  86.2 12.6 %slice-start.3 = ((s8[7340032]{0:T(1024)(128)(4,1)}), s8[3145728]{0:T(1024)(128)(4,1)S(1)}, s32[]{:S(2)}) async-start(s8[7340032]{0:T(1024)(128)(4,1)} %bitcast.56), calls=%async_computation.5 | async-start | bytes 6291456
  104.3 20.7 %collective-permute-start.13 = (bf16[384,1024]{1,0:T(8,128)(2,1)}, bf16[384,1024]{1,0:T(8,128)(2,1)}, u32[]{:S(2)}, u32[]{:S(2)}) collective-permute-start(bf16[384,1024]{1,0:T(8,128)(2,1)} %get-tuple-element.110), channel_id=1, source_target_pairs={{0,8},{4,12},{8,0},{12,4},{16,24},{20,28},{24,16},{28,20},{1,9},{5... | collective-permute-start | bytes 2359304 | tf_op jit(solution)/shard_map/ppermute | solution.py:19
  105.7 20.7 %collective-permute-start.14 = (bf16[384,1024]{1,0:T(8,128)(2,1)}, bf16[384,1024]{1,0:T(8,128)(2,1)}, u32[]{:S(2)}, u32[]{:S(2)}) collective-permute-start(bf16[384,1024]{1,0:T(8,128)(2,1)} %get-tuple-element.110), channel_id=1, source_target_pairs={{0,16},{4,20},{8,24},{12,28},{16,0},{20,4},{24,8},{28,12},{1,17},{... | collective-permute-start | bytes 2359304 | tf_op jit(solution)/shard_map/ppermute | solution.py:19
  107.8 55.9 %collective-permute-start.18 = (bf16[512,1024]{1,0:T(8,128)(2,1)}, bf16[512,1024]{1,0:T(8,128)(2,1)}, u32[]{:S(2)}, u32[]{:S(2)}) collective-permute-start(bf16[512,1024]{1,0:T(8,128)(2,1)} %get-tuple-element.112), channel_id=1, source_target_pairs={{0,8},{4,12},{8,0},{12,4},{16,24},{20,28},{24,16},{28,20},{1,9},{5... | collective-permute-start | bytes 3145736 | tf_op jit(solution)/shard_map/ppermute | solution.py:19
  108.5 55.3 %collective-permute-start.19 = (bf16[512,1024]{1,0:T(8,128)(2,1)}, bf16[512,1024]{1,0:T(8,128)(2,1)}, u32[]{:S(2)}, u32[]{:S(2)}) collective-permute-start(bf16[512,1024]{1,0:T(8,128)(2,1)} %get-tuple-element.112), channel_id=1, source_target_pairs={{0,16},{4,20},{8,24},{12,28},{16,0},{20,4},{24,8},{28,12},{1,17},{... | collective-permute-start | bytes 3145736 | tf_op jit(solution)/shard_map/ppermute | solution.py:19
  111.1 3.7 collective-permute-start.11
  114.8 5.2 %collective-permute-start.12 = (f32[896]{0:T(1024)S(1)}, f32[896]{0:T(1024)S(1)}, u32[]{:S(2)}, u32[]{:S(2)}) collective-permute-start(f32[896]{0:T(1024)S(1)} %add.166), channel_id=1, source_target_pairs={{0,2},{1,3},{2,0},{3,1},{4,6},{5,7},{6,4},{7,5},{8,10},{9,11},{10,... | collective-permute-start | bytes 10760 | tf_op jit(solution)/shard_map/ppermute | solution.py:125
  126.5 20.5 %collective-permute-start.15 = (f32[1024]{0:T(1024)S(1)}, f32[1024]{0:T(1024)S(1)}, u32[]{:S(2)}, u32[]{:S(2)}) collective-permute-start(f32[1024]{0:T(1024)S(1)} %concatenate.120), channel_id=1, source_target_pairs={{0,8},{4,12},{8,0},{12,4},{16,24},{20,28},{24,16},{28,20},{1,9},{5... | collective-permute-start | bytes 12296 | tf_op jit(solution)/shard_map/ppermute | solution.py:19
  131.5 29.2 %collective-permute-start.20 = (bf16[192,1024]{1,0:T(8,128)(2,1)}, bf16[192,1024]{1,0:T(8,128)(2,1)S(1)}, u32[]{:S(2)}, u32[]{:S(2)}) collective-permute-start(bf16[192,1024]{1,0:T(8,128)(2,1)} %slice.219), channel_id=1, source_target_pairs={{0,16},{4,20},{8,24},{12,28},{16,0},{20,4},{24,8},{28,12},{1,17},{... | collective-permute-start | bytes 1179656 | tf_op jit(solution)/shard_map/ppermute | solution.py:19
  147.0 9.6 %collective-permute-start.16 = (f32[2048]{0:T(1024)S(1)}, f32[2048]{0:T(1024)S(1)}, u32[]{:S(2)}, u32[]{:S(2)}) collective-permute-start(f32[2048]{0:T(1024)S(1)} %pad_maximum_fusion.19), channel_id=1, source_target_pairs={{0,16},{4,20},{8,24},{12,28},{16,0},{20,4},{24,8},{28,12},{1,17},{... | collective-permute-start | bytes 24584 | tf_op jit(solution)/shard_map/ppermute | solution.py:19
  151.4 10.7 %collective-permute-start.21 = (bf16[192,1024]{1,0:T(8,128)(2,1)}, bf16[192,1024]{1,0:T(8,128)(2,1)}, u32[]{:S(2)}, u32[]{:S(2)}) collective-permute-start(bf16[192,1024]{1,0:T(8,128)(2,1)} %slice.220), channel_id=1, source_target_pairs={{0,8},{4,12},{8,0},{12,4},{16,24},{20,28},{24,16},{28,20},{1,9},{5... | collective-permute-start | bytes 1179656 | tf_op jit(solution)/shard_map/ppermute | solution.py:19
  156.6 2.1 collective-permute-start.17
  164.9 14.8 %collective-permute-start.22 = (bf16[256,1024]{1,0:T(8,128)(2,1)S(1)}, bf16[256,1024]{1,0:T(8,128)(2,1)S(1)}, u32[]{:S(2)}, u32[]{:S(2)}) collective-permute-start(bf16[256,1024]{1,0:T(8,128)(2,1)S(1)} %slice.221), channel_id=1, source_target_pairs={{0,16},{4,20},{8,24},{12,28},{16,0},{20,4},{24,8},{28,12},{1,17},{... | collective-permute-start | bytes 1572872 | tf_op jit(solution)/shard_map/ppermute | solution.py:19
  167.5 14.9 %collective-permute-start.23 = (bf16[256,1024]{1,0:T(8,128)(2,1)S(1)}, bf16[256,1024]{1,0:T(8,128)(2,1)S(1)}, u32[]{:S(2)}, u32[]{:S(2)}) collective-permute-start(bf16[256,1024]{1,0:T(8,128)(2,1)S(1)} %slice.222), channel_id=1, source_target_pairs={{0,8},{4,12},{8,0},{12,4},{16,24},{20,28},{24,16},{28,20},{1,9},{5... | collective-permute-start | bytes 1572872 | tf_op jit(solution)/shard_map/ppermute | solution.py:19
  169.1 26.8 %collective-permute-start.9 = (bf16[2,1,2,192,512]{4,3,2,1,0:T(8,128)(2,1)S(1)}, bf16[2,1,2,192,512]{4,3,2,1,0:T(8,128)(2,1)S(1)}, u32[]{:S(2)}, u32[]{:S(2)}) collective-permute-start(bf16[2,1,2,192,512]{4,3,2,1,0:T(8,128)(2,1)S(1)} %copy-done.28), channel_id=1, source_target_pairs={{0,16},{4,20},{8,24},{12,28},{16,0},{20,4},{24,8},{28,12},{1,17},{... | collective-permute-start | bytes 2359304 | tf_op jit(solution)/shard_map/ppermute | solution.py:19
  169.7 27.6 %collective-permute-start.10 = (bf16[2,2,1,192,512]{4,3,2,1,0:T(8,128)(2,1)S(1)}, bf16[2,2,1,192,512]{4,3,2,1,0:T(8,128)(2,1)S(1)}, u32[]{:S(2)}, u32[]{:S(2)}) collective-permute-start(bf16[2,2,1,192,512]{4,3,2,1,0:T(8,128)(2,1)S(1)} %get-tuple-element.85), channel_id=1, source_target_pairs={{0,8},{4,12},{8,0},{12,4},{16,24},{20,28},{24,16},{28,20},{1,9},{5... | collective-permute-start | bytes 2359304 | tf_op jit(solution)/shard_map/ppermute | solution.py:19
  170.3 51.3 %collective-permute-start.27 = (bf16[1536,1024]{1,0:T(8,128)(2,1)}, bf16[1536,1024]{1,0:T(8,128)(2,1)}, u32[]{:S(2)}, u32[]{:S(2)}) collective-permute-start(bf16[1536,1024]{1,0:T(8,128)(2,1)} %constant_dynamic-update-slice_fusion.5), channel_id=1, source_target_pairs={{0,4},{4,0},{8,12},{12,8},{16,20},{20,16},{24,28},{28,24},{1,5},{5... | collective-permute-start | bytes 9437192 | tf_op jit(solution)/shard_map/ppermute | solution.py:19
  170.3 25.6 %copy-start.25 = (bf16[2,1,2,192,512]{4,3,2,1,0:T(8,128)(2,1)S(1)}, bf16[2,1,2,192,512]{4,3,2,1,0:T(8,128)(2,1)}, u32[]{:S(2)}) copy-start(bf16[2,1,2,192,512]{4,3,2,1,0:T(8,128)(2,1)} %get-tuple-element.84) | copy-start | bytes 2359300
  183.3 45.7 %collective-permute-start.24 = (bf16[2048,1024]{1,0:T(8,128)(2,1)}, bf16[2048,1024]{1,0:T(8,128)(2,1)}, u32[]{:S(2)}, u32[]{:S(2)}) collective-permute-start(bf16[2048,1024]{1,0:T(8,128)(2,1)} %constant_dynamic-update-slice_fusion.10), channel_id=1, source_target_pairs={{0,4},{4,0},{8,12},{12,8},{16,20},{20,16},{24,28},{28,24},{1,5},{5... | collective-permute-start | bytes 12582920 | tf_op jit(solution)/shard_map/ppermute | solution.py:19
  196.0 19.0 %collective-permute-start.25 = (bf16[2,2,1,192,512]{4,3,2,1,0:T(8,128)(2,1)S(1)}, bf16[2,2,1,192,512]{4,3,2,1,0:T(8,128)(2,1)S(1)}, u32[]{:S(2)}, u32[]{:S(2)}) collective-permute-start(bf16[2,2,1,192,512]{4,3,2,1,0:T(8,128)(2,1)S(1)} %get-tuple-element.114), channel_id=1, source_target_pairs={{0,8},{4,12},{8,0},{12,4},{16,24},{20,28},{24,16},{28,20},{1,9},{5... | collective-permute-start | bytes 2359304 | tf_op jit(solution)/shard_map/ppermute | solution.py:19
  197.4 18.4 %collective-permute-start.26 = (bf16[2,1,2,192,512]{4,3,2,1,0:T(8,128)(2,1)S(1)}, bf16[2,1,2,192,512]{4,3,2,1,0:T(8,128)(2,1)S(1)}, u32[]{:S(2)}, u32[]{:S(2)}) collective-permute-start(bf16[2,1,2,192,512]{4,3,2,1,0:T(8,128)(2,1)S(1)} %get-tuple-element.116), channel_id=1, source_target_pairs={{0,16},{4,20},{8,24},{12,28},{16,0},{20,4},{24,8},{28,12},{1,17},{... | collective-permute-start | bytes 2359304 | tf_op jit(solution)/shard_map/ppermute | solution.py:19
  238.6 4.2 collective-permute-start.36
  242.1 5.6 %collective-permute-start.28 = (f16[256,4096]{1,0:T(8,128)(2,1)S(1)}, f16[256,4096]{1,0:T(8,128)(2,1)S(1)}, u32[]{:S(2)}, u32[]{:S(2)}) collective-permute-start(f16[256,4096]{1,0:T(8,128)(2,1)S(1)} %fusion.2), channel_id=1, source_target_pairs={{0,4},{4,0},{8,12},{12,8},{16,20},{20,16},{24,28},{28,24},{1,5},{5... | collective-permute-start | bytes 6291464 | tf_op jit(solution)/shard_map/ppermute | solution.py:19
  245.9 9.2 %collective-permute-start.37 = (f16[32,4096]{1,0:T(8,128)(2,1)S(1)}, f16[32,4096]{1,0:T(8,128)(2,1)S(1)}, u32[]{:S(2)}, u32[]{:S(2)}) collective-permute-start(f16[32,4096]{1,0:T(8,128)(2,1)S(1)} %get-tuple-element.104), channel_id=1, source_target_pairs={{0,16},{4,20},{8,24},{12,28},{16,0},{20,4},{24,8},{28,12},{1,17},{... | collective-permute-start | bytes 786440 | tf_op jit(solution)/shard_map/ppermute | solution.py:19
  247.7 9.2 %collective-permute-start.39 = (f16[32,4096]{1,0:T(8,128)(2,1)S(1)}, f16[32,4096]{1,0:T(8,128)(2,1)S(1)}, u32[]{:S(2)}, u32[]{:S(2)}) collective-permute-start(f16[32,4096]{1,0:T(8,128)(2,1)S(1)} %get-tuple-element.103), channel_id=1, source_target_pairs={{0,8},{4,12},{8,0},{12,4},{16,24},{20,28},{24,16},{28,20},{1,9},{5... | collective-permute-start | bytes 786440 | tf_op jit(solution)/shard_map/ppermute | solution.py:19
  250.8 10.0 %collective-permute-start.29 = (f16[32,4096]{1,0:T(8,128)(2,1)S(1)}, f16[32,4096]{1,0:T(8,128)(2,1)S(1)}, u32[]{:S(2)}, u32[]{:S(2)}) collective-permute-start(f16[32,4096]{1,0:T(8,128)(2,1)S(1)} %get-tuple-element.108), channel_id=1, source_target_pairs={{0,16},{4,20},{8,24},{12,28},{16,0},{20,4},{24,8},{28,12},{1,17},{... | collective-permute-start | bytes 786440 | tf_op jit(solution)/shard_map/ppermute | solution.py:19
  252.2 10.3 %collective-permute-start.31 = (f16[32,4096]{1,0:T(8,128)(2,1)S(1)}, f16[32,4096]{1,0:T(8,128)(2,1)S(1)}, u32[]{:S(2)}, u32[]{:S(2)}) collective-permute-start(f16[32,4096]{1,0:T(8,128)(2,1)S(1)} %get-tuple-element.107), channel_id=1, source_target_pairs={{0,8},{4,12},{8,0},{12,4},{16,24},{20,28},{24,16},{28,20},{1,9},{5... | collective-permute-start | bytes 786440 | tf_op jit(solution)/shard_map/ppermute | solution.py:19
  257.2 16.6 %collective-permute-start.38 = (f16[64,4096]{1,0:T(8,128)(2,1)S(1)}, f16[64,4096]{1,0:T(8,128)(2,1)S(1)}, u32[]{:S(2)}, u32[]{:S(2)}) collective-permute-start(f16[64,4096]{1,0:T(8,128)(2,1)S(1)} %pad_maximum_fusion.12), channel_id=1, source_target_pairs={{0,8},{4,12},{8,0},{12,4},{16,24},{20,28},{24,16},{28,20},{1,9},{5... | collective-permute-start | bytes 1572872 | tf_op jit(solution)/shard_map/ppermute | solution.py:19
  257.4 16.4 %collective-permute-start.40 = (f16[64,4096]{1,0:T(8,128)(2,1)S(1)}, f16[64,4096]{1,0:T(8,128)(2,1)S(1)}, u32[]{:S(2)}, u32[]{:S(2)}) collective-permute-start(f16[64,4096]{1,0:T(8,128)(2,1)S(1)} %pad_maximum_fusion.13), channel_id=1, source_target_pairs={{0,16},{4,20},{8,24},{12,28},{16,0},{20,4},{24,8},{28,12},{1,17},{... | collective-permute-start | bytes 1572872 | tf_op jit(solution)/shard_map/ppermute | solution.py:19
  262.8 21.1 %collective-permute-start.30 = (f16[64,4096]{1,0:T(8,128)(2,1)S(1)}, f16[64,4096]{1,0:T(8,128)(2,1)S(1)}, u32[]{:S(2)}, u32[]{:S(2)}) collective-permute-start(f16[64,4096]{1,0:T(8,128)(2,1)S(1)} %pad_maximum_fusion.10), channel_id=1, source_target_pairs={{0,8},{4,12},{8,0},{12,4},{16,24},{20,28},{24,16},{28,20},{1,9},{5... | collective-permute-start | bytes 1572872 | tf_op jit(solution)/shard_map/ppermute | solution.py:19
  263.0 20.9 %collective-permute-start.32 = (f16[64,4096]{1,0:T(8,128)(2,1)S(1)}, f16[64,4096]{1,0:T(8,128)(2,1)S(1)}, u32[]{:S(2)}, u32[]{:S(2)}) collective-permute-start(f16[64,4096]{1,0:T(8,128)(2,1)S(1)} %pad_maximum_fusion.11), channel_id=1, source_target_pairs={{0,16},{4,20},{8,24},{12,28},{16,0},{20,4},{24,8},{28,12},{1,17},{... | collective-permute-start | bytes 1572872 | tf_op jit(solution)/shard_map/ppermute | solution.py:19
  287.1 3.9 collective-permute-start.41
  287.1 17.9 %collective-permute-start.33 = (f16[64,4096]{1,0:T(8,128)(2,1)S(1)}, f16[64,4096]{1,0:T(8,128)(2,1)}, u32[]{:S(2)}, u32[]{:S(2)}) collective-permute-start(f16[64,4096]{1,0:T(8,128)(2,1)S(1)} %convert_element_type.202), channel_id=1, source_target_pairs={{0,3},{1,0},{2,1},{3,2},{4,7},{5,4},{6,5},{7,6},{8,11},{9,8},{10,9... | collective-permute-start | bytes 1572872 | tf_op jit(solution)/shard_map/ppermute | solution.py:110
  290.8 24.0 %collective-permute-start.34 = (f16[64,4096]{1,0:T(8,128)(2,1)S(1)}, f16[64,4096]{1,0:T(8,128)(2,1)}, u32[]{:S(2)}, u32[]{:S(2)}) collective-permute-start(f16[64,4096]{1,0:T(8,128)(2,1)S(1)} %convert_element_type.202), channel_id=1, source_target_pairs={{0,1},{1,2},{2,3},{3,0},{4,5},{5,6},{6,7},{7,4},{8,9},{9,10},{10,1... | collective-permute-start | bytes 1572872 | tf_op jit(solution)/shard_map/ppermute | solution.py:110
  291.8 8.7 %collective-permute-start.42 = (f16[2,1,2,64,512]{4,3,2,1,0:T(8,128)(2,1)}, f16[2,1,2,64,512]{4,3,2,1,0:T(8,128)(2,1)}, u32[]{:S(2)}, u32[]{:S(2)}) collective-permute-start(f16[2,1,2,64,512]{4,3,2,1,0:T(8,128)(2,1)} %get-tuple-element.118), channel_id=1, source_target_pairs={{0,16},{4,20},{8,24},{12,28},{16,0},{20,4},{24,8},{28,12},{1,17},{... | collective-permute-start | bytes 786440 | tf_op jit(solution)/shard_map/ppermute | solution.py:19
  293.0 9.0 %collective-permute-start.44 = (f16[2,2,1,64,512]{4,3,2,1,0:T(8,128)(2,1)}, f16[2,2,1,64,512]{4,3,2,1,0:T(8,128)(2,1)S(1)}, u32[]{:S(2)}, u32[]{:S(2)}) collective-permute-start(f16[2,2,1,64,512]{4,3,2,1,0:T(8,128)(2,1)} %get-tuple-element.120), channel_id=1, source_target_pairs={{0,8},{4,12},{8,0},{12,4},{16,24},{20,28},{24,16},{28,20},{1,9},{5... | collective-permute-start | bytes 786440 | tf_op jit(solution)/shard_map/ppermute | solution.py:19
  301.6 16.0 %collective-permute-start.43 = (f16[2,2,1,64,512]{4,3,2,1,0:T(8,128)(2,1)S(1)}, f16[2,2,1,64,512]{4,3,2,1,0:T(8,128)(2,1)S(1)}, u32[]{:S(2)}, u32[]{:S(2)}) collective-permute-start(f16[2,2,1,64,512]{4,3,2,1,0:T(8,128)(2,1)S(1)} %get-tuple-element.124), channel_id=1, source_target_pairs={{0,8},{4,12},{8,0},{12,4},{16,24},{20,28},{24,16},{28,20},{1,9},{5... | collective-permute-start | bytes 786440 | tf_op jit(solution)/shard_map/ppermute | solution.py:19
  303.8 13.8 %collective-permute-start.45 = (f16[2,1,2,64,512]{4,3,2,1,0:T(8,128)(2,1)S(1)}, f16[2,1,2,64,512]{4,3,2,1,0:T(8,128)(2,1)S(1)}, u32[]{:S(2)}, u32[]{:S(2)}) collective-permute-start(f16[2,1,2,64,512]{4,3,2,1,0:T(8,128)(2,1)S(1)} %get-tuple-element.126), channel_id=1, source_target_pairs={{0,16},{4,20},{8,24},{12,28},{16,0},{20,4},{24,8},{28,12},{1,17},{... | collective-permute-start | bytes 786440 | tf_op jit(solution)/shard_map/ppermute | solution.py:19
  315.9 15.7 %collective-permute-start.35 = (f16[64,4096]{1,0:T(8,128)(2,1)}, f16[64,4096]{1,0:T(8,128)(2,1)}, u32[]{:S(2)}, u32[]{:S(2)}) collective-permute-start(f16[64,4096]{1,0:T(8,128)(2,1)} %select_select_fusion.1), channel_id=1, source_target_pairs={{3,1},{0,2},{1,0},{2,3},{7,5},{4,6},{5,4},{6,7},{11,9},{8,10},{9,8... | collective-permute-start | bytes 1572872 | tf_op jit(solution)/shard_map/ppermute | solution.py:117
  318.3 31.5 %collective-permute-start.51 = (f16[64,4096]{1,0:T(8,128)(2,1)S(1)}, f16[64,4096]{1,0:T(8,128)(2,1)}, u32[]{:S(2)}, u32[]{:S(2)}) collective-permute-start(f16[64,4096]{1,0:T(8,128)(2,1)S(1)} %convert_element_type.210), channel_id=1, source_target_pairs={{0,3},{1,0},{2,1},{3,2},{4,7},{5,4},{6,5},{7,6},{8,11},{9,8},{10,9... | collective-permute-start | bytes 1572872 | tf_op jit(solution)/shard_map/ppermute | solution.py:110
  321.6 33.6 %collective-permute-start.52 = (f16[64,4096]{1,0:T(8,128)(2,1)S(1)}, f16[64,4096]{1,0:T(8,128)(2,1)}, u32[]{:S(2)}, u32[]{:S(2)}) collective-permute-start(f16[64,4096]{1,0:T(8,128)(2,1)S(1)} %convert_element_type.210), channel_id=1, source_target_pairs={{0,1},{1,2},{2,3},{3,0},{4,5},{5,6},{6,7},{7,4},{8,9},{9,10},{10,1... | collective-permute-start | bytes 1572872 | tf_op jit(solution)/shard_map/ppermute | solution.py:110
  348.3 12.0 %collective-permute-start.46 = (f16[256,1024]{1,0:T(8,128)(2,1)S(1)}, f16[256,1024]{1,0:T(8,128)(2,1)S(1)}, u32[]{:S(2)}, u32[]{:S(2)}) collective-permute-start(f16[256,1024]{1,0:T(8,128)(2,1)S(1)} %get-tuple-element.70), channel_id=1, source_target_pairs={{0,8},{4,12},{8,0},{12,4},{16,24},{20,28},{24,16},{28,20},{1,9},{5... | collective-permute-start | bytes 1572872 | tf_op jit(solution)/shard_map/ppermute | solution.py:19
  348.6 12.1 %collective-permute-start.47 = (f16[256,1024]{1,0:T(8,128)(2,1)S(1)}, f16[256,1024]{1,0:T(8,128)(2,1)S(1)}, u32[]{:S(2)}, u32[]{:S(2)}) collective-permute-start(f16[256,1024]{1,0:T(8,128)(2,1)S(1)} %get-tuple-element.70), channel_id=1, source_target_pairs={{0,16},{4,20},{8,24},{12,28},{16,0},{20,4},{24,8},{28,12},{1,17},{... | collective-permute-start | bytes 1572872 | tf_op jit(solution)/shard_map/ppermute | solution.py:19
  355.6 13.8 %collective-permute-start.53 = (f16[64,4096]{1,0:T(8,128)(2,1)S(1)}, f16[64,4096]{1,0:T(8,128)(2,1)S(1)}, u32[]{:S(2)}, u32[]{:S(2)}) collective-permute-start(f16[64,4096]{1,0:T(8,128)(2,1)S(1)} %select_select_fusion), channel_id=1, source_target_pairs={{3,1},{0,2},{1,0},{2,3},{7,5},{4,6},{5,4},{6,7},{11,9},{8,10},{9,8... | collective-permute-start | bytes 1572872 | tf_op jit(solution)/shard_map/ppermute | solution.py:117
  360.3 6.4 %collective-permute-start.48 = (f16[128,1024]{1,0:T(8,128)(2,1)S(1)}, f16[128,1024]{1,0:T(8,128)(2,1)S(1)}, u32[]{:S(2)}, u32[]{:S(2)}) collective-permute-start(f16[128,1024]{1,0:T(8,128)(2,1)S(1)} %slice.274), channel_id=1, source_target_pairs={{0,16},{4,20},{8,24},{12,28},{16,0},{20,4},{24,8},{28,12},{1,17},{... | collective-permute-start | bytes 786440 | tf_op jit(solution)/shard_map/ppermute | solution.py:19
  360.7 7.2 %collective-permute-start.49 = (f16[128,1024]{1,0:T(8,128)(2,1)S(1)}, f16[128,1024]{1,0:T(8,128)(2,1)S(1)}, u32[]{:S(2)}, u32[]{:S(2)}) collective-permute-start(f16[128,1024]{1,0:T(8,128)(2,1)S(1)} %slice.275), channel_id=1, source_target_pairs={{0,8},{4,12},{8,0},{12,4},{16,24},{20,28},{24,16},{28,20},{1,9},{5... | collective-permute-start | bytes 786440 | tf_op jit(solution)/shard_map/ppermute | solution.py:19
  384.0 11.9 %collective-permute-start.54 = (f16[256,1024]{1,0:T(8,128)(2,1)S(1)}, f16[256,1024]{1,0:T(8,128)(2,1)S(1)}, u32[]{:S(2)}, u32[]{:S(2)}) collective-permute-start(f16[256,1024]{1,0:T(8,128)(2,1)S(1)} %get-tuple-element.68), channel_id=1, source_target_pairs={{0,8},{4,12},{8,0},{12,4},{16,24},{20,28},{24,16},{28,20},{1,9},{5... | collective-permute-start | bytes 1572872 | tf_op jit(solution)/shard_map/ppermute | solution.py:19
  386.1 10.5 %collective-permute-start.55 = (f16[256,1024]{1,0:T(8,128)(2,1)S(1)}, f16[256,1024]{1,0:T(8,128)(2,1)S(1)}, u32[]{:S(2)}, u32[]{:S(2)}) collective-permute-start(f16[256,1024]{1,0:T(8,128)(2,1)S(1)} %get-tuple-element.68), channel_id=1, source_target_pairs={{0,16},{4,20},{8,24},{12,28},{16,0},{20,4},{24,8},{28,12},{1,17},{... | collective-permute-start | bytes 1572872 | tf_op jit(solution)/shard_map/ppermute | solution.py:19
  386.1 19.1 %collective-permute-start.50 = (f16[1024,1024]{1,0:T(8,128)(2,1)S(1)}, f16[1024,1024]{1,0:T(8,128)(2,1)S(1)}, u32[]{:S(2)}, u32[]{:S(2)}) collective-permute-start(f16[1024,1024]{1,0:T(8,128)(2,1)S(1)} %copy-done.24), channel_id=1, source_target_pairs={{0,4},{4,0},{8,12},{12,8},{16,20},{20,16},{24,28},{28,24},{1,5},{5... | collective-permute-start | bytes 6291464 | tf_op jit(solution)/shard_map/ppermute | solution.py:19
  396.0 6.4 %collective-permute-start.56 = (f16[128,1024]{1,0:T(8,128)(2,1)S(1)}, f16[128,1024]{1,0:T(8,128)(2,1)S(1)}, u32[]{:S(2)}, u32[]{:S(2)}) collective-permute-start(f16[128,1024]{1,0:T(8,128)(2,1)S(1)} %slice.276), channel_id=1, source_target_pairs={{0,16},{4,20},{8,24},{12,28},{16,0},{20,4},{24,8},{28,12},{1,17},{... | collective-permute-start | bytes 786440 | tf_op jit(solution)/shard_map/ppermute | solution.py:19
  396.6 7.4 %collective-permute-start.57 = (f16[128,1024]{1,0:T(8,128)(2,1)S(1)}, f16[128,1024]{1,0:T(8,128)(2,1)S(1)}, u32[]{:S(2)}, u32[]{:S(2)}) collective-permute-start(f16[128,1024]{1,0:T(8,128)(2,1)S(1)} %slice.277), channel_id=1, source_target_pairs={{0,8},{4,12},{8,0},{12,4},{16,24},{20,28},{24,16},{28,20},{1,9},{5... | collective-permute-start | bytes 786440 | tf_op jit(solution)/shard_map/ppermute | solution.py:19
  404.1 14.0 %collective-permute-start.58 = (f16[1024,1024]{1,0:T(8,128)(2,1)S(1)}, f16[1024,1024]{1,0:T(8,128)(2,1)S(1)}, u32[]{:S(2)}, u32[]{:S(2)}) collective-permute-start(f16[1024,1024]{1,0:T(8,128)(2,1)S(1)} %constant_dynamic-update-slice_fusion.20), channel_id=1, source_target_pairs={{0,4},{4,0},{8,12},{12,8},{16,20},{20,16},{24,28},{28,24},{1,5},{5... | collective-permute-start | bytes 6291464 | tf_op jit(solution)/shard_map/ppermute | solution.py:19
  (37 other events, 164.9 us)
Sparse Core Ops, SparseCore 0:
  22.9 81.0 all-gather.4
  105.6 79.4 all-gather.6

commit v3 on v2

--- a/solution.py
+++ b/solution.py
@@ -32,29 +32,41 @@
     return jnp.concatenate([x, swap(x, 1)], axis=0)
 
 
+def tie(*values):
+    return lax.optimization_barrier(values)
+
+
+def first_step(x):
+    return (swap(x, 2), swap(x, 4)) if lax.axis_size("dp") == 8 else ()
+
+
 def after(x, *earlier):
     return lax.optimization_barrier((x,) + earlier)[0]
 
 
-def first_step(x):
-    return (swap(x, 2), swap(x, 4)) if lax.axis_size("dp") == 8 else ()
-
-
-def second_step(x, came):
+def far_step(x, came):
+    if lax.axis_size("dp") != 8:
+        return ()
+    half = x.shape[0] // 2
+    return swap(came[0][:half], 4), swap(came[1][half:], 2)
+
+
+def join(x, came, far):
     if lax.axis_size("dp") != 8:
         bit = 1
         while bit < lax.axis_size("dp") // 2:
             x = jnp.concatenate([x, swap(x, 2 * bit)], axis=0)
             bit *= 2
         return x
-    half = x.shape[0] // 2
-    from_x, from_y = came
-    far = [swap(from_x[:half], 4), swap(from_y[half:], 2)]
-    return jnp.concatenate([x, from_x, from_y] + far, axis=0)
+    return jnp.concatenate([x, *came, *far], axis=0)
+
+
+def second_step(x, came):
+    return join(x, came, far_step(x, came))
 
 
 def trade(x, mask):
-    return swap(x.astype(F16), mask).astype(F32)
+    return swap(x.astype(F16), mask)
 
 
 def scatter_first(total):
@@ -70,16 +82,16 @@
         bit = chips // 2
         while bit:
             half = total.shape[0] // 2
-            total = total[:half] + trade(total[half:], 2 * bit)
+            total = total[:half] + trade(total[half:], 2 * bit).astype(F32)
             bit //= 2
         return total
-    via_x, via_y = came
+    via_x, via_y = (x.astype(F32) for x in came)
     size = total.shape[0] // chips
     half = size // 2
     own, to_x, to_y = (total[i * size : (i + 1) * size] for i in range(3))
     to_y = jnp.concatenate([to_y[:half] + via_x, to_y[half:]], axis=0)
     to_x = jnp.concatenate([to_x[:half], to_x[half:] + via_y], axis=0)
-    return own + trade(to_x, 2) + trade(to_y, 4)
+    return own + trade(to_x, 2).astype(F32) + trade(to_y, 4).astype(F32)
 
 
 def exchange_steps(x):
@@ -91,19 +103,19 @@
         stay, go = jnp.split(x, 2, axis=axis)
         return jnp.concatenate([stay, swap(go, 1 if axis == 0 else n >> axis)], axis=axis)
 
-    x = yield halve(x.reshape((2,) * bits + shape[1:]), 0)
+    x = x.reshape((2,) * bits + shape[1:])
     if bits != 3:
         x = yield halve(x, 1)
         for axis in range(2, bits):
             x = halve(x, axis)
-        yield x.reshape(shape)
-        return
-    upper, lower = jnp.split(x, 2, axis=3)
-    upper, lower = yield (halve(upper, 1), halve(lower, 2))
-    yield jnp.concatenate([halve(upper, 2), halve(lower, 1)], axis=3).reshape(shape)
-
-
-def gather_loop(x):
+    else:
+        upper, lower = jnp.split(x, 2, axis=3)
+        upper, lower = yield (halve(upper, 1), halve(lower, 2))
+        x = jnp.concatenate([halve(upper, 2), halve(lower, 1)], axis=3)
+    yield halve(x, 0).reshape(shape)
+
+
+def gather_loop(x, then=None):
     n = lax.axis_size("loop")
 
     def turn(r):
@@ -113,6 +125,8 @@
         return [x] + [turn(r) for r in range(1, n)]
     me = lax.axis_index("loop")
     after_me, before_me = turn(1), turn(3)
+    if then is not None:
+        after_me, before_me, then[0] = tie(after_me, before_me, then[0])
     across = jnp.where(me == 1, after_me, jnp.where(me == 2, before_me, x))
     across = lax.ppermute(across, "loop", [(3, 1), (0, 2), (1, 0), (2, 3)])
     return [x, after_me, across, before_me]
@@ -322,10 +336,10 @@
     while bit < half:
         rot_units = jnp.concatenate([rot_units, swap(rot_units, 2 * bit)], axis=0)
         bit *= 2
-    rot_code = after(rot_code, rot_units)
+    rot_code, rot_units = tie(rot_code, rot_units)
     rot_units = jnp.concatenate([rot_units, swap(rot_units, 1)], axis=0)
     rot_units = rot_units.reshape(2, half, 1, 128)[:, :, :, :1]
-    tokens, cotangent, proj_weight = after((tokens, cotangent, proj_weight), rot_code)
+    tokens, cotangent, proj_weight, rot_code = tie(tokens, cotangent, proj_weight, rot_code)
     rot_came = first_step(rot_code)
 
     def decode(part, units):
@@ -345,28 +359,32 @@
     source = cols - cols % wide + (((cols % wide) // sub) ^ place) * sub + cols % sub
     shuffle = (cols[:, None] == source[None, :]).astype(BF16)
     rows_terms = [
-        dot(x, shuffle, 1, 0).astype(BF16) for x in split(after(rotation, tokens))
+        dot(x, shuffle, 1, 0).astype(BF16) for x in split(tie(rotation, tokens)[0])
     ]
+    rows_sent = rows_terms
+    rot_came, cuts, rows_terms, rot_units = tie(rot_came, cuts, rows_terms, rot_units)
+    rows_terms = [lax.all_gather(x, "loop", axis=0) for x in rows_sent]
+    rot_far = far_step(rot_code, rot_came)
+    rot_far, both, both_plain = tie(rot_far, both, both_plain)
+    rot_near = join(rot_code, rot_came, rot_far)
+    rot_away = swap(rot_near, 1)
     cuts_way = exchange_steps(cuts)
     cuts = next(cuts_way)
-    rot_came = after(rot_came, both, cuts, *rows_terms)
-    rows_terms = [lax.all_gather(x, "loop", axis=0) for x in rows_terms]
-    rot_near = second_step(rot_code, rot_came)
-    rot_away = swap(rot_near, 1)
     rot_terms = [decode(rot_near, rot_units[0])]
     near_part = dot(both[:, : feat_width // 2], rot_terms[0][0], 1, 0)
-    cuts = cuts_way.send(after(cuts, *rot_came))
 
     half_feat, half_out = feat_width // 2, all_outs // 2
-    rot_terms.append(decode(after(rot_away, near_part, cuts), rot_units[1]))
+    rot_away, near_part, cuts = tie(rot_away, near_part, cuts)
+    rot_terms.append(decode(rot_away, rot_units[1]))
     cuts = cuts_way.send(cuts)
-    cot_owned = cuts.reshape(2, half * tok_rows, out_block)
     rotated = near_part + dot(both[:, half_feat:], rot_terms[1][0], 1, 0)
     acts_raw, mixed_raw = rotated[:tok_rows].astype(BF16), rotated[tok_rows:].astype(BF16)
-    acts_came, mixed_came = first_step(acts_raw), first_step(mixed_raw)
     power = after(jnp.sum(rotated * rotated, axis=1), acts_raw, mixed_raw)
+    acts_came = first_step(acts_raw)
+    acts_came, mixed_raw = tie(acts_came, mixed_raw)
+    mixed_came = first_step(mixed_raw)
     power = sum_loop(power)
-    tokens, proj_weight, rotation = after((tokens, proj_weight, rotation), acts_raw, mixed_raw)
+    tokens, proj_weight, rotation = after((tokens, proj_weight, rotation), acts_raw)
     limit = clip_ratio * jnp.sqrt(power / feat_width + eps_power)
     tok_top = jnp.max(jnp.abs(tokens), axis=1).astype(F32)
     weight_top = jnp.max(jnp.abs(proj_weight), axis=0).astype(F32)
@@ -378,14 +396,20 @@
         jnp.max(jnp.sum(rotation**2, axis=0)),
     ]
     sizes = jnp.concatenate([jnp.stack(sizes), jnp.zeros((128 - len(sizes),), F32)])
-    told = gather_small(after(jnp.concatenate([limit, sizes]), *acts_came)).reshape(2, half, -1)
+    acts_came, rows_high = tie(acts_came, rows_terms[0])
+    rows_terms = [rows_high, rows_terms[1]]
+    acts_far = far_step(acts_raw, acts_came)
+    told = jnp.concatenate([limit, sizes])
+    acts_far, told, cuts = tie(acts_far, told, cuts)
+    acts_near = join(acts_raw, acts_came, acts_far)
+    acts_away = swap(acts_near, 1)
+    told = gather_small(told)
+    cot_owned = cuts.reshape(2, half * tok_rows, out_block)
+    mixed_near = second_step(mixed_raw, mixed_came)
+    mixed_near, told = tie(mixed_near, told)
+    told = told.reshape(2, half, -1)
+    mixed_away = swap(mixed_near, 1)
     limits = told[:, :, : limit.shape[0]].astype(BF16)
-    acts_came = after(acts_came, cuts, rows_terms[0])
-    acts_near = second_step(acts_raw, acts_came)
-    acts_away = swap(acts_near, 1)
-    mixed_came = after(mixed_came, acts_near, told)
-    mixed_near = second_step(mixed_raw, mixed_came)
-    mixed_away = swap(mixed_near, 1)
     norms = jnp.sqrt(n * jnp.max(told[:, :, limit.shape[0] :], axis=(0, 1)))
     bound = cot_limit * all_outs**0.5 * (norms[0] * norms[2] + norms[1] * norms[3])
     grad_scale = code_top / jnp.clip(1.02 * bound, 1e-30, 3e38)
@@ -402,7 +426,10 @@
 
     acts_q = [clip(x, top) for x, top in zip((acts_near, acts_away), acts_limit)]
     grad_mixed = sum(dot(x, y, 0, 0) for x, y in zip(cot_owned, acts_q)).astype(BF16)
-    mixed_near, mixed_away = after((mixed_near, mixed_away), grad_mixed, rows_terms[1])
+    mixed_near, mixed_away, grad_mixed, rows_low = tie(
+        mixed_near, mixed_away, grad_mixed, rows_terms[1]
+    )
+    rows_terms = [rows_terms[0], rows_low]
     mixed_q = [clip(x, top) for x, top in zip((mixed_near, mixed_away), mixed_limit)]
     grad_acts = sum(
         dot(masked[:, h * half_out : (h + 1) * half_out], mixed_q[h], 1, 0) for h in range(2)
@@ -417,43 +444,51 @@
         near = dot(pair[:, : wide // 2], both_plain, 0, 0) * to_code
         totals.append(near + swap(away, 1).astype(F32))
     for c in range(chunks):
-        total = after(totals[c], *came) if c else totals[c]
-        came = scatter_first(total) if n == 8 else ()
-        strip = scatter_last(total, came)
+        came = scatter_first(totals[c]) if n == 8 else ()
+        if c + 1 < chunks:
+            totals[c + 1], came = tie(totals[c + 1], came)
+        strip = scatter_last(totals[c], came)
         strip = lay_columns(order, strip, jnp.ones((sub, 1), F32), row_block).astype(F16)
         strips.append(strip)
 
     strip = jnp.concatenate(strips, axis=0)
     blocks = strip.reshape(chunks * sub, n, row_block).transpose(1, 0, 2)
     blocks_way = exchange_steps(blocks)
-    blocks = blocks_way.send(blocks_way.send(next(blocks_way)))
+    blocks = blocks_way.send(next(blocks_way))
     blocks = jnp.concatenate(
         [lax.dynamic_slice_in_dim(blocks, place ^ q, 1, 0) for q in range(n)], axis=0
     )
     gradient = blocks.reshape(n, chunks, sub, row_block).transpose(1, 0, 2, 3)
     unit = 1.0 / grad_scale
-    result = after(gradient.reshape(panel, row_block).astype(F32) * unit, strip).T
+    gradient = lax.optimization_barrier(gradient.reshape(panel, row_block).astype(F32) * unit)
+    result = gradient.T
     factor = -(unit / cross_scale).reshape(1, 1)
 
     levels = (level + jnp.arange(loops, dtype=jnp.int32)) % loops
 
     cross_pairs = []
     for c in range(chunks):
-        strip = after(strips[c], gradient) if c else strips[c]
-        rows = jnp.concatenate(gather_loop(strip), axis=0)
-        if c == 0:
-            rows, result = after((rows, result), gradient)
+        later = strips[c + 1 : c + 2]
+        rows = jnp.concatenate(gather_loop(strips[c], later or None), axis=0)
+        strips[c + 1 : c + 2] = later
+        if c:
+            rows, cross_near = tie(rows, cross_near)
+            cross_pairs.append((cross_near, swap(cross_near, 1)))
         else:
-            rows = after(rows, cross_near)
+            rows, result = tie(rows, result)
         stacked = jnp.concatenate(split(rows.astype(F32)), axis=0)
         cross = cross_rows(cross_scale.reshape(1, 1), stacked, rot_terms).astype(F16)
-        cross_near = second_step(cross, first_step(cross))
-        cross_pairs.append((cross_near, swap(cross_near, 1)))
+        came = first_step(cross)
+        if c + 1 < chunks:
+            cross_near = second_step(cross, came)
     for c, pair in enumerate(cross_pairs):
-        if c:
-            pair = after(pair, result)
-        terms = [split(x.astype(F32)) for x in pair]
-        result = add_product(result, factor, levels, c, rows_terms, terms)
+        result = add_product(result, factor, levels, c, rows_terms, [split(x.astype(F32)) for x in pair])
+    far = far_step(cross, came)
+    far, result = tie(far, result)
+    cross_near = join(cross, came, far)
+    pair = (cross_near, swap(cross_near, 1))
+    terms = [split(x.astype(F32)) for x in pair]
+    result = add_product(result, factor, levels, chunks - 1, rows_terms, terms)
     return result
 
 

time: 444 us -> 418 us (0.941)
  waiting for transfers between devices: 149 us -> 116 us
  local copies, waits for them, and re-layouts: 73.7 us -> 79.1 us
  starting transfers between devices: 59.5 us -> 64.8 us
    ppermute x51, waiting for transfers between devices: 126 us -> 107 us  [swap(): return lax.ppermute(x, 'dp', [(i, i ^ mask) for i in range(n)])]
    ppermute x4, waiting for transfers between devices: 15.3 us -> 1.52 us  [turn(): return lax.ppermute(x, 'loop', [(i, (i - r) % n) for i in range(n)])]
    unnamed x113 -> x95, local copies, waits for them, and re-layouts: 42.1 us -> 49 us
    ppermute x2, starting transfers between devices: 2.11 us -> 6.57 us  [gather_loop(): across = lax.ppermute(across, 'loop', [(3, 1), (0, 2), (1, 0), (2, 3)])]
    concatenate x7 -> x6, other arithmetic: 8.05 us -> 3.6 us  [halve(): jnp.concatenate([stay, swap(go, 1 if axis == 0 else n >> axis)], axis=axis)]
  transfers between devices with their start and end apart: 61 -> 61, of which waited for: 37 -> 32; matrix products, arithmetic and copies ran while one was open for 28% -> 30% of each run, Pallas kernels for 6% -> 9%
where the time goes in v3:
time: 418 us; the launch traced here: 413 us
  waiting for transfers between devices  116 us (28%)
  local copies, waits for them, and re-layouts  79.1 us (19%)
  starting transfers between devices  64.8 us (16%)
  Pallas kernels  48.4 us (12%)
  other arithmetic  43.1 us (10%)
  matrix products  42.4 us (10%)
  between operations  19 us (5%)
    ppermute x51, waiting for transfers between devices, swap(): return lax.ppermute(x, 'dp', [(i, i ^ mask) for i in range(n)])  107 us
    unnamed x95, local copies, waits for them, and re-layouts  49 us
    ppermute x51, starting transfers between devices, swap(): return lax.ppermute(x, 'dp', [(i, i ^ mask) for i in range(n)])  46.7 us
    dot_general x12, matrix products, dot(): lax.dot_general(a, b, (((ca,), (cb,)), ((), ())), preferred_element_type=...  41 us
    pallas_call x4, Pallas kernels, plain_call(): pl.pallas_call(body, out_shape=out, grid=grid, in_specs=in_specs, out_spe...  39.2 us
    convert_element_type x8, other arithmetic, split(): return (high.astype(BF16), (x - high).astype(BF16))  16.8 us
    pallas_call x4, Pallas kernels, ordered_call(): pl.pallas_call(body, out_shape=outs, grid_spec=pltpu.PrefetchScalarGridSp...  9.2 us
  transfers between devices with their start and end apart: 61, of which 32 were waited for; matrix products, arithmetic and copies ran while one was open for 30% of the time, Pallas kernels for 9%

profile of v3, /device:TPU:0, one launch (start us, length us, event | category | flops | bytes accessed | tf_op | source)
XLA Modules:
  0.0 413.2 jit_solution(15403396038289775301)
XLA Ops:
  6.5 2.5 abs_reduce_fusion.2
  9.8 3.0 collective-permute-start
  12.8 4.0 fusion.34
  18.4 2.0 collective-permute-done.1
  20.5 2.4 fusion.49
  23.3 2.0 collective-permute-start.3
  25.7 2.3 fusion.50
  30.0 2.2 shard_map.64
  32.2 3.2 copy.53
  35.4 11.6 %collective-permute-done.2 = f16[512,1024]{1,0:T(8,128)(2,1)} collective-permute-done((f16[512,1024]{1,0:T(8,128)(2,1)}, f16[512,1024]{1,0:T(8,128)(2,1)}, u32[]{:S(2)}, u32[]{:S(2)}) %collective-permute-start.2) | collective-permute-done | bytes 1048608 | tf_op jit(solution)/shard_map/ppermute | solution.py:19
  52.7 3.8 shard_map.65
  56.6 3.0 copy-done
  59.5 3.0 copy-done.15
  62.5 2.5 constant_dynamic-update-slice_fusion.4
  65.0 2.5 constant_dynamic-update-slice_fusion.3
  67.5 2.5 constant_dynamic-update-slice_fusion.2
  72.0 3.0 copy.51
  76.2 4.7 %fusion = (bf16[2048,1024]{1,0:T(8,128)(2,1)}, bf16[2048,1024]{1,0:T(8,128)(2,1)S(1)}) fusion(f16[2048,1024]{1,0:T(8,128)(2,1)} %constant_dynamic-update-slice_fusion, f32[2048]{0:T(1024)S(1)} %bitcast.83), kind=kLoop, calls=%fused_computation.4 | loop fusion | flops 12582912 | bytes 12591104 | tf_op jit(solution)/shard_map/convert_element_type | solution.py:150
  81.2 4.0 fusion.20
  85.1 10.0 %collective-permute-done.8 = bf16[2,1,2,192,512]{4,3,2,1,0:T(8,128)(2,1)S(1)} collective-permute-done((bf16[2,1,2,192,512]{4,3,2,1,0:T(8,128)(2,1)S(1)}, bf16[2,1,2,192,512]{4,3,2,1,0:T(8,128)(2,1)S(1)}, u32[]{:S(2)}, u32[]{:S(2)}) %collective-permute-start.8) | collective-permute-done | bytes 786464 | tf_op jit(solution)/shard_map/ppermute | solution.py:19
  95.7 4.9 %fusion.1 = (bf16[2048,1024]{1,0:T(8,128)(2,1)}, bf16[2048,1024]{1,0:T(8,128)(2,1)S(1)}) fusion(f16[2048,1024]{1,0:T(8,128)(2,1)} %collective-permute-done.7, f32[2048]{0:T(1024)S(1)} %bitcast.82), kind=kLoop, calls=%fused_computation.5 | loop fusion | flops 12582912 | bytes 12591104 | tf_op jit(solution)/shard_map/convert_element_type | solution.py:150
  100.6 4.0 fusion.18
  113.7 11.6 %collective-permute-done.20 = bf16[2,2,1,192,512]{4,3,2,1,0:T(8,128)(2,1)S(1)} collective-permute-done((bf16[2,2,1,192,512]{4,3,2,1,0:T(8,128)(2,1)S(1)}, bf16[2,2,1,192,512]{4,3,2,1,0:T(8,128)(2,1)S(1)}, u32[]{:S(2)}, u32[]{:S(2)}) %collective-permute-start.20) | collective-permute-done | bytes 786464 | tf_op jit(solution)/shard_map/ppermute | solution.py:19
  126.1 2.0 fusion.95
  130.2 10.5 %collective-permute-done.10 = bf16[384,1024]{1,0:T(8,128)(2,1)} collective-permute-done((bf16[384,1024]{1,0:T(8,128)(2,1)S(1)}, bf16[384,1024]{1,0:T(8,128)(2,1)}, u32[]{:S(2)}, u32[]{:S(2)}) %collective-permute-start.10) | collective-permute-done | bytes 786464 | tf_op jit(solution)/shard_map/ppermute | solution.py:19
  144.8 2.6 collective-permute-start.19
  150.8 3.2 concatenate.126
  158.0 2.1 constant_dynamic-update-slice_fusion.13
  160.0 2.1 constant_dynamic-update-slice_fusion.12
  162.1 2.3 constant_dynamic-update-slice_fusion.9
  164.5 3.2 collective-permute-done.12
  172.8 2.3 constant_dynamic-update-slice_fusion.8
  175.1 2.3 constant_dynamic-update-slice_fusion.7
  181.3 3.5 collective-permute-done.23
  196.9 4.4 %fusion.22 = f32[512,1024]{1,0:T(8,128)S(1)} fusion(bf16[1536,512]{1,0:T(8,128)(2,1)} %bitcast.81, bf16[1536,1024]{1,0:T(8,128)(2,1)} %collective-permute-done.27, bf16[1536]{0:T(1024)(128)(2,1)S(1)} %neg.45, bf16[1536]{0:T(1024)(128)(2,1)S(1)} %min.58), kind=kOutput, calls=%fused_computation.51 | convolution fusion | flops 1613758464 | bytes 6821888 | tf_op jit(solution)/shard_map/dot_general | solution.py:145
  201.3 4.8 %add_convert_fusion = bf16[512,1024]{1,0:T(8,128)(2,1)} fusion(f32[512,1024]{1,0:T(8,128)S(1)} %fusion.22, bf16[1536,512]{1,0:T(8,128)(2,1)S(1)} %bitcast.80, bf16[1536,1024]{1,0:T(8,128)(2,1)} %constant_dynamic-update-slice_fusion.10, bf16[1536]{0:T(1024)(128)(2,1)S(1)} %neg.44, bf16[1536]{0:T(1024)(128)(2,1)S(1)} %min.55), kind=kOutput, calls=%fused_computation.77 | convolution fusion | flops 1614807040 | bytes 7870464 | tf_op jit(solution)/shard_map/dot_general | solution.py:145
  206.1 4.3 %fusion.12 = f32[384,1024]{1,0:T(8,128)S(1)} fusion(bf16[2048,1024]{1,0:T(8,128)(2,1)} %collective-permute-done.26, bf16[2048]{0:T(1024)(128)(2,1)S(1)} %neg.46, bf16[2048]{0:T(1024)(128)(2,1)S(1)} %bitcast.87, bf16[384,4096]{1,0:T(8,128)(2,1)S(1)} %shard_map.64), kind=kOutput, calls=%fused_computation.36 | convolution fusion | flops 1614807040 | bytes 7348224 | tf_op jit(solution)/shard_map/dot_general | solution.py:145
  210.4 4.3 %add_convert_fusion.2 = bf16[384,1024]{1,0:T(8,128)(2,1)S(1)} fusion(f32[384,1024]{1,0:T(8,128)S(1)} %fusion.12, bf16[2048,1024]{1,0:T(8,128)(2,1)} %constant_dynamic-update-slice_fusion.5, bf16[2048]{0:T(1024)(128)(2,1)S(1)} %neg.43, bf16[2048]{0:T(1024)(128)(2,1)S(1)} %bitcast.85, bf16[384,4096]{1,0:T(8,128)(2,1)S(1)} %shard_map.64), kind=kOutput, calls=%fused_computation.93 | convolution fusion | flops 1615593472 | bytes 8134656 | tf_op jit(solution)/shard_map/dot_general | solution.py:145
  215.4 2.7 fusion.4
  219.3 2.5 fusion.5
  222.4 2.8 fusion.107
  228.1 2.6 fusion.3
  230.8 3.3 collective-permute-done.30
  240.2 4.7 %collective-permute-done.36 = f16[32,4096]{1,0:T(8,128)(2,1)S(1)} collective-permute-done((f16[32,4096]{1,0:T(8,128)(2,1)S(1)}, f16[32,4096]{1,0:T(8,128)(2,1)S(1)}, u32[]{:S(2)}, u32[]{:S(2)}) %collective-permute-start.36) | collective-permute-done | bytes 262176 | tf_op jit(solution)/shard_map/ppermute | solution.py:19
  248.1 9.3 %collective-permute-done.32 = f16[64,4096]{1,0:T(8,128)(2,1)S(1)} collective-permute-done((f16[64,4096]{1,0:T(8,128)(2,1)S(1)}, f16[64,4096]{1,0:T(8,128)(2,1)S(1)}, u32[]{:S(2)}, u32[]{:S(2)}) %collective-permute-start.32) | collective-permute-done | bytes 524320 | tf_op jit(solution)/shard_map/ppermute | solution.py:19
  259.2 3.7 collective-permute-start.34
  262.9 3.7 collective-permute-done.37
  272.2 5.0 %collective-permute-done.44 = f16[2,1,2,64,512]{4,3,2,1,0:T(8,128)(2,1)S(1)} collective-permute-done((f16[2,1,2,64,512]{4,3,2,1,0:T(8,128)(2,1)}, f16[2,1,2,64,512]{4,3,2,1,0:T(8,128)(2,1)S(1)}, u32[]{:S(2)}, u32[]{:S(2)}) %collective-permute-start.44) | collective-permute-done | bytes 262176 | tf_op jit(solution)/shard_map/ppermute | solution.py:19
  278.7 2.2 collective-permute-start.47
  287.6 3.5 collective-permute-start.40
  291.1 5.6 %collective-permute-done.43 = f16[64,4096]{1,0:T(8,128)(2,1)} collective-permute-done((f16[64,4096]{1,0:T(8,128)(2,1)S(1)}, f16[64,4096]{1,0:T(8,128)(2,1)}, u32[]{:S(2)}, u32[]{:S(2)}) %collective-permute-start.43) | collective-permute-done | bytes 524320 | tf_op jit(solution)/shard_map/ppermute | solution.py:131
  302.2 2.9 copy.50
  310.0 2.2 copy-done.11
  312.2 9.6 %shard_map.68 = f32[256,1024]{1,0:T(8,128)S(1)} custom-call(f32[1,1]{1,0:T(1,128)} %bitcast.11.scale_ref, bf16[512,4096]{1,0:T(8,128)(2,1)S(1)} %pad_maximum_fusion.rows_ref, bf16[2048,1024]{1,0:T(8,128)(2,1)S(1)} %copy-done.7, bf16[2048,1024]{1,0:T(8,128)(2,1)S(1)} %copy-done.5, bf16[2048,1024]{1,0:T(8,128)(2,1)S(1)} %copy-done.11, ...), custom_call_target="tpu_custom_call" | custom-call | flops 6442450944 | bytes 22020100 | tf_op jit(solution)/shard_map/pallas_call | solution.py:215
  323.7 4.6 %collective-permute-start.42 = (f16[64,4096]{1,0:T(8,128)(2,1)S(1)}, f16[64,4096]{1,0:T(8,128)(2,1)S(1)}, u32[]{:S(2)}, u32[]{:S(2)}) collective-permute-start(f16[64,4096]{1,0:T(8,128)(2,1)S(1)} %select_select_fusion.1), channel_id=1, source_target_pairs={{3,1},{0,2},{1,0},{2,3},{7,5},{4,6},{5,4},{6,7},{11,9},{8,10},{9,8... | collective-permute-start | bytes 1572872 | tf_op jit(solution)/shard_map/ppermute | solution.py:131
  328.8 3.1 collective-permute-done.49
  336.9 2.5 collective-permute-done.50
  343.3 2.6 collective-permute-done.52
  351.1 9.8 %shard_map.69 = f32[256,1024]{1,0:T(8,128)S(1)} custom-call(f32[1,1]{1,0:T(1,128)} %bitcast.11.scale_ref, bf16[512,4096]{1,0:T(8,128)(2,1)S(1)} %pad_maximum_fusion.1.rows_ref, bf16[2048,1024]{1,0:T(8,128)(2,1)S(1)} %copy-done.7, bf16[2048,1024]{1,0:T(8,128)(2,1)S(1)} %copy-done.5, bf16[2048,1024]{1,0:T(8,128)(2,1)S(1)} %copy-done.12, ...), custom_call_target="tpu_custom_call" | custom-call | flops 6442450944 | bytes 22020100 | tf_op jit(solution)/shard_map/pallas_call | solution.py:215
  363.2 2.7 fusion.8
  366.0 9.5 %collective-permute-done.53 = f16[256,1024]{1,0:T(8,128)(2,1)S(1)} collective-permute-done((f16[256,1024]{1,0:T(8,128)(2,1)S(1)}, f16[256,1024]{1,0:T(8,128)(2,1)S(1)}, u32[]{:S(2)}, u32[]{:S(2)}) %collective-permute-start.53) | collective-permute-done | bytes 524320 | tf_op jit(solution)/shard_map/ppermute | solution.py:19
  380.8 9.5 %shard_map.70.base_ref = f32[512,1024]{1,0:T(8,128)S(1)} custom-call(f32[1,1]{1,0:T(1,128)} %bitcast.10.factor_ref, s32[4]{0:T(128)S(1)} %and_select_fusion.1.level_ref, f32[512,1024]{1,0:T(8,128)S(1)} %bitcast.55, bf16[4,512,1024]{2,1,0:T(8,128)(2,1)S(1)} %bitcast.58, bf16[4,512,1024]{2,1,0:T(8,128)(2,1)S(1)} %bitcast.60, ...), custom_call_target="tpu_custom_call" | custom-call | flops 6442450944 | bytes 20971540 | tf_op jit(solution)/shard_map/pallas_call | solution.py:215
  391.5 3.2 collective-permute-done.58
  395.7 10.2 %shard_map.71 = f32[512,1024]{1,0:T(8,128)} custom-call(f32[1,1]{1,0:T(1,128)} %bitcast.10.factor_ref, s32[4]{0:T(128)S(1)} %and_select_fusion.1.level_ref, f32[512,1024]{1,0:T(8,128)S(1)} %shard_map.70.base_ref, bf16[4,512,1024]{2,1,0:T(8,128)(2,1)S(1)} %bitcast.59, bf16[4,512,1024]{2,1,0:T(8,128)(2,1)S(1)} %bitcast.61, ...), custom_call_target="tpu_custom_call" | custom-call | flops 6442450944 | bytes 20971540 | tf_op jit(solution)/shard_map/pallas_call | solution.py:215
  (293 shorter events, 121.9 us)
Async XLA Ops:
  6.5 147.4 %all-gather.5.cloned.1.call-start = ((), (), s32[]{:S(2)}) async-start(), calls=%async_computation | async-start | bytes 5242880 | tf_op jit(solution)/shard_map/all_gather | solution.py:366
  9.8 7.0 %collective-permute-start = (f32[128]{0:T(128)S(1)}, f32[128]{0:T(128)S(1)}, u32[]{:S(2)}, u32[]{:S(2)}) collective-permute-start(f32[128]{0:T(128)S(1)} %broadcast_in_dim.24), channel_id=1, source_target_pairs={{0,8},{4,12},{8,0},{12,4},{16,24},{20,28},{24,16},{28,20},{1,9},{5... | collective-permute-start | bytes 1544 | tf_op jit(solution)/shard_map/ppermute | solution.py:19
  16.8 3.6 collective-permute-start.1
  22.9 183.2 %all-gather.7.cloned.1.call-start = ((), (), s32[]{:S(2)}) async-start(), calls=%async_computation.1 | async-start | bytes 5242880 | tf_op jit(solution)/shard_map/all_gather | solution.py:366
  23.2 23.9 %collective-permute-start.2 = (f16[512,1024]{1,0:T(8,128)(2,1)}, f16[512,1024]{1,0:T(8,128)(2,1)}, u32[]{:S(2)}, u32[]{:S(2)}) collective-permute-start(f16[512,1024]{1,0:T(8,128)(2,1)} %fusion.34), channel_id=1, source_target_pairs={{0,8},{4,12},{8,0},{12,4},{16,24},{20,28},{24,16},{28,20},{1,9},{5... | collective-permute-start | bytes 3145736 | tf_op jit(solution)/shard_map/ppermute | solution.py:19
  23.3 23.9 %collective-permute-start.3 = (f16[512,1024]{1,0:T(8,128)(2,1)}, f16[512,1024]{1,0:T(8,128)(2,1)}, u32[]{:S(2)}, u32[]{:S(2)}) collective-permute-start(f16[512,1024]{1,0:T(8,128)(2,1)} %fusion.34), channel_id=1, source_target_pairs={{0,16},{4,20},{8,24},{12,28},{16,0},{20,4},{24,8},{28,12},{1,17},{... | collective-permute-start | bytes 3145736 | tf_op jit(solution)/shard_map/ppermute | solution.py:19
  25.6 9.8 %collective-permute-start.4 = (f32[512]{0:T(512)S(1)}, f32[512]{0:T(512)S(1)}, u32[]{:S(2)}, u32[]{:S(2)}) collective-permute-start(f32[512]{0:T(512)S(1)} %pad_maximum_fusion.21), channel_id=1, source_target_pairs={{0,4},{4,0},{8,12},{12,8},{16,20},{20,16},{24,28},{28,24},{1,5},{5... | collective-permute-start | bytes 6152 | tf_op jit(solution)/shard_map/ppermute | solution.py:19
  32.1 20.6 %copy-start.1 = (bf16[4096,512]{1,0:T(8,128)(2,1)S(1)}, bf16[4096,512]{1,0:T(8,128)(2,1)}, u32[]{:S(2)}) copy-start(bf16[4096,512]{1,0:T(8,128)(2,1)} %weight_ref) | copy-start | bytes 12582916
  32.1 20.6 %copy-start.3 = (bf16[384,4096]{1,0:T(8,128)(2,1)S(1)}, bf16[384,4096]{1,0:T(8,128)(2,1)}, u32[]{:S(2)}) copy-start(bf16[384,4096]{1,0:T(8,128)(2,1)} %tok_ref) | copy-start | bytes 9437188
  48.3 21.7 %collective-permute-start.5 = (f16[256,1024]{1,0:T(8,128)(2,1)S(1)}, f16[256,1024]{1,0:T(8,128)(2,1)S(1)}, u32[]{:S(2)}, u32[]{:S(2)}) collective-permute-start(f16[256,1024]{1,0:T(8,128)(2,1)S(1)} %slice.199), channel_id=1, source_target_pairs={{0,16},{4,20},{8,24},{12,28},{16,0},{20,4},{24,8},{28,12},{1,17},{... | collective-permute-start | bytes 1572872 | tf_op jit(solution)/shard_map/ppermute | solution.py:19
  51.1 18.8 %collective-permute-start.6 = (f16[256,1024]{1,0:T(8,128)(2,1)S(1)}, f16[256,1024]{1,0:T(8,128)(2,1)S(1)}, u32[]{:S(2)}, u32[]{:S(2)}) collective-permute-start(f16[256,1024]{1,0:T(8,128)(2,1)S(1)} %slice.200), channel_id=1, source_target_pairs={{0,8},{4,12},{8,0},{12,4},{16,24},{20,28},{24,16},{28,20},{1,9},{5... | collective-permute-start | bytes 1572872 | tf_op jit(solution)/shard_map/ppermute | solution.py:19
  71.8 23.9 %collective-permute-start.7 = (f16[2048,1024]{1,0:T(8,128)(2,1)}, f16[2048,1024]{1,0:T(8,128)(2,1)}, u32[]{:S(2)}, u32[]{:S(2)}) collective-permute-start(f16[2048,1024]{1,0:T(8,128)(2,1)} %constant_dynamic-update-slice_fusion), channel_id=1, source_target_pairs={{0,4},{4,0},{8,12},{12,8},{16,20},{20,16},{24,28},{28,24},{1,5},{5... | collective-permute-start | bytes 12582920 | tf_op jit(solution)/shard_map/ppermute | solution.py:19
  75.1 20.0 %collective-permute-start.8 = (bf16[2,1,2,192,512]{4,3,2,1,0:T(8,128)(2,1)S(1)}, bf16[2,1,2,192,512]{4,3,2,1,0:T(8,128)(2,1)S(1)}, u32[]{:S(2)}, u32[]{:S(2)}) collective-permute-start(bf16[2,1,2,192,512]{4,3,2,1,0:T(8,128)(2,1)S(1)} %get-tuple-element.136), channel_id=1, source_target_pairs={{0,16},{4,20},{8,24},{12,28},{16,0},{20,4},{24,8},{28,12},{1,17},{... | collective-permute-start | bytes 2359304 | tf_op jit(solution)/shard_map/ppermute | solution.py:19
  75.8 19.7 %collective-permute-start.9 = (bf16[2,2,1,192,512]{4,3,2,1,0:T(8,128)(2,1)S(1)}, bf16[2,2,1,192,512]{4,3,2,1,0:T(8,128)(2,1)S(1)}, u32[]{:S(2)}, u32[]{:S(2)}) collective-permute-start(bf16[2,2,1,192,512]{4,3,2,1,0:T(8,128)(2,1)S(1)} %get-tuple-element.134), channel_id=1, source_target_pairs={{0,8},{4,12},{8,0},{12,4},{16,24},{20,28},{24,16},{28,20},{1,9},{5... | collective-permute-start | bytes 2359304 | tf_op jit(solution)/shard_map/ppermute | solution.py:19
  104.7 20.5 %collective-permute-start.20 = (bf16[2,2,1,192,512]{4,3,2,1,0:T(8,128)(2,1)S(1)}, bf16[2,2,1,192,512]{4,3,2,1,0:T(8,128)(2,1)S(1)}, u32[]{:S(2)}, u32[]{:S(2)}) collective-permute-start(bf16[2,2,1,192,512]{4,3,2,1,0:T(8,128)(2,1)S(1)} %get-tuple-element.160), channel_id=1, source_target_pairs={{0,8},{4,12},{8,0},{12,4},{16,24},{20,28},{24,16},{28,20},{1,9},{5... | collective-permute-start | bytes 2359304 | tf_op jit(solution)/shard_map/ppermute | solution.py:19
  105.3 20.5 %collective-permute-start.21 = (bf16[2,1,2,192,512]{4,3,2,1,0:T(8,128)(2,1)S(1)}, bf16[2,1,2,192,512]{4,3,2,1,0:T(8,128)(2,1)S(1)}, u32[]{:S(2)}, u32[]{:S(2)}) collective-permute-start(bf16[2,1,2,192,512]{4,3,2,1,0:T(8,128)(2,1)S(1)} %get-tuple-element.162), channel_id=1, source_target_pairs={{0,16},{4,20},{8,24},{12,28},{16,0},{20,4},{24,8},{28,12},{1,17},{... | collective-permute-start | bytes 2359304 | tf_op jit(solution)/shard_map/ppermute | solution.py:19
  108.7 32.1 %collective-permute-start.10 = (bf16[384,1024]{1,0:T(8,128)(2,1)S(1)}, bf16[384,1024]{1,0:T(8,128)(2,1)}, u32[]{:S(2)}, u32[]{:S(2)}) collective-permute-start(bf16[384,1024]{1,0:T(8,128)(2,1)S(1)} %get-tuple-element.158), channel_id=1, source_target_pairs={{0,8},{4,12},{8,0},{12,4},{16,24},{20,28},{24,16},{28,20},{1,9},{5... | collective-permute-start | bytes 2359304 | tf_op jit(solution)/shard_map/ppermute | solution.py:19
  110.2 31.1 %collective-permute-start.11 = (bf16[384,1024]{1,0:T(8,128)(2,1)S(1)}, bf16[384,1024]{1,0:T(8,128)(2,1)}, u32[]{:S(2)}, u32[]{:S(2)}) collective-permute-start(bf16[384,1024]{1,0:T(8,128)(2,1)S(1)} %get-tuple-element.158), channel_id=1, source_target_pairs={{0,16},{4,20},{8,24},{12,28},{16,0},{20,4},{24,8},{28,12},{1,17},{... | collective-permute-start | bytes 2359304 | tf_op jit(solution)/shard_map/ppermute | solution.py:19
  111.7 33.0 %collective-permute-start.18 = (f32[896]{0:T(1024)S(1)}, f32[896]{0:T(1024)S(1)}, u32[]{:S(2)}, u32[]{:S(2)}) collective-permute-start(f32[896]{0:T(1024)S(1)} %get-tuple-element.82), channel_id=1, source_target_pairs={{0,1},{1,0},{2,3},{3,2},{4,5},{5,4},{6,7},{7,6},{8,9},{9,8},{10,11... | collective-permute-start | bytes 10760 | tf_op jit(solution)/shard_map/ppermute | solution.py:139
  128.2 49.2 %collective-permute-start.22 = (bf16[1,2,2,384,512]{4,3,2,1,0:T(8,128)(2,1)}, bf16[1,2,2,384,512]{4,3,2,1,0:T(8,128)(2,1)}, u32[]{:S(2)}, u32[]{:S(2)}) collective-permute-start(bf16[1,2,2,384,512]{4,3,2,1,0:T(8,128)(2,1)} %get-tuple-element.132), channel_id=1, source_target_pairs={{0,4},{4,0},{8,12},{12,8},{16,20},{20,16},{24,28},{28,24},{1,5},{5... | collective-permute-start | bytes 4718600 | tf_op jit(solution)/shard_map/ppermute | solution.py:19
  141.2 26.4 %collective-permute-start.12 = (bf16[512,1024]{1,0:T(8,128)(2,1)}, bf16[512,1024]{1,0:T(8,128)(2,1)}, u32[]{:S(2)}, u32[]{:S(2)}) collective-permute-start(bf16[512,1024]{1,0:T(8,128)(2,1)} %slice.247), channel_id=1, source_target_pairs={{0,8},{4,12},{8,0},{12,4},{16,24},{20,28},{24,16},{28,20},{1,9},{5... | collective-permute-start | bytes 3145736 | tf_op jit(solution)/shard_map/ppermute | solution.py:19
  142.7 27.5 %collective-permute-start.13 = (bf16[512,1024]{1,0:T(8,128)(2,1)}, bf16[512,1024]{1,0:T(8,128)(2,1)}, u32[]{:S(2)}, u32[]{:S(2)}) collective-permute-start(bf16[512,1024]{1,0:T(8,128)(2,1)} %slice.247), channel_id=1, source_target_pairs={{0,16},{4,20},{8,24},{12,28},{16,0},{20,4},{24,8},{28,12},{1,17},{... | collective-permute-start | bytes 3145736 | tf_op jit(solution)/shard_map/ppermute | solution.py:19
  144.8 4.7 %collective-permute-start.19 = (f32[896]{0:T(1024)S(1)}, f32[896]{0:T(1024)S(1)}, u32[]{:S(2)}, u32[]{:S(2)}) collective-permute-start(f32[896]{0:T(1024)S(1)} %add.166), channel_id=1, source_target_pairs={{0,2},{1,3},{2,0},{3,1},{4,6},{5,7},{6,4},{7,5},{8,10},{9,11},{10,... | collective-permute-start | bytes 10760 | tf_op jit(solution)/shard_map/ppermute | solution.py:139
  155.0 24.1 %collective-permute-start.16 = (bf16[192,1024]{1,0:T(8,128)(2,1)S(1)}, bf16[192,1024]{1,0:T(8,128)(2,1)S(1)}, u32[]{:S(2)}, u32[]{:S(2)}) collective-permute-start(bf16[192,1024]{1,0:T(8,128)(2,1)S(1)} %slice.209), channel_id=1, source_target_pairs={{0,16},{4,20},{8,24},{12,28},{16,0},{20,4},{24,8},{28,12},{1,17},{... | collective-permute-start | bytes 1179656 | tf_op jit(solution)/shard_map/ppermute | solution.py:19
  156.8 22.3 %collective-permute-start.17 = (bf16[192,1024]{1,0:T(8,128)(2,1)S(1)}, bf16[192,1024]{1,0:T(8,128)(2,1)S(1)}, u32[]{:S(2)}, u32[]{:S(2)}) collective-permute-start(bf16[192,1024]{1,0:T(8,128)(2,1)S(1)} %slice.210), channel_id=1, source_target_pairs={{0,8},{4,12},{8,0},{12,4},{16,24},{20,28},{24,16},{28,20},{1,9},{5... | collective-permute-start | bytes 1179656 | tf_op jit(solution)/shard_map/ppermute | solution.py:19
  168.7 17.3 %collective-permute-start.14 = (bf16[256,1024]{1,0:T(8,128)(2,1)S(1)}, bf16[256,1024]{1,0:T(8,128)(2,1)S(1)}, u32[]{:S(2)}, u32[]{:S(2)}) collective-permute-start(bf16[256,1024]{1,0:T(8,128)(2,1)S(1)} %slice.248), channel_id=1, source_target_pairs={{0,16},{4,20},{8,24},{12,28},{16,0},{20,4},{24,8},{28,12},{1,17},{... | collective-permute-start | bytes 1572872 | tf_op jit(solution)/shard_map/ppermute | solution.py:19
  171.3 17.2 %collective-permute-start.15 = (bf16[256,1024]{1,0:T(8,128)(2,1)S(1)}, bf16[256,1024]{1,0:T(8,128)(2,1)S(1)}, u32[]{:S(2)}, u32[]{:S(2)}) collective-permute-start(bf16[256,1024]{1,0:T(8,128)(2,1)S(1)} %slice.249), channel_id=1, source_target_pairs={{0,8},{4,12},{8,0},{12,4},{16,24},{20,28},{24,16},{28,20},{1,9},{5... | collective-permute-start | bytes 1572872 | tf_op jit(solution)/shard_map/ppermute | solution.py:19
  179.1 5.7 %collective-permute-start.23 = (f32[1024]{0:T(1024)S(1)}, f32[1024]{0:T(1024)S(1)}, u32[]{:S(2)}, u32[]{:S(2)}) collective-permute-start(f32[1024]{0:T(1024)S(1)} %concatenate.126), channel_id=1, source_target_pairs={{0,8},{4,12},{8,0},{12,4},{16,24},{20,28},{24,16},{28,20},{1,9},{5... | collective-permute-start | bytes 12296 | tf_op jit(solution)/shard_map/ppermute | solution.py:19
  181.3 15.6 %collective-permute-start.27 = (bf16[1536,1024]{1,0:T(8,128)(2,1)}, bf16[1536,1024]{1,0:T(8,128)(2,1)}, u32[]{:S(2)}, u32[]{:S(2)}) collective-permute-start(bf16[1536,1024]{1,0:T(8,128)(2,1)} %constant_dynamic-update-slice_fusion.10), channel_id=1, source_target_pairs={{0,4},{4,0},{8,12},{12,8},{16,20},{20,16},{24,28},{28,24},{1,5},{5... | collective-permute-start | bytes 9437192 | tf_op jit(solution)/shard_map/ppermute | solution.py:19
  184.8 3.7 collective-permute-start.24
  188.4 1.2 collective-permute-start.25
  189.6 16.4 %collective-permute-start.26 = (bf16[2048,1024]{1,0:T(8,128)(2,1)}, bf16[2048,1024]{1,0:T(8,128)(2,1)}, u32[]{:S(2)}, u32[]{:S(2)}) collective-permute-start(bf16[2048,1024]{1,0:T(8,128)(2,1)} %constant_dynamic-update-slice_fusion.5), channel_id=1, source_target_pairs={{0,4},{4,0},{8,12},{12,8},{16,20},{20,16},{24,28},{28,24},{1,5},{5... | collective-permute-start | bytes 12582920 | tf_op jit(solution)/shard_map/ppermute | solution.py:19
  218.1 4.2 %collective-permute-start.28 = (f16[256,4096]{1,0:T(8,128)(2,1)S(1)}, f16[256,4096]{1,0:T(8,128)(2,1)S(1)}, u32[]{:S(2)}, u32[]{:S(2)}) collective-permute-start(f16[256,4096]{1,0:T(8,128)(2,1)S(1)} %fusion.4), channel_id=1, source_target_pairs={{0,4},{4,0},{8,12},{12,8},{16,20},{20,16},{24,28},{28,24},{1,5},{5... | collective-permute-start | bytes 6291464 | tf_op jit(solution)/shard_map/ppermute | solution.py:19
  221.8 6.4 %collective-permute-start.29 = (f16[256,4096]{1,0:T(8,128)(2,1)S(1)}, f16[256,4096]{1,0:T(8,128)(2,1)S(1)}, u32[]{:S(2)}, u32[]{:S(2)}) collective-permute-start(f16[256,4096]{1,0:T(8,128)(2,1)S(1)} %fusion.5), channel_id=1, source_target_pairs={{0,4},{4,0},{8,12},{12,8},{16,20},{20,16},{24,28},{28,24},{1,5},{5... | collective-permute-start | bytes 6291464 | tf_op jit(solution)/shard_map/ppermute | solution.py:19
  225.4 8.6 %collective-permute-start.30 = (f16[32,4096]{1,0:T(8,128)(2,1)S(1)}, f16[32,4096]{1,0:T(8,128)(2,1)S(1)}, u32[]{:S(2)}, u32[]{:S(2)}) collective-permute-start(f16[32,4096]{1,0:T(8,128)(2,1)S(1)} %get-tuple-element.156), channel_id=1, source_target_pairs={{0,8},{4,12},{8,0},{12,4},{16,24},{20,28},{24,16},{28,20},{1,9},{5... | collective-permute-start | bytes 786440 | tf_op jit(solution)/shard_map/ppermute | solution.py:19
  226.8 8.3 %collective-permute-start.31 = (f16[32,4096]{1,0:T(8,128)(2,1)S(1)}, f16[32,4096]{1,0:T(8,128)(2,1)S(1)}, u32[]{:S(2)}, u32[]{:S(2)}) collective-permute-start(f16[32,4096]{1,0:T(8,128)(2,1)S(1)} %get-tuple-element.155), channel_id=1, source_target_pairs={{0,16},{4,20},{8,24},{12,28},{16,0},{20,4},{24,8},{28,12},{1,17},{... | collective-permute-start | bytes 786440 | tf_op jit(solution)/shard_map/ppermute | solution.py:19
  235.5 9.3 %collective-permute-start.36 = (f16[32,4096]{1,0:T(8,128)(2,1)S(1)}, f16[32,4096]{1,0:T(8,128)(2,1)S(1)}, u32[]{:S(2)}, u32[]{:S(2)}) collective-permute-start(f16[32,4096]{1,0:T(8,128)(2,1)S(1)} %get-tuple-element.152), channel_id=1, source_target_pairs={{0,16},{4,20},{8,24},{12,28},{16,0},{20,4},{24,8},{28,12},{1,17},{... | collective-permute-start | bytes 786440 | tf_op jit(solution)/shard_map/ppermute | solution.py:19
  237.0 9.2 %collective-permute-start.38 = (f16[32,4096]{1,0:T(8,128)(2,1)S(1)}, f16[32,4096]{1,0:T(8,128)(2,1)S(1)}, u32[]{:S(2)}, u32[]{:S(2)}) collective-permute-start(f16[32,4096]{1,0:T(8,128)(2,1)S(1)} %get-tuple-element.151), channel_id=1, source_target_pairs={{0,8},{4,12},{8,0},{12,4},{16,24},{20,28},{24,16},{28,20},{1,9},{5... | collective-permute-start | bytes 786440 | tf_op jit(solution)/shard_map/ppermute | solution.py:19
  237.8 19.6 %collective-permute-start.32 = (f16[64,4096]{1,0:T(8,128)(2,1)S(1)}, f16[64,4096]{1,0:T(8,128)(2,1)S(1)}, u32[]{:S(2)}, u32[]{:S(2)}) collective-permute-start(f16[64,4096]{1,0:T(8,128)(2,1)S(1)} %pad_maximum_fusion.11), channel_id=1, source_target_pairs={{0,8},{4,12},{8,0},{12,4},{16,24},{20,28},{24,16},{28,20},{1,9},{5... | collective-permute-start | bytes 1572872 | tf_op jit(solution)/shard_map/ppermute | solution.py:19
  239.4 18.0 %collective-permute-start.33 = (f16[64,4096]{1,0:T(8,128)(2,1)S(1)}, f16[64,4096]{1,0:T(8,128)(2,1)S(1)}, u32[]{:S(2)}, u32[]{:S(2)}) collective-permute-start(f16[64,4096]{1,0:T(8,128)(2,1)S(1)} %pad_maximum_fusion.12), channel_id=1, source_target_pairs={{0,16},{4,20},{8,24},{12,28},{16,0},{20,4},{24,8},{28,12},{1,17},{... | collective-permute-start | bytes 1572872 | tf_op jit(solution)/shard_map/ppermute | solution.py:19
  246.5 20.1 %collective-permute-start.37 = (f16[64,4096]{1,0:T(8,128)(2,1)S(1)}, f16[64,4096]{1,0:T(8,128)(2,1)S(1)}, u32[]{:S(2)}, u32[]{:S(2)}) collective-permute-start(f16[64,4096]{1,0:T(8,128)(2,1)S(1)} %pad_maximum_fusion.13), channel_id=1, source_target_pairs={{0,8},{4,12},{8,0},{12,4},{16,24},{20,28},{24,16},{28,20},{1,9},{5... | collective-permute-start | bytes 1572872 | tf_op jit(solution)/shard_map/ppermute | solution.py:19
  247.2 19.3 %collective-permute-start.39 = (f16[64,4096]{1,0:T(8,128)(2,1)S(1)}, f16[64,4096]{1,0:T(8,128)(2,1)S(1)}, u32[]{:S(2)}, u32[]{:S(2)}) collective-permute-start(f16[64,4096]{1,0:T(8,128)(2,1)S(1)} %pad_maximum_fusion.14), channel_id=1, source_target_pairs={{0,16},{4,20},{8,24},{12,28},{16,0},{20,4},{24,8},{28,12},{1,17},{... | collective-permute-start | bytes 1572872 | tf_op jit(solution)/shard_map/ppermute | solution.py:19
  259.2 21.7 %collective-permute-start.34 = (f16[64,4096]{1,0:T(8,128)(2,1)S(1)}, f16[64,4096]{1,0:T(8,128)(2,1)}, u32[]{:S(2)}, u32[]{:S(2)}) collective-permute-start(f16[64,4096]{1,0:T(8,128)(2,1)S(1)} %convert_element_type.207), channel_id=1, source_target_pairs={{0,3},{1,0},{2,1},{3,2},{4,7},{5,4},{6,5},{7,6},{8,11},{9,8},{10,9... | collective-permute-start | bytes 1572872 | tf_op jit(solution)/shard_map/ppermute | solution.py:122
  262.9 19.5 %collective-permute-start.35 = (f16[64,4096]{1,0:T(8,128)(2,1)S(1)}, f16[64,4096]{1,0:T(8,128)(2,1)}, u32[]{:S(2)}, u32[]{:S(2)}) collective-permute-start(f16[64,4096]{1,0:T(8,128)(2,1)S(1)} %convert_element_type.207), channel_id=1, source_target_pairs={{0,1},{1,2},{2,3},{3,0},{4,5},{5,6},{6,7},{7,4},{8,9},{9,10},{10,1... | collective-permute-start | bytes 1572872 | tf_op jit(solution)/shard_map/ppermute | solution.py:122
  270.6 6.6 %collective-permute-start.44 = (f16[2,1,2,64,512]{4,3,2,1,0:T(8,128)(2,1)}, f16[2,1,2,64,512]{4,3,2,1,0:T(8,128)(2,1)S(1)}, u32[]{:S(2)}, u32[]{:S(2)}) collective-permute-start(f16[2,1,2,64,512]{4,3,2,1,0:T(8,128)(2,1)} %get-tuple-element.166), channel_id=1, source_target_pairs={{0,16},{4,20},{8,24},{12,28},{16,0},{20,4},{24,8},{28,12},{1,17},{... | collective-permute-start | bytes 786440 | tf_op jit(solution)/shard_map/ppermute | solution.py:19
  271.4 7.2 %collective-permute-start.46 = (f16[2,2,1,64,512]{4,3,2,1,0:T(8,128)(2,1)S(1)}, f16[2,2,1,64,512]{4,3,2,1,0:T(8,128)(2,1)S(1)}, u32[]{:S(2)}, u32[]{:S(2)}) collective-permute-start(f16[2,2,1,64,512]{4,3,2,1,0:T(8,128)(2,1)S(1)} %get-tuple-element.168), channel_id=1, source_target_pairs={{0,8},{4,12},{8,0},{12,4},{16,24},{20,28},{24,16},{28,20},{1,9},{5... | collective-permute-start | bytes 786440 | tf_op jit(solution)/shard_map/ppermute | solution.py:19
  277.3 7.3 %collective-permute-start.45 = (f16[2,2,1,64,512]{4,3,2,1,0:T(8,128)(2,1)S(1)}, f16[2,2,1,64,512]{4,3,2,1,0:T(8,128)(2,1)S(1)}, u32[]{:S(2)}, u32[]{:S(2)}) collective-permute-start(f16[2,2,1,64,512]{4,3,2,1,0:T(8,128)(2,1)S(1)} %get-tuple-element.170), channel_id=1, source_target_pairs={{0,8},{4,12},{8,0},{12,4},{16,24},{20,28},{24,16},{28,20},{1,9},{5... | collective-permute-start | bytes 786440 | tf_op jit(solution)/shard_map/ppermute | solution.py:19
  278.7 6.5 %collective-permute-start.47 = (f16[2,1,2,64,512]{4,3,2,1,0:T(8,128)(2,1)S(1)}, f16[2,1,2,64,512]{4,3,2,1,0:T(8,128)(2,1)S(1)}, u32[]{:S(2)}, u32[]{:S(2)}) collective-permute-start(f16[2,1,2,64,512]{4,3,2,1,0:T(8,128)(2,1)S(1)} %get-tuple-element.172), channel_id=1, source_target_pairs={{0,16},{4,20},{8,24},{12,28},{16,0},{20,4},{24,8},{28,12},{1,17},{... | collective-permute-start | bytes 786440 | tf_op jit(solution)/shard_map/ppermute | solution.py:19
  282.6 14.0 %collective-permute-start.43 = (f16[64,4096]{1,0:T(8,128)(2,1)S(1)}, f16[64,4096]{1,0:T(8,128)(2,1)}, u32[]{:S(2)}, u32[]{:S(2)}) collective-permute-start(f16[64,4096]{1,0:T(8,128)(2,1)S(1)} %select_select_fusion), channel_id=1, source_target_pairs={{3,1},{0,2},{1,0},{2,3},{7,5},{4,6},{5,4},{6,7},{11,9},{8,10},{9,8... | collective-permute-start | bytes 1572872 | tf_op jit(solution)/shard_map/ppermute | solution.py:131
  286.8 11.9 %collective-permute-start.48 = (f16[1,2,2,128,512]{4,3,2,1,0:T(8,128)(2,1)}, f16[1,2,2,128,512]{4,3,2,1,0:T(8,128)(2,1)}, u32[]{:S(2)}, u32[]{:S(2)}) collective-permute-start(f16[1,2,2,128,512]{4,3,2,1,0:T(8,128)(2,1)} %get-tuple-element.164), channel_id=1, source_target_pairs={{0,4},{4,0},{8,12},{12,8},{16,20},{20,16},{24,28},{28,24},{1,5},{5... | collective-permute-start | bytes 1572872 | tf_op jit(solution)/shard_map/ppermute | solution.py:19
  287.6 35.7 %collective-permute-start.40 = (f16[64,4096]{1,0:T(8,128)(2,1)S(1)}, f16[64,4096]{1,0:T(8,128)(2,1)}, u32[]{:S(2)}, u32[]{:S(2)}) collective-permute-start(f16[64,4096]{1,0:T(8,128)(2,1)S(1)} %convert_element_type.212), channel_id=1, source_target_pairs={{0,3},{1,0},{2,1},{3,2},{4,7},{5,4},{6,5},{7,6},{8,11},{9,8},{10,9... | collective-permute-start | bytes 1572872 | tf_op jit(solution)/shard_map/ppermute | solution.py:122
  291.1 32.2 %collective-permute-start.41 = (f16[64,4096]{1,0:T(8,128)(2,1)S(1)}, f16[64,4096]{1,0:T(8,128)(2,1)}, u32[]{:S(2)}, u32[]{:S(2)}) collective-permute-start(f16[64,4096]{1,0:T(8,128)(2,1)S(1)} %convert_element_type.212), channel_id=1, source_target_pairs={{0,1},{1,2},{2,3},{3,0},{4,5},{5,6},{6,7},{7,4},{8,9},{9,10},{10,1... | collective-permute-start | bytes 1572872 | tf_op jit(solution)/shard_map/ppermute | solution.py:122
  322.7 9.2 %collective-permute-start.49 = (f16[256,1024]{1,0:T(8,128)(2,1)S(1)}, f16[256,1024]{1,0:T(8,128)(2,1)S(1)}, u32[]{:S(2)}, u32[]{:S(2)}) collective-permute-start(f16[256,1024]{1,0:T(8,128)(2,1)S(1)} %get-tuple-element.118), channel_id=1, source_target_pairs={{0,8},{4,12},{8,0},{12,4},{16,24},{20,28},{24,16},{28,20},{1,9},{5... | collective-permute-start | bytes 1572872 | tf_op jit(solution)/shard_map/ppermute | solution.py:19
  323.7 11.3 %collective-permute-start.42 = (f16[64,4096]{1,0:T(8,128)(2,1)S(1)}, f16[64,4096]{1,0:T(8,128)(2,1)S(1)}, u32[]{:S(2)}, u32[]{:S(2)}) collective-permute-start(f16[64,4096]{1,0:T(8,128)(2,1)S(1)} %select_select_fusion.1), channel_id=1, source_target_pairs={{3,1},{0,2},{1,0},{2,3},{7,5},{4,6},{5,4},{6,7},{11,9},{8,10},{9,8... | collective-permute-start | bytes 1572872 | tf_op jit(solution)/shard_map/ppermute | solution.py:131
  328.3 11.1 %collective-permute-start.50 = (f16[256,1024]{1,0:T(8,128)(2,1)S(1)}, f16[256,1024]{1,0:T(8,128)(2,1)S(1)}, u32[]{:S(2)}, u32[]{:S(2)}) collective-permute-start(f16[256,1024]{1,0:T(8,128)(2,1)S(1)} %get-tuple-element.118), channel_id=1, source_target_pairs={{0,16},{4,20},{8,24},{12,28},{16,0},{20,4},{24,8},{28,12},{1,17},{... | collective-permute-start | bytes 1572872 | tf_op jit(solution)/shard_map/ppermute | solution.py:19
  331.9 10.6 %collective-permute-start.51 = (f16[128,1024]{1,0:T(8,128)(2,1)S(1)}, f16[128,1024]{1,0:T(8,128)(2,1)S(1)}, u32[]{:S(2)}, u32[]{:S(2)}) collective-permute-start(f16[128,1024]{1,0:T(8,128)(2,1)S(1)} %slice.271), channel_id=1, source_target_pairs={{0,16},{4,20},{8,24},{12,28},{16,0},{20,4},{24,8},{28,12},{1,17},{... | collective-permute-start | bytes 786440 | tf_op jit(solution)/shard_map/ppermute | solution.py:19
  339.4 6.4 %collective-permute-start.52 = (f16[128,1024]{1,0:T(8,128)(2,1)S(1)}, f16[128,1024]{1,0:T(8,128)(2,1)S(1)}, u32[]{:S(2)}, u32[]{:S(2)}) collective-permute-start(f16[128,1024]{1,0:T(8,128)(2,1)S(1)} %slice.272), channel_id=1, source_target_pairs={{0,8},{4,12},{8,0},{12,4},{16,24},{20,28},{24,16},{28,20},{1,9},{5... | collective-permute-start | bytes 786440 | tf_op jit(solution)/shard_map/ppermute | solution.py:19
  347.6 30.5 %collective-permute-start.57 = (f16[1024,1024]{1,0:T(8,128)(2,1)}, f16[1024,1024]{1,0:T(8,128)(2,1)S(1)}, u32[]{:S(2)}, u32[]{:S(2)}) collective-permute-start(f16[1024,1024]{1,0:T(8,128)(2,1)} %constant_dynamic-update-slice_fusion.15), channel_id=1, source_target_pairs={{0,4},{4,0},{8,12},{12,8},{16,20},{20,16},{24,28},{28,24},{1,5},{5... | collective-permute-start | bytes 6291464 | tf_op jit(solution)/shard_map/ppermute | solution.py:19
  361.1 14.4 %collective-permute-start.53 = (f16[256,1024]{1,0:T(8,128)(2,1)S(1)}, f16[256,1024]{1,0:T(8,128)(2,1)S(1)}, u32[]{:S(2)}, u32[]{:S(2)}) collective-permute-start(f16[256,1024]{1,0:T(8,128)(2,1)S(1)} %get-tuple-element.116), channel_id=1, source_target_pairs={{0,8},{4,12},{8,0},{12,4},{16,24},{20,28},{24,16},{28,20},{1,9},{5... | collective-permute-start | bytes 1572872 | tf_op jit(solution)/shard_map/ppermute | solution.py:19
  362.4 14.0 %collective-permute-start.55 = (f16[256,1024]{1,0:T(8,128)(2,1)S(1)}, f16[256,1024]{1,0:T(8,128)(2,1)S(1)}, u32[]{:S(2)}, u32[]{:S(2)}) collective-permute-start(f16[256,1024]{1,0:T(8,128)(2,1)S(1)} %get-tuple-element.116), channel_id=1, source_target_pairs={{0,16},{4,20},{8,24},{12,28},{16,0},{20,4},{24,8},{28,12},{1,17},{... | collective-permute-start | bytes 1572872 | tf_op jit(solution)/shard_map/ppermute | solution.py:19
  363.2 15.7 %copy-start.17 = (bf16[2048,1024]{1,0:T(8,128)(2,1)S(1)}, bf16[2048,1024]{1,0:T(8,128)(2,1)}, u32[]{:S(2)}) copy-start(bf16[2048,1024]{1,0:T(8,128)(2,1)} %all-gather.7.cloned.1.call-done) | copy-start | bytes 12582916
  375.5 14.8 %collective-permute-start.54 = (f16[128,1024]{1,0:T(8,128)(2,1)S(1)}, f16[128,1024]{1,0:T(8,128)(2,1)S(1)}, u32[]{:S(2)}, u32[]{:S(2)}) collective-permute-start(f16[128,1024]{1,0:T(8,128)(2,1)S(1)} %slice.273), channel_id=1, source_target_pairs={{0,16},{4,20},{8,24},{12,28},{16,0},{20,4},{24,8},{28,12},{1,17},{... | collective-permute-start | bytes 786440 | tf_op jit(solution)/shard_map/ppermute | solution.py:19
  376.5 13.9 %collective-permute-start.56 = (f16[128,1024]{1,0:T(8,128)(2,1)S(1)}, f16[128,1024]{1,0:T(8,128)(2,1)S(1)}, u32[]{:S(2)}, u32[]{:S(2)}) collective-permute-start(f16[128,1024]{1,0:T(8,128)(2,1)S(1)} %slice.274), channel_id=1, source_target_pairs={{0,8},{4,12},{8,0},{12,4},{16,24},{20,28},{24,16},{28,20},{1,9},{5... | collective-permute-start | bytes 786440 | tf_op jit(solution)/shard_map/ppermute | solution.py:19
  390.5 4.2 %collective-permute-start.58 = (f16[1024,1024]{1,0:T(8,128)(2,1)S(1)}, f16[1024,1024]{1,0:T(8,128)(2,1)S(1)}, u32[]{:S(2)}, u32[]{:S(2)}) collective-permute-start(f16[1024,1024]{1,0:T(8,128)(2,1)S(1)} %constant_dynamic-update-slice_fusion.20), channel_id=1, source_target_pairs={{0,4},{4,0},{8,12},{12,8},{16,20},{20,16},{24,28},{28,24},{1,5},{5... | collective-permute-start | bytes 6291464 | tf_op jit(solution)/shard_map/ppermute | solution.py:19
  (28 other events, 126.8 us)
Sparse Core Ops, SparseCore 0:
  23.0 81.1 all-gather.4
  105.8 79.4 all-gather.6

commit v4 on v3

--- a/solution.py
+++ b/solution.py
@@ -483,8 +483,8 @@
             cross_near = second_step(cross, came)
     for c, pair in enumerate(cross_pairs):
         result = add_product(result, factor, levels, c, rows_terms, [split(x.astype(F32)) for x in pair])
+    came, result = tie(came, result)
     far = far_step(cross, came)
-    far, result = tie(far, result)
     cross_near = join(cross, came, far)
     pair = (cross_near, swap(cross_near, 1))
     terms = [split(x.astype(F32)) for x in pair]

time: 418 us -> 416 us (level)
  transfers between devices with their start and end apart: 61 -> 61, of which waited for: 32 -> 33; matrix products, arithmetic and copies ran while one was open for 30% -> 31% of each run, Pallas kernels for 9% -> 9%
where the time goes in v4:
time: 416 us; the launch traced here: 410 us
  waiting for transfers between devices  114 us (27%)
  local copies, waits for them, and re-layouts  79.1 us (19%)
  starting transfers between devices  64.7 us (16%)
  Pallas kernels  48.4 us (12%)
  other arithmetic  43 us (10%)
  matrix products  42.4 us (10%)
  between operations  19 us (5%)
    ppermute x51, waiting for transfers between devices, swap(): return lax.ppermute(x, 'dp', [(i, i ^ mask) for i in range(n)])  104 us
    unnamed x95, local copies, waits for them, and re-layouts  49 us
    ppermute x51, starting transfers between devices, swap(): return lax.ppermute(x, 'dp', [(i, i ^ mask) for i in range(n)])  46.5 us
    dot_general x12, matrix products, dot(): lax.dot_general(a, b, (((ca,), (cb,)), ((), ())), preferred_element_type=...  41 us
    pallas_call x4, Pallas kernels, plain_call(): pl.pallas_call(body, out_shape=out, grid=grid, in_specs=in_specs, out_spe...  39.2 us
    convert_element_type x8, other arithmetic, split(): return (high.astype(BF16), (x - high).astype(BF16))  16.8 us
    pallas_call x4, Pallas kernels, ordered_call(): pl.pallas_call(body, out_shape=outs, grid_spec=pltpu.PrefetchScalarGridSp...  9.2 us
  transfers between devices with their start and end apart: 61, of which 33 were waited for; matrix products, arithmetic and copies ran while one was open for 31% of the time, Pallas kernels for 9%

profile of v4, /device:TPU:0, one launch (start us, length us, event | category | flops | bytes accessed | tf_op | source)
XLA Modules:
  0.0 410.3 jit_solution(7237847566576187868)
XLA Ops:
  6.5 2.5 abs_reduce_fusion.2
  9.8 3.0 collective-permute-start
  12.8 4.0 fusion.34
  18.4 2.0 collective-permute-done.1
  20.5 2.4 fusion.49
  23.3 2.0 collective-permute-start.3
  25.7 2.3 fusion.50
  30.0 2.2 shard_map.64
  32.2 3.2 copy.53
  35.4 11.6 %collective-permute-done.2 = f16[512,1024]{1,0:T(8,128)(2,1)} collective-permute-done((f16[512,1024]{1,0:T(8,128)(2,1)}, f16[512,1024]{1,0:T(8,128)(2,1)}, u32[]{:S(2)}, u32[]{:S(2)}) %collective-permute-start.2) | collective-permute-done | bytes 1048608 | tf_op jit(solution)/shard_map/ppermute | solution.py:19
  52.7 3.8 shard_map.65
  56.6 3.0 copy-done
  59.5 3.0 copy-done.15
  62.5 2.5 constant_dynamic-update-slice_fusion.4
  65.0 2.5 constant_dynamic-update-slice_fusion.3
  67.5 2.5 constant_dynamic-update-slice_fusion.2
  72.0 3.0 copy.51
  76.2 4.7 %fusion = (bf16[2048,1024]{1,0:T(8,128)(2,1)}, bf16[2048,1024]{1,0:T(8,128)(2,1)S(1)}) fusion(f16[2048,1024]{1,0:T(8,128)(2,1)} %constant_dynamic-update-slice_fusion, f32[2048]{0:T(1024)S(1)} %bitcast.83), kind=kLoop, calls=%fused_computation.4 | loop fusion | flops 12582912 | bytes 12591104 | tf_op jit(solution)/shard_map/convert_element_type | solution.py:150
  81.2 4.0 fusion.20
  85.1 10.0 %collective-permute-done.8 = bf16[2,1,2,192,512]{4,3,2,1,0:T(8,128)(2,1)S(1)} collective-permute-done((bf16[2,1,2,192,512]{4,3,2,1,0:T(8,128)(2,1)S(1)}, bf16[2,1,2,192,512]{4,3,2,1,0:T(8,128)(2,1)S(1)}, u32[]{:S(2)}, u32[]{:S(2)}) %collective-permute-start.8) | collective-permute-done | bytes 786464 | tf_op jit(solution)/shard_map/ppermute | solution.py:19
  95.7 4.9 %fusion.1 = (bf16[2048,1024]{1,0:T(8,128)(2,1)}, bf16[2048,1024]{1,0:T(8,128)(2,1)S(1)}) fusion(f16[2048,1024]{1,0:T(8,128)(2,1)} %collective-permute-done.7, f32[2048]{0:T(1024)S(1)} %bitcast.82), kind=kLoop, calls=%fused_computation.5 | loop fusion | flops 12582912 | bytes 12591104 | tf_op jit(solution)/shard_map/convert_element_type | solution.py:150
  100.6 4.0 fusion.18
  113.7 11.6 %collective-permute-done.20 = bf16[2,2,1,192,512]{4,3,2,1,0:T(8,128)(2,1)S(1)} collective-permute-done((bf16[2,2,1,192,512]{4,3,2,1,0:T(8,128)(2,1)S(1)}, bf16[2,2,1,192,512]{4,3,2,1,0:T(8,128)(2,1)S(1)}, u32[]{:S(2)}, u32[]{:S(2)}) %collective-permute-start.20) | collective-permute-done | bytes 786464 | tf_op jit(solution)/shard_map/ppermute | solution.py:19
  126.1 2.0 fusion.95
  130.2 10.5 %collective-permute-done.10 = bf16[384,1024]{1,0:T(8,128)(2,1)} collective-permute-done((bf16[384,1024]{1,0:T(8,128)(2,1)S(1)}, bf16[384,1024]{1,0:T(8,128)(2,1)}, u32[]{:S(2)}, u32[]{:S(2)}) %collective-permute-start.10) | collective-permute-done | bytes 786464 | tf_op jit(solution)/shard_map/ppermute | solution.py:19
  144.8 2.6 collective-permute-start.19
  150.8 3.2 concatenate.126
  158.0 2.1 constant_dynamic-update-slice_fusion.13
  160.0 2.1 constant_dynamic-update-slice_fusion.12
  162.1 2.3 constant_dynamic-update-slice_fusion.9
  164.5 3.2 collective-permute-done.12
  172.8 2.3 constant_dynamic-update-slice_fusion.8
  175.1 2.3 constant_dynamic-update-slice_fusion.7
  181.3 3.5 collective-permute-done.23
  196.9 4.4 %fusion.22 = f32[512,1024]{1,0:T(8,128)S(1)} fusion(bf16[1536,512]{1,0:T(8,128)(2,1)} %bitcast.81, bf16[1536,1024]{1,0:T(8,128)(2,1)} %collective-permute-done.27, bf16[1536]{0:T(1024)(128)(2,1)S(1)} %neg.45, bf16[1536]{0:T(1024)(128)(2,1)S(1)} %min.58), kind=kOutput, calls=%fused_computation.51 | convolution fusion | flops 1613758464 | bytes 6821888 | tf_op jit(solution)/shard_map/dot_general | solution.py:145
  201.3 4.8 %add_convert_fusion = bf16[512,1024]{1,0:T(8,128)(2,1)} fusion(f32[512,1024]{1,0:T(8,128)S(1)} %fusion.22, bf16[1536,512]{1,0:T(8,128)(2,1)S(1)} %bitcast.80, bf16[1536,1024]{1,0:T(8,128)(2,1)} %constant_dynamic-update-slice_fusion.10, bf16[1536]{0:T(1024)(128)(2,1)S(1)} %neg.44, bf16[1536]{0:T(1024)(128)(2,1)S(1)} %min.55), kind=kOutput, calls=%fused_computation.77 | convolution fusion | flops 1614807040 | bytes 7870464 | tf_op jit(solution)/shard_map/dot_general | solution.py:145
  206.1 4.3 %fusion.12 = f32[384,1024]{1,0:T(8,128)S(1)} fusion(bf16[2048,1024]{1,0:T(8,128)(2,1)} %collective-permute-done.26, bf16[2048]{0:T(1024)(128)(2,1)S(1)} %neg.46, bf16[2048]{0:T(1024)(128)(2,1)S(1)} %bitcast.87, bf16[384,4096]{1,0:T(8,128)(2,1)S(1)} %shard_map.64), kind=kOutput, calls=%fused_computation.36 | convolution fusion | flops 1614807040 | bytes 7348224 | tf_op jit(solution)/shard_map/dot_general | solution.py:145
  210.4 4.3 %add_convert_fusion.2 = bf16[384,1024]{1,0:T(8,128)(2,1)S(1)} fusion(f32[384,1024]{1,0:T(8,128)S(1)} %fusion.12, bf16[2048,1024]{1,0:T(8,128)(2,1)} %constant_dynamic-update-slice_fusion.5, bf16[2048]{0:T(1024)(128)(2,1)S(1)} %neg.43, bf16[2048]{0:T(1024)(128)(2,1)S(1)} %bitcast.85, bf16[384,4096]{1,0:T(8,128)(2,1)S(1)} %shard_map.64), kind=kOutput, calls=%fused_computation.93 | convolution fusion | flops 1615593472 | bytes 8134656 | tf_op jit(solution)/shard_map/dot_general | solution.py:145
  215.4 2.7 fusion.4
  219.3 2.5 fusion.5
  222.4 2.8 fusion.107
  228.1 2.6 fusion.3
  230.8 3.3 collective-permute-done.30
  240.2 4.7 %collective-permute-done.36 = f16[32,4096]{1,0:T(8,128)(2,1)S(1)} collective-permute-done((f16[32,4096]{1,0:T(8,128)(2,1)S(1)}, f16[32,4096]{1,0:T(8,128)(2,1)S(1)}, u32[]{:S(2)}, u32[]{:S(2)}) %collective-permute-start.36) | collective-permute-done | bytes 262176 | tf_op jit(solution)/shard_map/ppermute | solution.py:19
  248.1 9.3 %collective-permute-done.32 = f16[64,4096]{1,0:T(8,128)(2,1)S(1)} collective-permute-done((f16[64,4096]{1,0:T(8,128)(2,1)S(1)}, f16[64,4096]{1,0:T(8,128)(2,1)S(1)}, u32[]{:S(2)}, u32[]{:S(2)}) %collective-permute-start.32) | collective-permute-done | bytes 524320 | tf_op jit(solution)/shard_map/ppermute | solution.py:19
  259.2 3.7 collective-permute-start.34
  262.9 3.7 collective-permute-done.37
  272.2 5.0 %collective-permute-done.44 = f16[2,1,2,64,512]{4,3,2,1,0:T(8,128)(2,1)S(1)} collective-permute-done((f16[2,1,2,64,512]{4,3,2,1,0:T(8,128)(2,1)}, f16[2,1,2,64,512]{4,3,2,1,0:T(8,128)(2,1)S(1)}, u32[]{:S(2)}, u32[]{:S(2)}) %collective-permute-start.44) | collective-permute-done | bytes 262176 | tf_op jit(solution)/shard_map/ppermute | solution.py:19
  278.7 2.2 collective-permute-start.47
  287.6 3.5 collective-permute-start.40
  291.1 5.6 %collective-permute-done.43 = f16[64,4096]{1,0:T(8,128)(2,1)} collective-permute-done((f16[64,4096]{1,0:T(8,128)(2,1)S(1)}, f16[64,4096]{1,0:T(8,128)(2,1)}, u32[]{:S(2)}, u32[]{:S(2)}) %collective-permute-start.43) | collective-permute-done | bytes 524320 | tf_op jit(solution)/shard_map/ppermute | solution.py:131
  302.2 2.9 copy.50
  310.0 2.2 copy-done.11
  312.2 9.6 %shard_map.68 = f32[256,1024]{1,0:T(8,128)S(1)} custom-call(f32[1,1]{1,0:T(1,128)} %bitcast.11.scale_ref, bf16[512,4096]{1,0:T(8,128)(2,1)S(1)} %pad_maximum_fusion.rows_ref, bf16[2048,1024]{1,0:T(8,128)(2,1)S(1)} %copy-done.7, bf16[2048,1024]{1,0:T(8,128)(2,1)S(1)} %copy-done.5, bf16[2048,1024]{1,0:T(8,128)(2,1)S(1)} %copy-done.11, ...), custom_call_target="tpu_custom_call" | custom-call | flops 6442450944 | bytes 22020100 | tf_op jit(solution)/shard_map/pallas_call | solution.py:215
  323.7 4.6 %collective-permute-start.42 = (f16[64,4096]{1,0:T(8,128)(2,1)S(1)}, f16[64,4096]{1,0:T(8,128)(2,1)S(1)}, u32[]{:S(2)}, u32[]{:S(2)}) collective-permute-start(f16[64,4096]{1,0:T(8,128)(2,1)S(1)} %select_select_fusion.1), channel_id=1, source_target_pairs={{3,1},{0,2},{1,0},{2,3},{7,5},{4,6},{5,4},{6,7},{11,9},{8,10},{9,8... | collective-permute-start | bytes 1572872 | tf_op jit(solution)/shard_map/ppermute | solution.py:131
  328.8 3.1 collective-permute-done.49
  336.9 2.5 collective-permute-done.50
  343.3 2.6 collective-permute-done.52
  351.0 9.8 %shard_map.69 = f32[256,1024]{1,0:T(8,128)S(1)} custom-call(f32[1,1]{1,0:T(1,128)} %bitcast.11.scale_ref, bf16[512,4096]{1,0:T(8,128)(2,1)S(1)} %pad_maximum_fusion.1.rows_ref, bf16[2048,1024]{1,0:T(8,128)(2,1)S(1)} %copy-done.7, bf16[2048,1024]{1,0:T(8,128)(2,1)S(1)} %copy-done.5, bf16[2048,1024]{1,0:T(8,128)(2,1)S(1)} %copy-done.12, ...), custom_call_target="tpu_custom_call" | custom-call | flops 6442450944 | bytes 22020100 | tf_op jit(solution)/shard_map/pallas_call | solution.py:215
  363.1 2.7 fusion.8
  368.6 9.5 %shard_map.70.base_ref = f32[512,1024]{1,0:T(8,128)S(1)} custom-call(f32[1,1]{1,0:T(1,128)} %bitcast.10.factor_ref, s32[4]{0:T(128)S(1)} %and_select_fusion.1.level_ref, f32[512,1024]{1,0:T(8,128)S(1)} %bitcast.55, bf16[4,512,1024]{2,1,0:T(8,128)(2,1)S(1)} %bitcast.58, bf16[4,512,1024]{2,1,0:T(8,128)(2,1)S(1)} %bitcast.60, ...), custom_call_target="tpu_custom_call" | custom-call | flops 6442450944 | bytes 20971540 | tf_op jit(solution)/shard_map/pallas_call | solution.py:215
  380.6 5.9 %collective-permute-done.56 = f16[128,1024]{1,0:T(8,128)(2,1)S(1)} collective-permute-done((f16[128,1024]{1,0:T(8,128)(2,1)S(1)}, f16[128,1024]{1,0:T(8,128)(2,1)S(1)}, u32[]{:S(2)}, u32[]{:S(2)}) %collective-permute-start.56) | collective-permute-done | bytes 262176 | tf_op jit(solution)/shard_map/ppermute | solution.py:19
  388.6 3.2 collective-permute-done.58
  392.8 10.2 %shard_map.71 = f32[512,1024]{1,0:T(8,128)} custom-call(f32[1,1]{1,0:T(1,128)} %bitcast.10.factor_ref, s32[4]{0:T(128)S(1)} %and_select_fusion.1.level_ref, f32[512,1024]{1,0:T(8,128)S(1)} %shard_map.70.base_ref, bf16[4,512,1024]{2,1,0:T(8,128)(2,1)S(1)} %bitcast.59, bf16[4,512,1024]{2,1,0:T(8,128)(2,1)S(1)} %bitcast.61, ...), custom_call_target="tpu_custom_call" | custom-call | flops 6442450944 | bytes 20971540 | tf_op jit(solution)/shard_map/pallas_call | solution.py:215
  (293 shorter events, 122.6 us)
Async XLA Ops:
  6.5 147.4 %all-gather.5.cloned.1.call-start = ((), (), s32[]{:S(2)}) async-start(), calls=%async_computation | async-start | bytes 5242880 | tf_op jit(solution)/shard_map/all_gather | solution.py:366
  9.8 7.0 %collective-permute-start = (f32[128]{0:T(128)S(1)}, f32[128]{0:T(128)S(1)}, u32[]{:S(2)}, u32[]{:S(2)}) collective-permute-start(f32[128]{0:T(128)S(1)} %broadcast_in_dim.24), channel_id=1, source_target_pairs={{0,8},{4,12},{8,0},{12,4},{16,24},{20,28},{24,16},{28,20},{1,9},{5... | collective-permute-start | bytes 1544 | tf_op jit(solution)/shard_map/ppermute | solution.py:19
  16.8 3.6 collective-permute-start.1
  22.9 183.2 %all-gather.7.cloned.1.call-start = ((), (), s32[]{:S(2)}) async-start(), calls=%async_computation.1 | async-start | bytes 5242880 | tf_op jit(solution)/shard_map/all_gather | solution.py:366
  23.2 23.9 %collective-permute-start.2 = (f16[512,1024]{1,0:T(8,128)(2,1)}, f16[512,1024]{1,0:T(8,128)(2,1)}, u32[]{:S(2)}, u32[]{:S(2)}) collective-permute-start(f16[512,1024]{1,0:T(8,128)(2,1)} %fusion.34), channel_id=1, source_target_pairs={{0,8},{4,12},{8,0},{12,4},{16,24},{20,28},{24,16},{28,20},{1,9},{5... | collective-permute-start | bytes 3145736 | tf_op jit(solution)/shard_map/ppermute | solution.py:19
  23.3 23.9 %collective-permute-start.3 = (f16[512,1024]{1,0:T(8,128)(2,1)}, f16[512,1024]{1,0:T(8,128)(2,1)}, u32[]{:S(2)}, u32[]{:S(2)}) collective-permute-start(f16[512,1024]{1,0:T(8,128)(2,1)} %fusion.34), channel_id=1, source_target_pairs={{0,16},{4,20},{8,24},{12,28},{16,0},{20,4},{24,8},{28,12},{1,17},{... | collective-permute-start | bytes 3145736 | tf_op jit(solution)/shard_map/ppermute | solution.py:19
  25.6 9.8 %collective-permute-start.4 = (f32[512]{0:T(512)S(1)}, f32[512]{0:T(512)S(1)}, u32[]{:S(2)}, u32[]{:S(2)}) collective-permute-start(f32[512]{0:T(512)S(1)} %pad_maximum_fusion.21), channel_id=1, source_target_pairs={{0,4},{4,0},{8,12},{12,8},{16,20},{20,16},{24,28},{28,24},{1,5},{5... | collective-permute-start | bytes 6152 | tf_op jit(solution)/shard_map/ppermute | solution.py:19
  32.1 20.6 %copy-start.1 = (bf16[4096,512]{1,0:T(8,128)(2,1)S(1)}, bf16[4096,512]{1,0:T(8,128)(2,1)}, u32[]{:S(2)}) copy-start(bf16[4096,512]{1,0:T(8,128)(2,1)} %weight_ref) | copy-start | bytes 12582916
  32.1 20.6 %copy-start.3 = (bf16[384,4096]{1,0:T(8,128)(2,1)S(1)}, bf16[384,4096]{1,0:T(8,128)(2,1)}, u32[]{:S(2)}) copy-start(bf16[384,4096]{1,0:T(8,128)(2,1)} %tok_ref) | copy-start | bytes 9437188
  48.3 21.7 %collective-permute-start.5 = (f16[256,1024]{1,0:T(8,128)(2,1)S(1)}, f16[256,1024]{1,0:T(8,128)(2,1)S(1)}, u32[]{:S(2)}, u32[]{:S(2)}) collective-permute-start(f16[256,1024]{1,0:T(8,128)(2,1)S(1)} %slice.199), channel_id=1, source_target_pairs={{0,16},{4,20},{8,24},{12,28},{16,0},{20,4},{24,8},{28,12},{1,17},{... | collective-permute-start | bytes 1572872 | tf_op jit(solution)/shard_map/ppermute | solution.py:19
  51.1 18.8 %collective-permute-start.6 = (f16[256,1024]{1,0:T(8,128)(2,1)S(1)}, f16[256,1024]{1,0:T(8,128)(2,1)S(1)}, u32[]{:S(2)}, u32[]{:S(2)}) collective-permute-start(f16[256,1024]{1,0:T(8,128)(2,1)S(1)} %slice.200), channel_id=1, source_target_pairs={{0,8},{4,12},{8,0},{12,4},{16,24},{20,28},{24,16},{28,20},{1,9},{5... | collective-permute-start | bytes 1572872 | tf_op jit(solution)/shard_map/ppermute | solution.py:19
  71.8 23.9 %collective-permute-start.7 = (f16[2048,1024]{1,0:T(8,128)(2,1)}, f16[2048,1024]{1,0:T(8,128)(2,1)}, u32[]{:S(2)}, u32[]{:S(2)}) collective-permute-start(f16[2048,1024]{1,0:T(8,128)(2,1)} %constant_dynamic-update-slice_fusion), channel_id=1, source_target_pairs={{0,4},{4,0},{8,12},{12,8},{16,20},{20,16},{24,28},{28,24},{1,5},{5... | collective-permute-start | bytes 12582920 | tf_op jit(solution)/shard_map/ppermute | solution.py:19
  75.1 20.0 %collective-permute-start.8 = (bf16[2,1,2,192,512]{4,3,2,1,0:T(8,128)(2,1)S(1)}, bf16[2,1,2,192,512]{4,3,2,1,0:T(8,128)(2,1)S(1)}, u32[]{:S(2)}, u32[]{:S(2)}) collective-permute-start(bf16[2,1,2,192,512]{4,3,2,1,0:T(8,128)(2,1)S(1)} %get-tuple-element.136), channel_id=1, source_target_pairs={{0,16},{4,20},{8,24},{12,28},{16,0},{20,4},{24,8},{28,12},{1,17},{... | collective-permute-start | bytes 2359304 | tf_op jit(solution)/shard_map/ppermute | solution.py:19
  75.8 19.7 %collective-permute-start.9 = (bf16[2,2,1,192,512]{4,3,2,1,0:T(8,128)(2,1)S(1)}, bf16[2,2,1,192,512]{4,3,2,1,0:T(8,128)(2,1)S(1)}, u32[]{:S(2)}, u32[]{:S(2)}) collective-permute-start(bf16[2,2,1,192,512]{4,3,2,1,0:T(8,128)(2,1)S(1)} %get-tuple-element.134), channel_id=1, source_target_pairs={{0,8},{4,12},{8,0},{12,4},{16,24},{20,28},{24,16},{28,20},{1,9},{5... | collective-permute-start | bytes 2359304 | tf_op jit(solution)/shard_map/ppermute | solution.py:19
  104.7 20.5 %collective-permute-start.20 = (bf16[2,2,1,192,512]{4,3,2,1,0:T(8,128)(2,1)S(1)}, bf16[2,2,1,192,512]{4,3,2,1,0:T(8,128)(2,1)S(1)}, u32[]{:S(2)}, u32[]{:S(2)}) collective-permute-start(bf16[2,2,1,192,512]{4,3,2,1,0:T(8,128)(2,1)S(1)} %get-tuple-element.160), channel_id=1, source_target_pairs={{0,8},{4,12},{8,0},{12,4},{16,24},{20,28},{24,16},{28,20},{1,9},{5... | collective-permute-start | bytes 2359304 | tf_op jit(solution)/shard_map/ppermute | solution.py:19
  105.3 20.5 %collective-permute-start.21 = (bf16[2,1,2,192,512]{4,3,2,1,0:T(8,128)(2,1)S(1)}, bf16[2,1,2,192,512]{4,3,2,1,0:T(8,128)(2,1)S(1)}, u32[]{:S(2)}, u32[]{:S(2)}) collective-permute-start(bf16[2,1,2,192,512]{4,3,2,1,0:T(8,128)(2,1)S(1)} %get-tuple-element.162), channel_id=1, source_target_pairs={{0,16},{4,20},{8,24},{12,28},{16,0},{20,4},{24,8},{28,12},{1,17},{... | collective-permute-start | bytes 2359304 | tf_op jit(solution)/shard_map/ppermute | solution.py:19
  108.7 32.1 %collective-permute-start.10 = (bf16[384,1024]{1,0:T(8,128)(2,1)S(1)}, bf16[384,1024]{1,0:T(8,128)(2,1)}, u32[]{:S(2)}, u32[]{:S(2)}) collective-permute-start(bf16[384,1024]{1,0:T(8,128)(2,1)S(1)} %get-tuple-element.158), channel_id=1, source_target_pairs={{0,8},{4,12},{8,0},{12,4},{16,24},{20,28},{24,16},{28,20},{1,9},{5... | collective-permute-start | bytes 2359304 | tf_op jit(solution)/shard_map/ppermute | solution.py:19
  110.2 31.1 %collective-permute-start.11 = (bf16[384,1024]{1,0:T(8,128)(2,1)S(1)}, bf16[384,1024]{1,0:T(8,128)(2,1)}, u32[]{:S(2)}, u32[]{:S(2)}) collective-permute-start(bf16[384,1024]{1,0:T(8,128)(2,1)S(1)} %get-tuple-element.158), channel_id=1, source_target_pairs={{0,16},{4,20},{8,24},{12,28},{16,0},{20,4},{24,8},{28,12},{1,17},{... | collective-permute-start | bytes 2359304 | tf_op jit(solution)/shard_map/ppermute | solution.py:19
  111.7 33.0 %collective-permute-start.18 = (f32[896]{0:T(1024)S(1)}, f32[896]{0:T(1024)S(1)}, u32[]{:S(2)}, u32[]{:S(2)}) collective-permute-start(f32[896]{0:T(1024)S(1)} %get-tuple-element.82), channel_id=1, source_target_pairs={{0,1},{1,0},{2,3},{3,2},{4,5},{5,4},{6,7},{7,6},{8,9},{9,8},{10,11... | collective-permute-start | bytes 10760 | tf_op jit(solution)/shard_map/ppermute | solution.py:139
  128.2 49.2 %collective-permute-start.22 = (bf16[1,2,2,384,512]{4,3,2,1,0:T(8,128)(2,1)}, bf16[1,2,2,384,512]{4,3,2,1,0:T(8,128)(2,1)}, u32[]{:S(2)}, u32[]{:S(2)}) collective-permute-start(bf16[1,2,2,384,512]{4,3,2,1,0:T(8,128)(2,1)} %get-tuple-element.132), channel_id=1, source_target_pairs={{0,4},{4,0},{8,12},{12,8},{16,20},{20,16},{24,28},{28,24},{1,5},{5... | collective-permute-start | bytes 4718600 | tf_op jit(solution)/shard_map/ppermute | solution.py:19
  141.2 26.4 %collective-permute-start.12 = (bf16[512,1024]{1,0:T(8,128)(2,1)}, bf16[512,1024]{1,0:T(8,128)(2,1)}, u32[]{:S(2)}, u32[]{:S(2)}) collective-permute-start(bf16[512,1024]{1,0:T(8,128)(2,1)} %slice.247), channel_id=1, source_target_pairs={{0,8},{4,12},{8,0},{12,4},{16,24},{20,28},{24,16},{28,20},{1,9},{5... | collective-permute-start | bytes 3145736 | tf_op jit(solution)/shard_map/ppermute | solution.py:19
  142.7 27.5 %collective-permute-start.13 = (bf16[512,1024]{1,0:T(8,128)(2,1)}, bf16[512,1024]{1,0:T(8,128)(2,1)}, u32[]{:S(2)}, u32[]{:S(2)}) collective-permute-start(bf16[512,1024]{1,0:T(8,128)(2,1)} %slice.247), channel_id=1, source_target_pairs={{0,16},{4,20},{8,24},{12,28},{16,0},{20,4},{24,8},{28,12},{1,17},{... | collective-permute-start | bytes 3145736 | tf_op jit(solution)/shard_map/ppermute | solution.py:19
  144.8 4.7 %collective-permute-start.19 = (f32[896]{0:T(1024)S(1)}, f32[896]{0:T(1024)S(1)}, u32[]{:S(2)}, u32[]{:S(2)}) collective-permute-start(f32[896]{0:T(1024)S(1)} %add.166), channel_id=1, source_target_pairs={{0,2},{1,3},{2,0},{3,1},{4,6},{5,7},{6,4},{7,5},{8,10},{9,11},{10,... | collective-permute-start | bytes 10760 | tf_op jit(solution)/shard_map/ppermute | solution.py:139
  155.0 24.1 %collective-permute-start.16 = (bf16[192,1024]{1,0:T(8,128)(2,1)S(1)}, bf16[192,1024]{1,0:T(8,128)(2,1)S(1)}, u32[]{:S(2)}, u32[]{:S(2)}) collective-permute-start(bf16[192,1024]{1,0:T(8,128)(2,1)S(1)} %slice.209), channel_id=1, source_target_pairs={{0,16},{4,20},{8,24},{12,28},{16,0},{20,4},{24,8},{28,12},{1,17},{... | collective-permute-start | bytes 1179656 | tf_op jit(solution)/shard_map/ppermute | solution.py:19
  156.8 22.3 %collective-permute-start.17 = (bf16[192,1024]{1,0:T(8,128)(2,1)S(1)}, bf16[192,1024]{1,0:T(8,128)(2,1)S(1)}, u32[]{:S(2)}, u32[]{:S(2)}) collective-permute-start(bf16[192,1024]{1,0:T(8,128)(2,1)S(1)} %slice.210), channel_id=1, source_target_pairs={{0,8},{4,12},{8,0},{12,4},{16,24},{20,28},{24,16},{28,20},{1,9},{5... | collective-permute-start | bytes 1179656 | tf_op jit(solution)/shard_map/ppermute | solution.py:19
  164.5 12.9 %copy-start.20 = (bf16[1,2,2,384,512]{4,3,2,1,0:T(8,128)(2,1)S(1)}, bf16[1,2,2,384,512]{4,3,2,1,0:T(8,128)(2,1)}, u32[]{:S(2)}) copy-start(bf16[1,2,2,384,512]{4,3,2,1,0:T(8,128)(2,1)} %get-tuple-element.131) | copy-start | bytes 4718596
  168.7 17.3 %collective-permute-start.14 = (bf16[256,1024]{1,0:T(8,128)(2,1)S(1)}, bf16[256,1024]{1,0:T(8,128)(2,1)S(1)}, u32[]{:S(2)}, u32[]{:S(2)}) collective-permute-start(bf16[256,1024]{1,0:T(8,128)(2,1)S(1)} %slice.248), channel_id=1, source_target_pairs={{0,16},{4,20},{8,24},{12,28},{16,0},{20,4},{24,8},{28,12},{1,17},{... | collective-permute-start | bytes 1572872 | tf_op jit(solution)/shard_map/ppermute | solution.py:19
  171.3 17.2 %collective-permute-start.15 = (bf16[256,1024]{1,0:T(8,128)(2,1)S(1)}, bf16[256,1024]{1,0:T(8,128)(2,1)S(1)}, u32[]{:S(2)}, u32[]{:S(2)}) collective-permute-start(bf16[256,1024]{1,0:T(8,128)(2,1)S(1)} %slice.249), channel_id=1, source_target_pairs={{0,8},{4,12},{8,0},{12,4},{16,24},{20,28},{24,16},{28,20},{1,9},{5... | collective-permute-start | bytes 1572872 | tf_op jit(solution)/shard_map/ppermute | solution.py:19
  179.1 5.7 %collective-permute-start.23 = (f32[1024]{0:T(1024)S(1)}, f32[1024]{0:T(1024)S(1)}, u32[]{:S(2)}, u32[]{:S(2)}) collective-permute-start(f32[1024]{0:T(1024)S(1)} %concatenate.126), channel_id=1, source_target_pairs={{0,8},{4,12},{8,0},{12,4},{16,24},{20,28},{24,16},{28,20},{1,9},{5... | collective-permute-start | bytes 12296 | tf_op jit(solution)/shard_map/ppermute | solution.py:19
  181.3 15.6 %collective-permute-start.27 = (bf16[1536,1024]{1,0:T(8,128)(2,1)}, bf16[1536,1024]{1,0:T(8,128)(2,1)}, u32[]{:S(2)}, u32[]{:S(2)}) collective-permute-start(bf16[1536,1024]{1,0:T(8,128)(2,1)} %constant_dynamic-update-slice_fusion.10), channel_id=1, source_target_pairs={{0,4},{4,0},{8,12},{12,8},{16,20},{20,16},{24,28},{28,24},{1,5},{5... | collective-permute-start | bytes 9437192 | tf_op jit(solution)/shard_map/ppermute | solution.py:19
  184.8 3.7 collective-permute-start.24
  188.4 1.2 collective-permute-start.25
  189.6 16.4 %collective-permute-start.26 = (bf16[2048,1024]{1,0:T(8,128)(2,1)}, bf16[2048,1024]{1,0:T(8,128)(2,1)}, u32[]{:S(2)}, u32[]{:S(2)}) collective-permute-start(bf16[2048,1024]{1,0:T(8,128)(2,1)} %constant_dynamic-update-slice_fusion.5), channel_id=1, source_target_pairs={{0,4},{4,0},{8,12},{12,8},{16,20},{20,16},{24,28},{28,24},{1,5},{5... | collective-permute-start | bytes 12582920 | tf_op jit(solution)/shard_map/ppermute | solution.py:19
  218.1 4.2 %collective-permute-start.28 = (f16[256,4096]{1,0:T(8,128)(2,1)S(1)}, f16[256,4096]{1,0:T(8,128)(2,1)S(1)}, u32[]{:S(2)}, u32[]{:S(2)}) collective-permute-start(f16[256,4096]{1,0:T(8,128)(2,1)S(1)} %fusion.4), channel_id=1, source_target_pairs={{0,4},{4,0},{8,12},{12,8},{16,20},{20,16},{24,28},{28,24},{1,5},{5... | collective-permute-start | bytes 6291464 | tf_op jit(solution)/shard_map/ppermute | solution.py:19
  221.8 6.4 %collective-permute-start.29 = (f16[256,4096]{1,0:T(8,128)(2,1)S(1)}, f16[256,4096]{1,0:T(8,128)(2,1)S(1)}, u32[]{:S(2)}, u32[]{:S(2)}) collective-permute-start(f16[256,4096]{1,0:T(8,128)(2,1)S(1)} %fusion.5), channel_id=1, source_target_pairs={{0,4},{4,0},{8,12},{12,8},{16,20},{20,16},{24,28},{28,24},{1,5},{5... | collective-permute-start | bytes 6291464 | tf_op jit(solution)/shard_map/ppermute | solution.py:19
  225.4 8.6 %collective-permute-start.30 = (f16[32,4096]{1,0:T(8,128)(2,1)S(1)}, f16[32,4096]{1,0:T(8,128)(2,1)S(1)}, u32[]{:S(2)}, u32[]{:S(2)}) collective-permute-start(f16[32,4096]{1,0:T(8,128)(2,1)S(1)} %get-tuple-element.156), channel_id=1, source_target_pairs={{0,8},{4,12},{8,0},{12,4},{16,24},{20,28},{24,16},{28,20},{1,9},{5... | collective-permute-start | bytes 786440 | tf_op jit(solution)/shard_map/ppermute | solution.py:19
  226.8 8.3 %collective-permute-start.31 = (f16[32,4096]{1,0:T(8,128)(2,1)S(1)}, f16[32,4096]{1,0:T(8,128)(2,1)S(1)}, u32[]{:S(2)}, u32[]{:S(2)}) collective-permute-start(f16[32,4096]{1,0:T(8,128)(2,1)S(1)} %get-tuple-element.155), channel_id=1, source_target_pairs={{0,16},{4,20},{8,24},{12,28},{16,0},{20,4},{24,8},{28,12},{1,17},{... | collective-permute-start | bytes 786440 | tf_op jit(solution)/shard_map/ppermute | solution.py:19
  235.5 9.3 %collective-permute-start.36 = (f16[32,4096]{1,0:T(8,128)(2,1)S(1)}, f16[32,4096]{1,0:T(8,128)(2,1)S(1)}, u32[]{:S(2)}, u32[]{:S(2)}) collective-permute-start(f16[32,4096]{1,0:T(8,128)(2,1)S(1)} %get-tuple-element.152), channel_id=1, source_target_pairs={{0,16},{4,20},{8,24},{12,28},{16,0},{20,4},{24,8},{28,12},{1,17},{... | collective-permute-start | bytes 786440 | tf_op jit(solution)/shard_map/ppermute | solution.py:19
  237.0 9.2 %collective-permute-start.38 = (f16[32,4096]{1,0:T(8,128)(2,1)S(1)}, f16[32,4096]{1,0:T(8,128)(2,1)S(1)}, u32[]{:S(2)}, u32[]{:S(2)}) collective-permute-start(f16[32,4096]{1,0:T(8,128)(2,1)S(1)} %get-tuple-element.151), channel_id=1, source_target_pairs={{0,8},{4,12},{8,0},{12,4},{16,24},{20,28},{24,16},{28,20},{1,9},{5... | collective-permute-start | bytes 786440 | tf_op jit(solution)/shard_map/ppermute | solution.py:19
  237.8 19.6 %collective-permute-start.32 = (f16[64,4096]{1,0:T(8,128)(2,1)S(1)}, f16[64,4096]{1,0:T(8,128)(2,1)S(1)}, u32[]{:S(2)}, u32[]{:S(2)}) collective-permute-start(f16[64,4096]{1,0:T(8,128)(2,1)S(1)} %pad_maximum_fusion.11), channel_id=1, source_target_pairs={{0,8},{4,12},{8,0},{12,4},{16,24},{20,28},{24,16},{28,20},{1,9},{5... | collective-permute-start | bytes 1572872 | tf_op jit(solution)/shard_map/ppermute | solution.py:19
  239.4 18.0 %collective-permute-start.33 = (f16[64,4096]{1,0:T(8,128)(2,1)S(1)}, f16[64,4096]{1,0:T(8,128)(2,1)S(1)}, u32[]{:S(2)}, u32[]{:S(2)}) collective-permute-start(f16[64,4096]{1,0:T(8,128)(2,1)S(1)} %pad_maximum_fusion.12), channel_id=1, source_target_pairs={{0,16},{4,20},{8,24},{12,28},{16,0},{20,4},{24,8},{28,12},{1,17},{... | collective-permute-start | bytes 1572872 | tf_op jit(solution)/shard_map/ppermute | solution.py:19
  246.5 20.1 %collective-permute-start.37 = (f16[64,4096]{1,0:T(8,128)(2,1)S(1)}, f16[64,4096]{1,0:T(8,128)(2,1)S(1)}, u32[]{:S(2)}, u32[]{:S(2)}) collective-permute-start(f16[64,4096]{1,0:T(8,128)(2,1)S(1)} %pad_maximum_fusion.13), channel_id=1, source_target_pairs={{0,8},{4,12},{8,0},{12,4},{16,24},{20,28},{24,16},{28,20},{1,9},{5... | collective-permute-start | bytes 1572872 | tf_op jit(solution)/shard_map/ppermute | solution.py:19
  247.2 19.3 %collective-permute-start.39 = (f16[64,4096]{1,0:T(8,128)(2,1)S(1)}, f16[64,4096]{1,0:T(8,128)(2,1)S(1)}, u32[]{:S(2)}, u32[]{:S(2)}) collective-permute-start(f16[64,4096]{1,0:T(8,128)(2,1)S(1)} %pad_maximum_fusion.14), channel_id=1, source_target_pairs={{0,16},{4,20},{8,24},{12,28},{16,0},{20,4},{24,8},{28,12},{1,17},{... | collective-permute-start | bytes 1572872 | tf_op jit(solution)/shard_map/ppermute | solution.py:19
  259.2 21.7 %collective-permute-start.34 = (f16[64,4096]{1,0:T(8,128)(2,1)S(1)}, f16[64,4096]{1,0:T(8,128)(2,1)}, u32[]{:S(2)}, u32[]{:S(2)}) collective-permute-start(f16[64,4096]{1,0:T(8,128)(2,1)S(1)} %convert_element_type.207), channel_id=1, source_target_pairs={{0,3},{1,0},{2,1},{3,2},{4,7},{5,4},{6,5},{7,6},{8,11},{9,8},{10,9... | collective-permute-start | bytes 1572872 | tf_op jit(solution)/shard_map/ppermute | solution.py:122
  262.9 19.5 %collective-permute-start.35 = (f16[64,4096]{1,0:T(8,128)(2,1)S(1)}, f16[64,4096]{1,0:T(8,128)(2,1)}, u32[]{:S(2)}, u32[]{:S(2)}) collective-permute-start(f16[64,4096]{1,0:T(8,128)(2,1)S(1)} %convert_element_type.207), channel_id=1, source_target_pairs={{0,1},{1,2},{2,3},{3,0},{4,5},{5,6},{6,7},{7,4},{8,9},{9,10},{10,1... | collective-permute-start | bytes 1572872 | tf_op jit(solution)/shard_map/ppermute | solution.py:122
  270.6 6.6 %collective-permute-start.44 = (f16[2,1,2,64,512]{4,3,2,1,0:T(8,128)(2,1)}, f16[2,1,2,64,512]{4,3,2,1,0:T(8,128)(2,1)S(1)}, u32[]{:S(2)}, u32[]{:S(2)}) collective-permute-start(f16[2,1,2,64,512]{4,3,2,1,0:T(8,128)(2,1)} %get-tuple-element.166), channel_id=1, source_target_pairs={{0,16},{4,20},{8,24},{12,28},{16,0},{20,4},{24,8},{28,12},{1,17},{... | collective-permute-start | bytes 786440 | tf_op jit(solution)/shard_map/ppermute | solution.py:19
  271.4 7.2 %collective-permute-start.46 = (f16[2,2,1,64,512]{4,3,2,1,0:T(8,128)(2,1)S(1)}, f16[2,2,1,64,512]{4,3,2,1,0:T(8,128)(2,1)S(1)}, u32[]{:S(2)}, u32[]{:S(2)}) collective-permute-start(f16[2,2,1,64,512]{4,3,2,1,0:T(8,128)(2,1)S(1)} %get-tuple-element.168), channel_id=1, source_target_pairs={{0,8},{4,12},{8,0},{12,4},{16,24},{20,28},{24,16},{28,20},{1,9},{5... | collective-permute-start | bytes 786440 | tf_op jit(solution)/shard_map/ppermute | solution.py:19
  277.3 7.3 %collective-permute-start.45 = (f16[2,2,1,64,512]{4,3,2,1,0:T(8,128)(2,1)S(1)}, f16[2,2,1,64,512]{4,3,2,1,0:T(8,128)(2,1)S(1)}, u32[]{:S(2)}, u32[]{:S(2)}) collective-permute-start(f16[2,2,1,64,512]{4,3,2,1,0:T(8,128)(2,1)S(1)} %get-tuple-element.170), channel_id=1, source_target_pairs={{0,8},{4,12},{8,0},{12,4},{16,24},{20,28},{24,16},{28,20},{1,9},{5... | collective-permute-start | bytes 786440 | tf_op jit(solution)/shard_map/ppermute | solution.py:19
  278.7 6.5 %collective-permute-start.47 = (f16[2,1,2,64,512]{4,3,2,1,0:T(8,128)(2,1)S(1)}, f16[2,1,2,64,512]{4,3,2,1,0:T(8,128)(2,1)S(1)}, u32[]{:S(2)}, u32[]{:S(2)}) collective-permute-start(f16[2,1,2,64,512]{4,3,2,1,0:T(8,128)(2,1)S(1)} %get-tuple-element.172), channel_id=1, source_target_pairs={{0,16},{4,20},{8,24},{12,28},{16,0},{20,4},{24,8},{28,12},{1,17},{... | collective-permute-start | bytes 786440 | tf_op jit(solution)/shard_map/ppermute | solution.py:19
  282.6 14.0 %collective-permute-start.43 = (f16[64,4096]{1,0:T(8,128)(2,1)S(1)}, f16[64,4096]{1,0:T(8,128)(2,1)}, u32[]{:S(2)}, u32[]{:S(2)}) collective-permute-start(f16[64,4096]{1,0:T(8,128)(2,1)S(1)} %select_select_fusion), channel_id=1, source_target_pairs={{3,1},{0,2},{1,0},{2,3},{7,5},{4,6},{5,4},{6,7},{11,9},{8,10},{9,8... | collective-permute-start | bytes 1572872 | tf_op jit(solution)/shard_map/ppermute | solution.py:131
  286.8 11.9 %collective-permute-start.48 = (f16[1,2,2,128,512]{4,3,2,1,0:T(8,128)(2,1)}, f16[1,2,2,128,512]{4,3,2,1,0:T(8,128)(2,1)}, u32[]{:S(2)}, u32[]{:S(2)}) collective-permute-start(f16[1,2,2,128,512]{4,3,2,1,0:T(8,128)(2,1)} %get-tuple-element.164), channel_id=1, source_target_pairs={{0,4},{4,0},{8,12},{12,8},{16,20},{20,16},{24,28},{28,24},{1,5},{5... | collective-permute-start | bytes 1572872 | tf_op jit(solution)/shard_map/ppermute | solution.py:19
  287.6 35.7 %collective-permute-start.40 = (f16[64,4096]{1,0:T(8,128)(2,1)S(1)}, f16[64,4096]{1,0:T(8,128)(2,1)}, u32[]{:S(2)}, u32[]{:S(2)}) collective-permute-start(f16[64,4096]{1,0:T(8,128)(2,1)S(1)} %convert_element_type.212), channel_id=1, source_target_pairs={{0,3},{1,0},{2,1},{3,2},{4,7},{5,4},{6,5},{7,6},{8,11},{9,8},{10,9... | collective-permute-start | bytes 1572872 | tf_op jit(solution)/shard_map/ppermute | solution.py:122
  291.1 32.2 %collective-permute-start.41 = (f16[64,4096]{1,0:T(8,128)(2,1)S(1)}, f16[64,4096]{1,0:T(8,128)(2,1)}, u32[]{:S(2)}, u32[]{:S(2)}) collective-permute-start(f16[64,4096]{1,0:T(8,128)(2,1)S(1)} %convert_element_type.212), channel_id=1, source_target_pairs={{0,1},{1,2},{2,3},{3,0},{4,5},{5,6},{6,7},{7,4},{8,9},{9,10},{10,1... | collective-permute-start | bytes 1572872 | tf_op jit(solution)/shard_map/ppermute | solution.py:122
  322.7 9.2 %collective-permute-start.49 = (f16[256,1024]{1,0:T(8,128)(2,1)S(1)}, f16[256,1024]{1,0:T(8,128)(2,1)S(1)}, u32[]{:S(2)}, u32[]{:S(2)}) collective-permute-start(f16[256,1024]{1,0:T(8,128)(2,1)S(1)} %get-tuple-element.118), channel_id=1, source_target_pairs={{0,8},{4,12},{8,0},{12,4},{16,24},{20,28},{24,16},{28,20},{1,9},{5... | collective-permute-start | bytes 1572872 | tf_op jit(solution)/shard_map/ppermute | solution.py:19
  323.7 11.3 %collective-permute-start.42 = (f16[64,4096]{1,0:T(8,128)(2,1)S(1)}, f16[64,4096]{1,0:T(8,128)(2,1)S(1)}, u32[]{:S(2)}, u32[]{:S(2)}) collective-permute-start(f16[64,4096]{1,0:T(8,128)(2,1)S(1)} %select_select_fusion.1), channel_id=1, source_target_pairs={{3,1},{0,2},{1,0},{2,3},{7,5},{4,6},{5,4},{6,7},{11,9},{8,10},{9,8... | collective-permute-start | bytes 1572872 | tf_op jit(solution)/shard_map/ppermute | solution.py:131
  328.3 11.1 %collective-permute-start.50 = (f16[256,1024]{1,0:T(8,128)(2,1)S(1)}, f16[256,1024]{1,0:T(8,128)(2,1)S(1)}, u32[]{:S(2)}, u32[]{:S(2)}) collective-permute-start(f16[256,1024]{1,0:T(8,128)(2,1)S(1)} %get-tuple-element.118), channel_id=1, source_target_pairs={{0,16},{4,20},{8,24},{12,28},{16,0},{20,4},{24,8},{28,12},{1,17},{... | collective-permute-start | bytes 1572872 | tf_op jit(solution)/shard_map/ppermute | solution.py:19
  331.9 10.6 %collective-permute-start.51 = (f16[128,1024]{1,0:T(8,128)(2,1)S(1)}, f16[128,1024]{1,0:T(8,128)(2,1)S(1)}, u32[]{:S(2)}, u32[]{:S(2)}) collective-permute-start(f16[128,1024]{1,0:T(8,128)(2,1)S(1)} %slice.271), channel_id=1, source_target_pairs={{0,16},{4,20},{8,24},{12,28},{16,0},{20,4},{24,8},{28,12},{1,17},{... | collective-permute-start | bytes 786440 | tf_op jit(solution)/shard_map/ppermute | solution.py:19
  339.4 6.4 %collective-permute-start.52 = (f16[128,1024]{1,0:T(8,128)(2,1)S(1)}, f16[128,1024]{1,0:T(8,128)(2,1)S(1)}, u32[]{:S(2)}, u32[]{:S(2)}) collective-permute-start(f16[128,1024]{1,0:T(8,128)(2,1)S(1)} %slice.272), channel_id=1, source_target_pairs={{0,8},{4,12},{8,0},{12,4},{16,24},{20,28},{24,16},{28,20},{1,9},{5... | collective-permute-start | bytes 786440 | tf_op jit(solution)/shard_map/ppermute | solution.py:19
  346.6 19.2 %collective-permute-start.55 = (f16[1024,1024]{1,0:T(8,128)(2,1)}, f16[1024,1024]{1,0:T(8,128)(2,1)S(1)}, u32[]{:S(2)}, u32[]{:S(2)}) collective-permute-start(f16[1024,1024]{1,0:T(8,128)(2,1)} %constant_dynamic-update-slice_fusion.15), channel_id=1, source_target_pairs={{0,4},{4,0},{8,12},{12,8},{16,20},{20,16},{24,28},{28,24},{1,5},{5... | collective-permute-start | bytes 6291464 | tf_op jit(solution)/shard_map/ppermute | solution.py:19
  361.0 17.2 %collective-permute-start.53 = (f16[256,1024]{1,0:T(8,128)(2,1)S(1)}, f16[256,1024]{1,0:T(8,128)(2,1)S(1)}, u32[]{:S(2)}, u32[]{:S(2)}) collective-permute-start(f16[256,1024]{1,0:T(8,128)(2,1)S(1)} %get-tuple-element.116), channel_id=1, source_target_pairs={{0,8},{4,12},{8,0},{12,4},{16,24},{20,28},{24,16},{28,20},{1,9},{5... | collective-permute-start | bytes 1572872 | tf_op jit(solution)/shard_map/ppermute | solution.py:19
  362.3 15.9 %collective-permute-start.54 = (f16[256,1024]{1,0:T(8,128)(2,1)S(1)}, f16[256,1024]{1,0:T(8,128)(2,1)S(1)}, u32[]{:S(2)}, u32[]{:S(2)}) collective-permute-start(f16[256,1024]{1,0:T(8,128)(2,1)S(1)} %get-tuple-element.116), channel_id=1, source_target_pairs={{0,16},{4,20},{8,24},{12,28},{16,0},{20,4},{24,8},{28,12},{1,17},{... | collective-permute-start | bytes 1572872 | tf_op jit(solution)/shard_map/ppermute | solution.py:19
  378.3 8.2 %collective-permute-start.56 = (f16[128,1024]{1,0:T(8,128)(2,1)S(1)}, f16[128,1024]{1,0:T(8,128)(2,1)S(1)}, u32[]{:S(2)}, u32[]{:S(2)}) collective-permute-start(f16[128,1024]{1,0:T(8,128)(2,1)S(1)} %slice.244), channel_id=1, source_target_pairs={{0,16},{4,20},{8,24},{12,28},{16,0},{20,4},{24,8},{28,12},{1,17},{... | collective-permute-start | bytes 786440 | tf_op jit(solution)/shard_map/ppermute | solution.py:19
  379.6 7.9 %collective-permute-start.57 = (f16[128,1024]{1,0:T(8,128)(2,1)S(1)}, f16[128,1024]{1,0:T(8,128)(2,1)S(1)}, u32[]{:S(2)}, u32[]{:S(2)}) collective-permute-start(f16[128,1024]{1,0:T(8,128)(2,1)S(1)} %slice.245), channel_id=1, source_target_pairs={{0,8},{4,12},{8,0},{12,4},{16,24},{20,28},{24,16},{28,20},{1,9},{5... | collective-permute-start | bytes 786440 | tf_op jit(solution)/shard_map/ppermute | solution.py:19
  387.6 4.2 %collective-permute-start.58 = (f16[1024,1024]{1,0:T(8,128)(2,1)S(1)}, f16[1024,1024]{1,0:T(8,128)(2,1)S(1)}, u32[]{:S(2)}, u32[]{:S(2)}) collective-permute-start(f16[1024,1024]{1,0:T(8,128)(2,1)S(1)} %constant_dynamic-update-slice_fusion.20), channel_id=1, source_target_pairs={{0,4},{4,0},{8,12},{12,8},{16,20},{20,16},{24,28},{28,24},{1,5},{5... | collective-permute-start | bytes 6291464 | tf_op jit(solution)/shard_map/ppermute | solution.py:19
  (28 other events, 117.6 us)
Sparse Core Ops, SparseCore 0:
  23.0 81.1 all-gather.4
  105.8 79.4 all-gather.6

commit v5 on v4

--- a/solution.py
+++ b/solution.py
@@ -474,8 +474,6 @@
         if c:
             rows, cross_near = tie(rows, cross_near)
             cross_pairs.append((cross_near, swap(cross_near, 1)))
-        else:
-            rows, result = tie(rows, result)
         stacked = jnp.concatenate(split(rows.astype(F32)), axis=0)
         cross = cross_rows(cross_scale.reshape(1, 1), stacked, rot_terms).astype(F16)
         came = first_step(cross)

time: 416 us -> 417 us (level)
  other arithmetic: 43 us -> 54.6 us
  waiting for transfers between devices: 114 us -> 103 us
  starting transfers between devices: 64.7 us -> 70 us
  local copies, waits for them, and re-layouts: 79.1 us -> 74.8 us
    ppermute x51, waiting for transfers between devices: 104 us -> 94.4 us  [swap(): return lax.ppermute(x, 'dp', [(i, i ^ mask) for i in range(n)])]
    ppermute x2, starting transfers between devices: 6.57 us -> 14.1 us  [gather_loop(): across = lax.ppermute(across, 'loop', [(3, 1), (0, 2), (1, 0), (2, 3)])]
    unnamed x95 -> x99, local copies, waits for them, and re-layouts: 49 us -> 44.1 us
    convert_element_type x8, other arithmetic: 16.8 us -> 21.5 us  [split(): return (high.astype(BF16), (x - high).astype(BF16))]
  transfers between devices with their start and end apart: 61 -> 61, of which waited for: 33 -> 26; matrix products, arithmetic and copies ran while one was open for 31% -> 34% of each run, Pallas kernels for 9% -> 9%
where the time goes in v5:
time: 417 us; the launch traced here: 411 us
  waiting for transfers between devices  103 us (25%)
  local copies, waits for them, and re-layouts  74.8 us (18%)
  starting transfers between devices  70 us (17%)
  other arithmetic  54.6 us (13%)
  Pallas kernels  48.2 us (12%)
  matrix products  42.4 us (10%)
  between operations  18.8 us (5%)
    ppermute x51, waiting for transfers between devices, swap(): return lax.ppermute(x, 'dp', [(i, i ^ mask) for i in range(n)])  94.4 us
    ppermute x51, starting transfers between devices, swap(): return lax.ppermute(x, 'dp', [(i, i ^ mask) for i in range(n)])  45.7 us
    unnamed x99, local copies, waits for them, and re-layouts  44.1 us
    dot_general x12, matrix products, dot(): lax.dot_general(a, b, (((ca,), (cb,)), ((), ())), preferred_element_type=...  41 us
    pallas_call x4, Pallas kernels, plain_call(): pl.pallas_call(body, out_shape=out, grid=grid, in_specs=in_specs, out_spe...  39 us
    convert_element_type x8, other arithmetic, split(): return (high.astype(BF16), (x - high).astype(BF16))  21.5 us
    ppermute x2, starting transfers between devices, gather_loop(): across = lax.ppermute(across, 'loop', [(3, 1), (0, 2), (1, 0), (2, 3)])  14.1 us
    pallas_call x4, Pallas kernels, ordered_call(): pl.pallas_call(body, out_shape=outs, grid_spec=pltpu.PrefetchScalarGridSp...  9.2 us
  transfers between devices with their start and end apart: 61, of which 26 were waited for; matrix products, arithmetic and copies ran while one was open for 34% of the time, Pallas kernels for 9%

profile of v5, /device:TPU:0, one launch (start us, length us, event | category | flops | bytes accessed | tf_op | source)
XLA Modules:
  0.0 411.5 jit_solution(10497262669526684653)
XLA Ops:
  6.5 2.5 abs_reduce_fusion.2
  9.8 3.0 collective-permute-start
  12.8 4.0 fusion.34
  18.4 2.0 collective-permute-done.1
  20.5 2.4 fusion.49
  23.3 2.0 collective-permute-start.3
  25.7 2.3 fusion.50
  30.0 2.2 shard_map.64
  32.2 3.2 copy.53
  35.4 11.6 %collective-permute-done.2 = f16[512,1024]{1,0:T(8,128)(2,1)} collective-permute-done((f16[512,1024]{1,0:T(8,128)(2,1)}, f16[512,1024]{1,0:T(8,128)(2,1)}, u32[]{:S(2)}, u32[]{:S(2)}) %collective-permute-start.2) | collective-permute-done | bytes 1048608 | tf_op jit(solution)/shard_map/ppermute | solution.py:19
  52.7 3.8 shard_map.65
  56.6 3.0 copy-done
  59.5 3.0 copy-done.16
  62.5 2.5 constant_dynamic-update-slice_fusion.4
  65.0 2.5 constant_dynamic-update-slice_fusion.3
  67.4 2.5 constant_dynamic-update-slice_fusion.2
  72.0 3.0 copy.51
  76.2 4.7 %fusion = (bf16[2048,1024]{1,0:T(8,128)(2,1)}, bf16[2048,1024]{1,0:T(8,128)(2,1)S(1)}) fusion(f16[2048,1024]{1,0:T(8,128)(2,1)} %constant_dynamic-update-slice_fusion, f32[2048]{0:T(1024)S(1)} %bitcast.83), kind=kLoop, calls=%fused_computation.4 | loop fusion | flops 12582912 | bytes 12591104 | tf_op jit(solution)/shard_map/convert_element_type | solution.py:150
  81.1 4.0 fusion.20
  85.1 10.0 %collective-permute-done.8 = bf16[2,1,2,192,512]{4,3,2,1,0:T(8,128)(2,1)S(1)} collective-permute-done((bf16[2,1,2,192,512]{4,3,2,1,0:T(8,128)(2,1)S(1)}, bf16[2,1,2,192,512]{4,3,2,1,0:T(8,128)(2,1)S(1)}, u32[]{:S(2)}, u32[]{:S(2)}) %collective-permute-start.8) | collective-permute-done | bytes 786464 | tf_op jit(solution)/shard_map/ppermute | solution.py:19
  95.6 4.9 %fusion.1 = (bf16[2048,1024]{1,0:T(8,128)(2,1)}, bf16[2048,1024]{1,0:T(8,128)(2,1)S(1)}) fusion(f16[2048,1024]{1,0:T(8,128)(2,1)} %collective-permute-done.7, f32[2048]{0:T(1024)S(1)} %bitcast.82), kind=kLoop, calls=%fused_computation.5 | loop fusion | flops 12582912 | bytes 12591104 | tf_op jit(solution)/shard_map/convert_element_type | solution.py:150
  100.6 4.0 fusion.18
  113.6 11.6 %collective-permute-done.20 = bf16[2,2,1,192,512]{4,3,2,1,0:T(8,128)(2,1)S(1)} collective-permute-done((bf16[2,2,1,192,512]{4,3,2,1,0:T(8,128)(2,1)S(1)}, bf16[2,2,1,192,512]{4,3,2,1,0:T(8,128)(2,1)S(1)}, u32[]{:S(2)}, u32[]{:S(2)}) %collective-permute-start.20) | collective-permute-done | bytes 786464 | tf_op jit(solution)/shard_map/ppermute | solution.py:19
  130.1 10.5 %collective-permute-done.10 = bf16[384,1024]{1,0:T(8,128)(2,1)} collective-permute-done((bf16[384,1024]{1,0:T(8,128)(2,1)S(1)}, bf16[384,1024]{1,0:T(8,128)(2,1)}, u32[]{:S(2)}, u32[]{:S(2)}) %collective-permute-start.10) | collective-permute-done | bytes 786464 | tf_op jit(solution)/shard_map/ppermute | solution.py:19
  144.8 2.6 collective-permute-start.19
  150.7 3.1 concatenate.126
  157.8 2.1 constant_dynamic-update-slice_fusion.13
  159.9 2.1 constant_dynamic-update-slice_fusion.12
  161.9 2.4 constant_dynamic-update-slice_fusion.9
  164.3 3.3 collective-permute-done.12
  172.8 2.3 constant_dynamic-update-slice_fusion.8
  175.1 2.3 constant_dynamic-update-slice_fusion.7
  181.3 3.5 collective-permute-done.23
  196.8 4.4 %fusion.22 = f32[512,1024]{1,0:T(8,128)S(1)} fusion(bf16[1536,512]{1,0:T(8,128)(2,1)} %bitcast.81, bf16[1536,1024]{1,0:T(8,128)(2,1)} %collective-permute-done.27, bf16[1536]{0:T(1024)(128)(2,1)S(1)} %neg.45, bf16[1536]{0:T(1024)(128)(2,1)S(1)} %min.58), kind=kOutput, calls=%fused_computation.51 | convolution fusion | flops 1613758464 | bytes 6821888 | tf_op jit(solution)/shard_map/dot_general | solution.py:145
  201.2 4.8 %add_convert_fusion = bf16[512,1024]{1,0:T(8,128)(2,1)} fusion(f32[512,1024]{1,0:T(8,128)S(1)} %fusion.22, bf16[1536,512]{1,0:T(8,128)(2,1)S(1)} %bitcast.80, bf16[1536,1024]{1,0:T(8,128)(2,1)} %constant_dynamic-update-slice_fusion.10, bf16[1536]{0:T(1024)(128)(2,1)S(1)} %neg.44, bf16[1536]{0:T(1024)(128)(2,1)S(1)} %min.55), kind=kOutput, calls=%fused_computation.77 | convolution fusion | flops 1614807040 | bytes 7870464 | tf_op jit(solution)/shard_map/dot_general | solution.py:145
  206.0 4.3 %fusion.12 = f32[384,1024]{1,0:T(8,128)S(1)} fusion(bf16[2048,1024]{1,0:T(8,128)(2,1)} %collective-permute-done.26, bf16[2048]{0:T(1024)(128)(2,1)S(1)} %neg.46, bf16[2048]{0:T(1024)(128)(2,1)S(1)} %bitcast.87, bf16[384,4096]{1,0:T(8,128)(2,1)S(1)} %shard_map.64), kind=kOutput, calls=%fused_computation.36 | convolution fusion | flops 1614807040 | bytes 7348224 | tf_op jit(solution)/shard_map/dot_general | solution.py:145
  210.3 4.3 %add_convert_fusion.2 = bf16[384,1024]{1,0:T(8,128)(2,1)S(1)} fusion(f32[384,1024]{1,0:T(8,128)S(1)} %fusion.12, bf16[2048,1024]{1,0:T(8,128)(2,1)} %constant_dynamic-update-slice_fusion.5, bf16[2048]{0:T(1024)(128)(2,1)S(1)} %neg.43, bf16[2048]{0:T(1024)(128)(2,1)S(1)} %bitcast.85, bf16[384,4096]{1,0:T(8,128)(2,1)S(1)} %shard_map.64), kind=kOutput, calls=%fused_computation.93 | convolution fusion | flops 1615593472 | bytes 8134656 | tf_op jit(solution)/shard_map/dot_general | solution.py:145
  215.4 2.7 fusion.4
  219.2 2.5 fusion.5
  222.3 2.8 fusion.107
  228.1 2.6 fusion.3
  230.7 3.3 collective-permute-done.30
  240.1 4.7 %collective-permute-done.36 = f16[32,4096]{1,0:T(8,128)(2,1)S(1)} collective-permute-done((f16[32,4096]{1,0:T(8,128)(2,1)S(1)}, f16[32,4096]{1,0:T(8,128)(2,1)S(1)}, u32[]{:S(2)}, u32[]{:S(2)}) %collective-permute-start.36) | collective-permute-done | bytes 262176 | tf_op jit(solution)/shard_map/ppermute | solution.py:19
  248.1 9.3 %collective-permute-done.32 = f16[64,4096]{1,0:T(8,128)(2,1)S(1)} collective-permute-done((f16[64,4096]{1,0:T(8,128)(2,1)S(1)}, f16[64,4096]{1,0:T(8,128)(2,1)S(1)}, u32[]{:S(2)}, u32[]{:S(2)}) %collective-permute-start.32) | collective-permute-done | bytes 524320 | tf_op jit(solution)/shard_map/ppermute | solution.py:19
  259.1 3.7 collective-permute-start.34
  262.9 3.7 collective-permute-done.37
  272.8 4.5 %collective-permute-done.50 = f16[2,1,2,64,512]{4,3,2,1,0:T(8,128)(2,1)} collective-permute-done((f16[2,1,2,64,512]{4,3,2,1,0:T(8,128)(2,1)}, f16[2,1,2,64,512]{4,3,2,1,0:T(8,128)(2,1)}, u32[]{:S(2)}, u32[]{:S(2)}) %collective-permute-start.50) | collective-permute-done | bytes 262176 | tf_op jit(solution)/shard_map/ppermute | solution.py:19
  283.6 3.6 collective-permute-start.43
  292.7 7.3 %collective-permute-done.43 = f16[64,4096]{1,0:T(8,128)(2,1)} collective-permute-done((f16[64,4096]{1,0:T(8,128)(2,1)}, f16[64,4096]{1,0:T(8,128)(2,1)}, u32[]{:S(2)}, u32[]{:S(2)}) %collective-permute-start.43) | collective-permute-done | bytes 524320 | tf_op jit(solution)/shard_map/ppermute | solution.py:131
  300.0 2.4 reduce-precision_convert_fusion.7
  305.8 9.6 %shard_map.68 = f32[256,1024]{1,0:T(8,128)S(1)} custom-call(f32[1,1]{1,0:T(1,128)} %bitcast.11.scale_ref, bf16[512,4096]{1,0:T(8,128)(2,1)S(1)} %pad_maximum_fusion.rows_ref, bf16[2048,1024]{1,0:T(8,128)(2,1)S(1)} %copy-done.8, bf16[2048,1024]{1,0:T(8,128)(2,1)S(1)} %copy-done.5, bf16[2048,1024]{1,0:T(8,128)(2,1)S(1)} %copy-done.13, ...), custom_call_target="tpu_custom_call" | custom-call | flops 6442450944 | bytes 22020100 | tf_op jit(solution)/shard_map/pallas_call | solution.py:215
  320.4 10.5 %collective-permute-start.42 = (f16[64,4096]{1,0:T(8,128)(2,1)}, f16[64,4096]{1,0:T(8,128)(2,1)}, u32[]{:S(2)}, u32[]{:S(2)}) collective-permute-start(f16[64,4096]{1,0:T(8,128)(2,1)} %select_select_fusion.1), channel_id=1, source_target_pairs={{3,1},{0,2},{1,0},{2,3},{7,5},{4,6},{5,4},{6,7},{11,9},{8,10},{9,8... | collective-permute-start | bytes 1572872 | tf_op jit(solution)/shard_map/ppermute | solution.py:131
  334.4 2.2 copy.50
  339.3 2.0 pad_maximum_fusion.3
  342.2 2.1 constant_dynamic-update-slice_fusion.17
  345.8 2.2 reduce-precision_convert_fusion.6
  348.1 2.7 pad_maximum_fusion.1.rows_ref
  352.3 9.6 %shard_map.69 = f32[256,1024]{1,0:T(8,128)S(1)} custom-call(f32[1,1]{1,0:T(1,128)} %bitcast.11.scale_ref, bf16[512,4096]{1,0:T(8,128)(2,1)S(1)} %pad_maximum_fusion.1.rows_ref, bf16[2048,1024]{1,0:T(8,128)(2,1)S(1)} %copy-done.9, bf16[2048,1024]{1,0:T(8,128)(2,1)S(1)} %copy-done.6, bf16[2048,1024]{1,0:T(8,128)(2,1)S(1)} %copy-done.14, ...), custom_call_target="tpu_custom_call" | custom-call | flops 6442450944 | bytes 22020100 | tf_op jit(solution)/shard_map/pallas_call | solution.py:215
  364.6 2.7 fusion.8
  367.4 2.7 fusion.9
  370.2 9.5 %shard_map.70.base_ref = f32[512,1024]{1,0:T(8,128)S(1)} custom-call(f32[1,1]{1,0:T(1,128)} %bitcast.10.factor_ref, s32[4]{0:T(128)S(1)} %and_select_fusion.1.level_ref, f32[512,1024]{1,0:T(8,128)S(1)} %bitcast.55, bf16[4,512,1024]{2,1,0:T(8,128)(2,1)S(1)} %bitcast.58, bf16[4,512,1024]{2,1,0:T(8,128)(2,1)S(1)} %bitcast.60, ...), custom_call_target="tpu_custom_call" | custom-call | flops 6442450944 | bytes 20971540 | tf_op jit(solution)/shard_map/pallas_call | solution.py:215
  381.7 6.4 %collective-permute-done.56 = f16[128,1024]{1,0:T(8,128)(2,1)S(1)} collective-permute-done((f16[128,1024]{1,0:T(8,128)(2,1)S(1)}, f16[128,1024]{1,0:T(8,128)(2,1)S(1)}, u32[]{:S(2)}, u32[]{:S(2)}) %collective-permute-start.56) | collective-permute-done | bytes 262176 | tf_op jit(solution)/shard_map/ppermute | solution.py:19
  389.7 3.2 collective-permute-done.58
  393.9 10.3 %shard_map.71 = f32[512,1024]{1,0:T(8,128)} custom-call(f32[1,1]{1,0:T(1,128)} %bitcast.10.factor_ref, s32[4]{0:T(128)S(1)} %and_select_fusion.1.level_ref, f32[512,1024]{1,0:T(8,128)S(1)} %shard_map.70.base_ref, bf16[4,512,1024]{2,1,0:T(8,128)(2,1)S(1)} %bitcast.59, bf16[4,512,1024]{2,1,0:T(8,128)(2,1)S(1)} %bitcast.61, ...), custom_call_target="tpu_custom_call" | custom-call | flops 6442450944 | bytes 20971540 | tf_op jit(solution)/shard_map/pallas_call | solution.py:215
  (296 shorter events, 117.5 us)
Async XLA Ops:
  6.5 147.3 %all-gather.5.cloned.1.call-start = ((), (), s32[]{:S(2)}) async-start(), calls=%async_computation | async-start | bytes 5242880 | tf_op jit(solution)/shard_map/all_gather | solution.py:366
  9.8 7.0 %collective-permute-start = (f32[128]{0:T(128)S(1)}, f32[128]{0:T(128)S(1)}, u32[]{:S(2)}, u32[]{:S(2)}) collective-permute-start(f32[128]{0:T(128)S(1)} %broadcast_in_dim.24), channel_id=1, source_target_pairs={{0,8},{4,12},{8,0},{12,4},{16,24},{20,28},{24,16},{28,20},{1,9},{5... | collective-permute-start | bytes 1544 | tf_op jit(solution)/shard_map/ppermute | solution.py:19
  16.8 3.6 collective-permute-start.1
  22.9 183.1 %all-gather.7.cloned.1.call-start = ((), (), s32[]{:S(2)}) async-start(), calls=%async_computation.1 | async-start | bytes 5242880 | tf_op jit(solution)/shard_map/all_gather | solution.py:366
  23.2 23.9 %collective-permute-start.2 = (f16[512,1024]{1,0:T(8,128)(2,1)}, f16[512,1024]{1,0:T(8,128)(2,1)}, u32[]{:S(2)}, u32[]{:S(2)}) collective-permute-start(f16[512,1024]{1,0:T(8,128)(2,1)} %fusion.34), channel_id=1, source_target_pairs={{0,8},{4,12},{8,0},{12,4},{16,24},{20,28},{24,16},{28,20},{1,9},{5... | collective-permute-start | bytes 3145736 | tf_op jit(solution)/shard_map/ppermute | solution.py:19
  23.3 23.9 %collective-permute-start.3 = (f16[512,1024]{1,0:T(8,128)(2,1)}, f16[512,1024]{1,0:T(8,128)(2,1)}, u32[]{:S(2)}, u32[]{:S(2)}) collective-permute-start(f16[512,1024]{1,0:T(8,128)(2,1)} %fusion.34), channel_id=1, source_target_pairs={{0,16},{4,20},{8,24},{12,28},{16,0},{20,4},{24,8},{28,12},{1,17},{... | collective-permute-start | bytes 3145736 | tf_op jit(solution)/shard_map/ppermute | solution.py:19
  25.6 9.8 %collective-permute-start.4 = (f32[512]{0:T(512)S(1)}, f32[512]{0:T(512)S(1)}, u32[]{:S(2)}, u32[]{:S(2)}) collective-permute-start(f32[512]{0:T(512)S(1)} %pad_maximum_fusion.21), channel_id=1, source_target_pairs={{0,4},{4,0},{8,12},{12,8},{16,20},{20,16},{24,28},{28,24},{1,5},{5... | collective-permute-start | bytes 6152 | tf_op jit(solution)/shard_map/ppermute | solution.py:19
  32.2 20.5 %copy-start.1 = (bf16[4096,512]{1,0:T(8,128)(2,1)S(1)}, bf16[4096,512]{1,0:T(8,128)(2,1)}, u32[]{:S(2)}) copy-start(bf16[4096,512]{1,0:T(8,128)(2,1)} %weight_ref) | copy-start | bytes 12582916
  32.2 20.5 %copy-start.3 = (bf16[384,4096]{1,0:T(8,128)(2,1)S(1)}, bf16[384,4096]{1,0:T(8,128)(2,1)}, u32[]{:S(2)}) copy-start(bf16[384,4096]{1,0:T(8,128)(2,1)} %tok_ref) | copy-start | bytes 9437188
  48.3 21.6 %collective-permute-start.5 = (f16[256,1024]{1,0:T(8,128)(2,1)S(1)}, f16[256,1024]{1,0:T(8,128)(2,1)S(1)}, u32[]{:S(2)}, u32[]{:S(2)}) collective-permute-start(f16[256,1024]{1,0:T(8,128)(2,1)S(1)} %slice.199), channel_id=1, source_target_pairs={{0,16},{4,20},{8,24},{12,28},{16,0},{20,4},{24,8},{28,12},{1,17},{... | collective-permute-start | bytes 1572872 | tf_op jit(solution)/shard_map/ppermute | solution.py:19
  51.1 18.8 %collective-permute-start.6 = (f16[256,1024]{1,0:T(8,128)(2,1)S(1)}, f16[256,1024]{1,0:T(8,128)(2,1)S(1)}, u32[]{:S(2)}, u32[]{:S(2)}) collective-permute-start(f16[256,1024]{1,0:T(8,128)(2,1)S(1)} %slice.200), channel_id=1, source_target_pairs={{0,8},{4,12},{8,0},{12,4},{16,24},{20,28},{24,16},{28,20},{1,9},{5... | collective-permute-start | bytes 1572872 | tf_op jit(solution)/shard_map/ppermute | solution.py:19
  71.7 23.9 %collective-permute-start.7 = (f16[2048,1024]{1,0:T(8,128)(2,1)}, f16[2048,1024]{1,0:T(8,128)(2,1)}, u32[]{:S(2)}, u32[]{:S(2)}) collective-permute-start(f16[2048,1024]{1,0:T(8,128)(2,1)} %constant_dynamic-update-slice_fusion), channel_id=1, source_target_pairs={{0,4},{4,0},{8,12},{12,8},{16,20},{20,16},{24,28},{28,24},{1,5},{5... | collective-permute-start | bytes 12582920 | tf_op jit(solution)/shard_map/ppermute | solution.py:19
  75.1 20.0 %collective-permute-start.8 = (bf16[2,1,2,192,512]{4,3,2,1,0:T(8,128)(2,1)S(1)}, bf16[2,1,2,192,512]{4,3,2,1,0:T(8,128)(2,1)S(1)}, u32[]{:S(2)}, u32[]{:S(2)}) collective-permute-start(bf16[2,1,2,192,512]{4,3,2,1,0:T(8,128)(2,1)S(1)} %get-tuple-element.132), channel_id=1, source_target_pairs={{0,16},{4,20},{8,24},{12,28},{16,0},{20,4},{24,8},{28,12},{1,17},{... | collective-permute-start | bytes 2359304 | tf_op jit(solution)/shard_map/ppermute | solution.py:19
  75.7 19.7 %collective-permute-start.9 = (bf16[2,2,1,192,512]{4,3,2,1,0:T(8,128)(2,1)S(1)}, bf16[2,2,1,192,512]{4,3,2,1,0:T(8,128)(2,1)S(1)}, u32[]{:S(2)}, u32[]{:S(2)}) collective-permute-start(bf16[2,2,1,192,512]{4,3,2,1,0:T(8,128)(2,1)S(1)} %get-tuple-element.130), channel_id=1, source_target_pairs={{0,8},{4,12},{8,0},{12,4},{16,24},{20,28},{24,16},{28,20},{1,9},{5... | collective-permute-start | bytes 2359304 | tf_op jit(solution)/shard_map/ppermute | solution.py:19
  104.6 20.5 %collective-permute-start.20 = (bf16[2,2,1,192,512]{4,3,2,1,0:T(8,128)(2,1)S(1)}, bf16[2,2,1,192,512]{4,3,2,1,0:T(8,128)(2,1)S(1)}, u32[]{:S(2)}, u32[]{:S(2)}) collective-permute-start(bf16[2,2,1,192,512]{4,3,2,1,0:T(8,128)(2,1)S(1)} %get-tuple-element.156), channel_id=1, source_target_pairs={{0,8},{4,12},{8,0},{12,4},{16,24},{20,28},{24,16},{28,20},{1,9},{5... | collective-permute-start | bytes 2359304 | tf_op jit(solution)/shard_map/ppermute | solution.py:19
  105.3 20.5 %collective-permute-start.21 = (bf16[2,1,2,192,512]{4,3,2,1,0:T(8,128)(2,1)S(1)}, bf16[2,1,2,192,512]{4,3,2,1,0:T(8,128)(2,1)S(1)}, u32[]{:S(2)}, u32[]{:S(2)}) collective-permute-start(bf16[2,1,2,192,512]{4,3,2,1,0:T(8,128)(2,1)S(1)} %get-tuple-element.158), channel_id=1, source_target_pairs={{0,16},{4,20},{8,24},{12,28},{16,0},{20,4},{24,8},{28,12},{1,17},{... | collective-permute-start | bytes 2359304 | tf_op jit(solution)/shard_map/ppermute | solution.py:19
  108.6 32.1 %collective-permute-start.10 = (bf16[384,1024]{1,0:T(8,128)(2,1)S(1)}, bf16[384,1024]{1,0:T(8,128)(2,1)}, u32[]{:S(2)}, u32[]{:S(2)}) collective-permute-start(bf16[384,1024]{1,0:T(8,128)(2,1)S(1)} %get-tuple-element.154), channel_id=1, source_target_pairs={{0,8},{4,12},{8,0},{12,4},{16,24},{20,28},{24,16},{28,20},{1,9},{5... | collective-permute-start | bytes 2359304 | tf_op jit(solution)/shard_map/ppermute | solution.py:19
  110.0 31.2 %collective-permute-start.11 = (bf16[384,1024]{1,0:T(8,128)(2,1)S(1)}, bf16[384,1024]{1,0:T(8,128)(2,1)}, u32[]{:S(2)}, u32[]{:S(2)}) collective-permute-start(bf16[384,1024]{1,0:T(8,128)(2,1)S(1)} %get-tuple-element.154), channel_id=1, source_target_pairs={{0,16},{4,20},{8,24},{12,28},{16,0},{20,4},{24,8},{28,12},{1,17},{... | collective-permute-start | bytes 2359304 | tf_op jit(solution)/shard_map/ppermute | solution.py:19
  111.6 33.2 %collective-permute-start.18 = (f32[896]{0:T(1024)S(1)}, f32[896]{0:T(1024)S(1)}, u32[]{:S(2)}, u32[]{:S(2)}) collective-permute-start(f32[896]{0:T(1024)S(1)} %get-tuple-element.80), channel_id=1, source_target_pairs={{0,1},{1,0},{2,3},{3,2},{4,5},{5,4},{6,7},{7,6},{8,9},{9,8},{10,11... | collective-permute-start | bytes 10760 | tf_op jit(solution)/shard_map/ppermute | solution.py:139
  128.0 49.4 %collective-permute-start.22 = (bf16[1,2,2,384,512]{4,3,2,1,0:T(8,128)(2,1)}, bf16[1,2,2,384,512]{4,3,2,1,0:T(8,128)(2,1)}, u32[]{:S(2)}, u32[]{:S(2)}) collective-permute-start(bf16[1,2,2,384,512]{4,3,2,1,0:T(8,128)(2,1)} %get-tuple-element.128), channel_id=1, source_target_pairs={{0,4},{4,0},{8,12},{12,8},{16,20},{20,16},{24,28},{28,24},{1,5},{5... | collective-permute-start | bytes 4718600 | tf_op jit(solution)/shard_map/ppermute | solution.py:19
  141.2 26.4 %collective-permute-start.12 = (bf16[512,1024]{1,0:T(8,128)(2,1)}, bf16[512,1024]{1,0:T(8,128)(2,1)}, u32[]{:S(2)}, u32[]{:S(2)}) collective-permute-start(bf16[512,1024]{1,0:T(8,128)(2,1)} %slice.247), channel_id=1, source_target_pairs={{0,8},{4,12},{8,0},{12,4},{16,24},{20,28},{24,16},{28,20},{1,9},{5... | collective-permute-start | bytes 3145736 | tf_op jit(solution)/shard_map/ppermute | solution.py:19
  142.7 27.5 %collective-permute-start.13 = (bf16[512,1024]{1,0:T(8,128)(2,1)}, bf16[512,1024]{1,0:T(8,128)(2,1)}, u32[]{:S(2)}, u32[]{:S(2)}) collective-permute-start(bf16[512,1024]{1,0:T(8,128)(2,1)} %slice.247), channel_id=1, source_target_pairs={{0,16},{4,20},{8,24},{12,28},{16,0},{20,4},{24,8},{28,12},{1,17},{... | collective-permute-start | bytes 3145736 | tf_op jit(solution)/shard_map/ppermute | solution.py:19
  144.8 4.7 %collective-permute-start.19 = (f32[896]{0:T(1024)S(1)}, f32[896]{0:T(1024)S(1)}, u32[]{:S(2)}, u32[]{:S(2)}) collective-permute-start(f32[896]{0:T(1024)S(1)} %add.166), channel_id=1, source_target_pairs={{0,2},{1,3},{2,0},{3,1},{4,6},{5,7},{6,4},{7,5},{8,10},{9,11},{10,... | collective-permute-start | bytes 10760 | tf_op jit(solution)/shard_map/ppermute | solution.py:139
  154.8 24.2 %collective-permute-start.16 = (bf16[192,1024]{1,0:T(8,128)(2,1)S(1)}, bf16[192,1024]{1,0:T(8,128)(2,1)S(1)}, u32[]{:S(2)}, u32[]{:S(2)}) collective-permute-start(bf16[192,1024]{1,0:T(8,128)(2,1)S(1)} %slice.209), channel_id=1, source_target_pairs={{0,16},{4,20},{8,24},{12,28},{16,0},{20,4},{24,8},{28,12},{1,17},{... | collective-permute-start | bytes 1179656 | tf_op jit(solution)/shard_map/ppermute | solution.py:19
  156.5 22.5 %collective-permute-start.17 = (bf16[192,1024]{1,0:T(8,128)(2,1)S(1)}, bf16[192,1024]{1,0:T(8,128)(2,1)S(1)}, u32[]{:S(2)}, u32[]{:S(2)}) collective-permute-start(bf16[192,1024]{1,0:T(8,128)(2,1)S(1)} %slice.210), channel_id=1, source_target_pairs={{0,8},{4,12},{8,0},{12,4},{16,24},{20,28},{24,16},{28,20},{1,9},{5... | collective-permute-start | bytes 1179656 | tf_op jit(solution)/shard_map/ppermute | solution.py:19
  168.7 17.3 %collective-permute-start.14 = (bf16[256,1024]{1,0:T(8,128)(2,1)S(1)}, bf16[256,1024]{1,0:T(8,128)(2,1)S(1)}, u32[]{:S(2)}, u32[]{:S(2)}) collective-permute-start(bf16[256,1024]{1,0:T(8,128)(2,1)S(1)} %slice.248), channel_id=1, source_target_pairs={{0,16},{4,20},{8,24},{12,28},{16,0},{20,4},{24,8},{28,12},{1,17},{... | collective-permute-start | bytes 1572872 | tf_op jit(solution)/shard_map/ppermute | solution.py:19
  171.3 17.2 %collective-permute-start.15 = (bf16[256,1024]{1,0:T(8,128)(2,1)S(1)}, bf16[256,1024]{1,0:T(8,128)(2,1)S(1)}, u32[]{:S(2)}, u32[]{:S(2)}) collective-permute-start(bf16[256,1024]{1,0:T(8,128)(2,1)S(1)} %slice.249), channel_id=1, source_target_pairs={{0,8},{4,12},{8,0},{12,4},{16,24},{20,28},{24,16},{28,20},{1,9},{5... | collective-permute-start | bytes 1572872 | tf_op jit(solution)/shard_map/ppermute | solution.py:19
  179.1 5.7 %collective-permute-start.23 = (f32[1024]{0:T(1024)S(1)}, f32[1024]{0:T(1024)S(1)}, u32[]{:S(2)}, u32[]{:S(2)}) collective-permute-start(f32[1024]{0:T(1024)S(1)} %concatenate.126), channel_id=1, source_target_pairs={{0,8},{4,12},{8,0},{12,4},{16,24},{20,28},{24,16},{28,20},{1,9},{5... | collective-permute-start | bytes 12296 | tf_op jit(solution)/shard_map/ppermute | solution.py:19
  181.3 15.5 %collective-permute-start.27 = (bf16[1536,1024]{1,0:T(8,128)(2,1)}, bf16[1536,1024]{1,0:T(8,128)(2,1)}, u32[]{:S(2)}, u32[]{:S(2)}) collective-permute-start(bf16[1536,1024]{1,0:T(8,128)(2,1)} %constant_dynamic-update-slice_fusion.10), channel_id=1, source_target_pairs={{0,4},{4,0},{8,12},{12,8},{16,20},{20,16},{24,28},{28,24},{1,5},{5... | collective-permute-start | bytes 9437192 | tf_op jit(solution)/shard_map/ppermute | solution.py:19
  184.8 3.7 collective-permute-start.24
  188.4 1.2 collective-permute-start.25
  189.6 16.4 %collective-permute-start.26 = (bf16[2048,1024]{1,0:T(8,128)(2,1)}, bf16[2048,1024]{1,0:T(8,128)(2,1)}, u32[]{:S(2)}, u32[]{:S(2)}) collective-permute-start(bf16[2048,1024]{1,0:T(8,128)(2,1)} %constant_dynamic-update-slice_fusion.5), channel_id=1, source_target_pairs={{0,4},{4,0},{8,12},{12,8},{16,20},{20,16},{24,28},{28,24},{1,5},{5... | collective-permute-start | bytes 12582920 | tf_op jit(solution)/shard_map/ppermute | solution.py:19
  218.1 4.2 %collective-permute-start.28 = (f16[256,4096]{1,0:T(8,128)(2,1)S(1)}, f16[256,4096]{1,0:T(8,128)(2,1)S(1)}, u32[]{:S(2)}, u32[]{:S(2)}) collective-permute-start(f16[256,4096]{1,0:T(8,128)(2,1)S(1)} %fusion.4), channel_id=1, source_target_pairs={{0,4},{4,0},{8,12},{12,8},{16,20},{20,16},{24,28},{28,24},{1,5},{5... | collective-permute-start | bytes 6291464 | tf_op jit(solution)/shard_map/ppermute | solution.py:19
  221.7 6.4 %collective-permute-start.29 = (f16[256,4096]{1,0:T(8,128)(2,1)S(1)}, f16[256,4096]{1,0:T(8,128)(2,1)S(1)}, u32[]{:S(2)}, u32[]{:S(2)}) collective-permute-start(f16[256,4096]{1,0:T(8,128)(2,1)S(1)} %fusion.5), channel_id=1, source_target_pairs={{0,4},{4,0},{8,12},{12,8},{16,20},{20,16},{24,28},{28,24},{1,5},{5... | collective-permute-start | bytes 6291464 | tf_op jit(solution)/shard_map/ppermute | solution.py:19
  225.4 8.6 %collective-permute-start.30 = (f16[32,4096]{1,0:T(8,128)(2,1)S(1)}, f16[32,4096]{1,0:T(8,128)(2,1)S(1)}, u32[]{:S(2)}, u32[]{:S(2)}) collective-permute-start(f16[32,4096]{1,0:T(8,128)(2,1)S(1)} %get-tuple-element.152), channel_id=1, source_target_pairs={{0,8},{4,12},{8,0},{12,4},{16,24},{20,28},{24,16},{28,20},{1,9},{5... | collective-permute-start | bytes 786440 | tf_op jit(solution)/shard_map/ppermute | solution.py:19
  226.7 8.3 %collective-permute-start.31 = (f16[32,4096]{1,0:T(8,128)(2,1)S(1)}, f16[32,4096]{1,0:T(8,128)(2,1)S(1)}, u32[]{:S(2)}, u32[]{:S(2)}) collective-permute-start(f16[32,4096]{1,0:T(8,128)(2,1)S(1)} %get-tuple-element.151), channel_id=1, source_target_pairs={{0,16},{4,20},{8,24},{12,28},{16,0},{20,4},{24,8},{28,12},{1,17},{... | collective-permute-start | bytes 786440 | tf_op jit(solution)/shard_map/ppermute | solution.py:19
  235.5 9.3 %collective-permute-start.36 = (f16[32,4096]{1,0:T(8,128)(2,1)S(1)}, f16[32,4096]{1,0:T(8,128)(2,1)S(1)}, u32[]{:S(2)}, u32[]{:S(2)}) collective-permute-start(f16[32,4096]{1,0:T(8,128)(2,1)S(1)} %get-tuple-element.148), channel_id=1, source_target_pairs={{0,16},{4,20},{8,24},{12,28},{16,0},{20,4},{24,8},{28,12},{1,17},{... | collective-permute-start | bytes 786440 | tf_op jit(solution)/shard_map/ppermute | solution.py:19
  236.9 9.2 %collective-permute-start.38 = (f16[32,4096]{1,0:T(8,128)(2,1)S(1)}, f16[32,4096]{1,0:T(8,128)(2,1)S(1)}, u32[]{:S(2)}, u32[]{:S(2)}) collective-permute-start(f16[32,4096]{1,0:T(8,128)(2,1)S(1)} %get-tuple-element.147), channel_id=1, source_target_pairs={{0,8},{4,12},{8,0},{12,4},{16,24},{20,28},{24,16},{28,20},{1,9},{5... | collective-permute-start | bytes 786440 | tf_op jit(solution)/shard_map/ppermute | solution.py:19
  237.8 19.6 %collective-permute-start.32 = (f16[64,4096]{1,0:T(8,128)(2,1)S(1)}, f16[64,4096]{1,0:T(8,128)(2,1)S(1)}, u32[]{:S(2)}, u32[]{:S(2)}) collective-permute-start(f16[64,4096]{1,0:T(8,128)(2,1)S(1)} %pad_maximum_fusion.11), channel_id=1, source_target_pairs={{0,8},{4,12},{8,0},{12,4},{16,24},{20,28},{24,16},{28,20},{1,9},{5... | collective-permute-start | bytes 1572872 | tf_op jit(solution)/shard_map/ppermute | solution.py:19
  239.4 18.0 %collective-permute-start.33 = (f16[64,4096]{1,0:T(8,128)(2,1)S(1)}, f16[64,4096]{1,0:T(8,128)(2,1)S(1)}, u32[]{:S(2)}, u32[]{:S(2)}) collective-permute-start(f16[64,4096]{1,0:T(8,128)(2,1)S(1)} %pad_maximum_fusion.12), channel_id=1, source_target_pairs={{0,16},{4,20},{8,24},{12,28},{16,0},{20,4},{24,8},{28,12},{1,17},{... | collective-permute-start | bytes 1572872 | tf_op jit(solution)/shard_map/ppermute | solution.py:19
  246.4 20.1 %collective-permute-start.37 = (f16[64,4096]{1,0:T(8,128)(2,1)S(1)}, f16[64,4096]{1,0:T(8,128)(2,1)S(1)}, u32[]{:S(2)}, u32[]{:S(2)}) collective-permute-start(f16[64,4096]{1,0:T(8,128)(2,1)S(1)} %pad_maximum_fusion.13), channel_id=1, source_target_pairs={{0,8},{4,12},{8,0},{12,4},{16,24},{20,28},{24,16},{28,20},{1,9},{5... | collective-permute-start | bytes 1572872 | tf_op jit(solution)/shard_map/ppermute | solution.py:19
  247.2 19.3 %collective-permute-start.39 = (f16[64,4096]{1,0:T(8,128)(2,1)S(1)}, f16[64,4096]{1,0:T(8,128)(2,1)S(1)}, u32[]{:S(2)}, u32[]{:S(2)}) collective-permute-start(f16[64,4096]{1,0:T(8,128)(2,1)S(1)} %pad_maximum_fusion.14), channel_id=1, source_target_pairs={{0,16},{4,20},{8,24},{12,28},{16,0},{20,4},{24,8},{28,12},{1,17},{... | collective-permute-start | bytes 1572872 | tf_op jit(solution)/shard_map/ppermute | solution.py:19
  259.1 23.4 %collective-permute-start.34 = (f16[64,4096]{1,0:T(8,128)(2,1)S(1)}, f16[64,4096]{1,0:T(8,128)(2,1)S(1)}, u32[]{:S(2)}, u32[]{:S(2)}) collective-permute-start(f16[64,4096]{1,0:T(8,128)(2,1)S(1)} %convert_element_type.207), channel_id=1, source_target_pairs={{0,3},{1,0},{2,1},{3,2},{4,7},{5,4},{6,5},{7,6},{8,11},{9,8},{10,9... | collective-permute-start | bytes 1572872 | tf_op jit(solution)/shard_map/ppermute | solution.py:122
  262.9 19.7 %collective-permute-start.35 = (f16[64,4096]{1,0:T(8,128)(2,1)S(1)}, f16[64,4096]{1,0:T(8,128)(2,1)}, u32[]{:S(2)}, u32[]{:S(2)}) collective-permute-start(f16[64,4096]{1,0:T(8,128)(2,1)S(1)} %convert_element_type.207), channel_id=1, source_target_pairs={{0,1},{1,2},{2,3},{3,0},{4,5},{5,6},{6,7},{7,4},{8,9},{9,10},{10,1... | collective-permute-start | bytes 1572872 | tf_op jit(solution)/shard_map/ppermute | solution.py:122
  270.5 6.7 %collective-permute-start.50 = (f16[2,1,2,64,512]{4,3,2,1,0:T(8,128)(2,1)}, f16[2,1,2,64,512]{4,3,2,1,0:T(8,128)(2,1)}, u32[]{:S(2)}, u32[]{:S(2)}) collective-permute-start(f16[2,1,2,64,512]{4,3,2,1,0:T(8,128)(2,1)} %get-tuple-element.162), channel_id=1, source_target_pairs={{0,16},{4,20},{8,24},{12,28},{16,0},{20,4},{24,8},{28,12},{1,17},{... | collective-permute-start | bytes 786440 | tf_op jit(solution)/shard_map/ppermute | solution.py:19
  272.0 7.8 %collective-permute-start.52 = (f16[2,2,1,64,512]{4,3,2,1,0:T(8,128)(2,1)}, f16[2,2,1,64,512]{4,3,2,1,0:T(8,128)(2,1)}, u32[]{:S(2)}, u32[]{:S(2)}) collective-permute-start(f16[2,2,1,64,512]{4,3,2,1,0:T(8,128)(2,1)} %get-tuple-element.164), channel_id=1, source_target_pairs={{0,8},{4,12},{8,0},{12,4},{16,24},{20,28},{24,16},{28,20},{1,9},{5... | collective-permute-start | bytes 786440 | tf_op jit(solution)/shard_map/ppermute | solution.py:19
  279.2 10.8 %collective-permute-start.51 = (f16[2,2,1,64,512]{4,3,2,1,0:T(8,128)(2,1)}, f16[2,2,1,64,512]{4,3,2,1,0:T(8,128)(2,1)}, u32[]{:S(2)}, u32[]{:S(2)}) collective-permute-start(f16[2,2,1,64,512]{4,3,2,1,0:T(8,128)(2,1)} %get-tuple-element.166), channel_id=1, source_target_pairs={{0,8},{4,12},{8,0},{12,4},{16,24},{20,28},{24,16},{28,20},{1,9},{5... | collective-permute-start | bytes 786440 | tf_op jit(solution)/shard_map/ppermute | solution.py:19
  281.7 8.3 %collective-permute-start.53 = (f16[2,1,2,64,512]{4,3,2,1,0:T(8,128)(2,1)}, f16[2,1,2,64,512]{4,3,2,1,0:T(8,128)(2,1)S(1)}, u32[]{:S(2)}, u32[]{:S(2)}) collective-permute-start(f16[2,1,2,64,512]{4,3,2,1,0:T(8,128)(2,1)} %get-tuple-element.168), channel_id=1, source_target_pairs={{0,16},{4,20},{8,24},{12,28},{16,0},{20,4},{24,8},{28,12},{1,17},{... | collective-permute-start | bytes 786440 | tf_op jit(solution)/shard_map/ppermute | solution.py:19
  283.6 16.3 %collective-permute-start.43 = (f16[64,4096]{1,0:T(8,128)(2,1)}, f16[64,4096]{1,0:T(8,128)(2,1)}, u32[]{:S(2)}, u32[]{:S(2)}) collective-permute-start(f16[64,4096]{1,0:T(8,128)(2,1)} %select_select_fusion), channel_id=1, source_target_pairs={{3,1},{0,2},{1,0},{2,3},{7,5},{4,6},{5,4},{6,7},{11,9},{8,10},{9,8... | collective-permute-start | bytes 1572872 | tf_op jit(solution)/shard_map/ppermute | solution.py:131
  288.0 31.3 %collective-permute-start.40 = (f16[64,4096]{1,0:T(8,128)(2,1)S(1)}, f16[64,4096]{1,0:T(8,128)(2,1)}, u32[]{:S(2)}, u32[]{:S(2)}) collective-permute-start(f16[64,4096]{1,0:T(8,128)(2,1)S(1)} %convert_element_type.212), channel_id=1, source_target_pairs={{0,3},{1,0},{2,1},{3,2},{4,7},{5,4},{6,5},{7,6},{8,11},{9,8},{10,9... | collective-permute-start | bytes 1572872 | tf_op jit(solution)/shard_map/ppermute | solution.py:122
  288.5 30.7 %collective-permute-start.41 = (f16[64,4096]{1,0:T(8,128)(2,1)S(1)}, f16[64,4096]{1,0:T(8,128)(2,1)}, u32[]{:S(2)}, u32[]{:S(2)}) collective-permute-start(f16[64,4096]{1,0:T(8,128)(2,1)S(1)} %convert_element_type.212), channel_id=1, source_target_pairs={{0,1},{1,2},{2,3},{3,0},{4,5},{5,6},{6,7},{7,4},{8,9},{9,10},{10,1... | collective-permute-start | bytes 1572872 | tf_op jit(solution)/shard_map/ppermute | solution.py:122
  292.7 38.2 %collective-permute-start.54 = (f16[1,2,2,128,512]{4,3,2,1,0:T(8,128)(2,1)}, f16[1,2,2,128,512]{4,3,2,1,0:T(8,128)(2,1)}, u32[]{:S(2)}, u32[]{:S(2)}) collective-permute-start(f16[1,2,2,128,512]{4,3,2,1,0:T(8,128)(2,1)} %get-tuple-element.160), channel_id=1, source_target_pairs={{0,4},{4,0},{8,12},{12,8},{16,20},{20,16},{24,28},{28,24},{1,5},{5... | collective-permute-start | bytes 1572872 | tf_op jit(solution)/shard_map/ppermute | solution.py:19
  315.4 15.5 %copy-start.22 = (f16[1,2,2,128,512]{4,3,2,1,0:T(8,128)(2,1)S(1)}, f16[1,2,2,128,512]{4,3,2,1,0:T(8,128)(2,1)}, u32[]{:S(2)}) copy-start(f16[1,2,2,128,512]{4,3,2,1,0:T(8,128)(2,1)} %get-tuple-element.159) | copy-start | bytes 1572868
  316.5 20.0 %collective-permute-start.44 = (f16[256,1024]{1,0:T(8,128)(2,1)}, f16[256,1024]{1,0:T(8,128)(2,1)S(1)}, u32[]{:S(2)}, u32[]{:S(2)}) collective-permute-start(f16[256,1024]{1,0:T(8,128)(2,1)} %get-tuple-element.114), channel_id=1, source_target_pairs={{0,8},{4,12},{8,0},{12,4},{16,24},{20,28},{24,16},{28,20},{1,9},{5... | collective-permute-start | bytes 1572872 | tf_op jit(solution)/shard_map/ppermute | solution.py:19
  317.9 19.7 %collective-permute-start.45 = (f16[256,1024]{1,0:T(8,128)(2,1)}, f16[256,1024]{1,0:T(8,128)(2,1)}, u32[]{:S(2)}, u32[]{:S(2)}) collective-permute-start(f16[256,1024]{1,0:T(8,128)(2,1)} %get-tuple-element.114), channel_id=1, source_target_pairs={{0,16},{4,20},{8,24},{12,28},{16,0},{20,4},{24,8},{28,12},{1,17},{... | collective-permute-start | bytes 1572872 | tf_op jit(solution)/shard_map/ppermute | solution.py:19
  320.4 18.9 %collective-permute-start.42 = (f16[64,4096]{1,0:T(8,128)(2,1)}, f16[64,4096]{1,0:T(8,128)(2,1)}, u32[]{:S(2)}, u32[]{:S(2)}) collective-permute-start(f16[64,4096]{1,0:T(8,128)(2,1)} %select_select_fusion.1), channel_id=1, source_target_pairs={{3,1},{0,2},{1,0},{2,3},{7,5},{4,6},{5,4},{6,7},{11,9},{8,10},{9,8... | collective-permute-start | bytes 1572872 | tf_op jit(solution)/shard_map/ppermute | solution.py:131
  336.7 7.7 %collective-permute-start.46 = (f16[128,1024]{1,0:T(8,128)(2,1)S(1)}, f16[128,1024]{1,0:T(8,128)(2,1)S(1)}, u32[]{:S(2)}, u32[]{:S(2)}) collective-permute-start(f16[128,1024]{1,0:T(8,128)(2,1)S(1)} %slice.271), channel_id=1, source_target_pairs={{0,16},{4,20},{8,24},{12,28},{16,0},{20,4},{24,8},{28,12},{1,17},{... | collective-permute-start | bytes 786440 | tf_op jit(solution)/shard_map/ppermute | solution.py:19
  338.5 6.6 %collective-permute-start.47 = (f16[128,1024]{1,0:T(8,128)(2,1)S(1)}, f16[128,1024]{1,0:T(8,128)(2,1)S(1)}, u32[]{:S(2)}, u32[]{:S(2)}) collective-permute-start(f16[128,1024]{1,0:T(8,128)(2,1)S(1)} %slice.272), channel_id=1, source_target_pairs={{0,8},{4,12},{8,0},{12,4},{16,24},{20,28},{24,16},{28,20},{1,9},{5... | collective-permute-start | bytes 786440 | tf_op jit(solution)/shard_map/ppermute | solution.py:19
  345.8 21.5 %collective-permute-start.55 = (f16[1024,1024]{1,0:T(8,128)(2,1)}, f16[1024,1024]{1,0:T(8,128)(2,1)}, u32[]{:S(2)}, u32[]{:S(2)}) collective-permute-start(f16[1024,1024]{1,0:T(8,128)(2,1)} %constant_dynamic-update-slice_fusion.15), channel_id=1, source_target_pairs={{0,4},{4,0},{8,12},{12,8},{16,20},{20,16},{24,28},{28,24},{1,5},{5... | collective-permute-start | bytes 6291464 | tf_op jit(solution)/shard_map/ppermute | solution.py:19
  362.0 17.7 %collective-permute-start.48 = (f16[256,1024]{1,0:T(8,128)(2,1)S(1)}, f16[256,1024]{1,0:T(8,128)(2,1)S(1)}, u32[]{:S(2)}, u32[]{:S(2)}) collective-permute-start(f16[256,1024]{1,0:T(8,128)(2,1)S(1)} %get-tuple-element.112), channel_id=1, source_target_pairs={{0,8},{4,12},{8,0},{12,4},{16,24},{20,28},{24,16},{28,20},{1,9},{5... | collective-permute-start | bytes 1572872 | tf_op jit(solution)/shard_map/ppermute | solution.py:19
  363.4 16.4 %collective-permute-start.49 = (f16[256,1024]{1,0:T(8,128)(2,1)S(1)}, f16[256,1024]{1,0:T(8,128)(2,1)S(1)}, u32[]{:S(2)}, u32[]{:S(2)}) collective-permute-start(f16[256,1024]{1,0:T(8,128)(2,1)S(1)} %get-tuple-element.112), channel_id=1, source_target_pairs={{0,16},{4,20},{8,24},{12,28},{16,0},{20,4},{24,8},{28,12},{1,17},{... | collective-permute-start | bytes 1572872 | tf_op jit(solution)/shard_map/ppermute | solution.py:19
  379.8 8.2 %collective-permute-start.56 = (f16[128,1024]{1,0:T(8,128)(2,1)S(1)}, f16[128,1024]{1,0:T(8,128)(2,1)S(1)}, u32[]{:S(2)}, u32[]{:S(2)}) collective-permute-start(f16[128,1024]{1,0:T(8,128)(2,1)S(1)} %slice.244), channel_id=1, source_target_pairs={{0,16},{4,20},{8,24},{12,28},{16,0},{20,4},{24,8},{28,12},{1,17},{... | collective-permute-start | bytes 786440 | tf_op jit(solution)/shard_map/ppermute | solution.py:19
  380.7 7.9 %collective-permute-start.57 = (f16[128,1024]{1,0:T(8,128)(2,1)S(1)}, f16[128,1024]{1,0:T(8,128)(2,1)S(1)}, u32[]{:S(2)}, u32[]{:S(2)}) collective-permute-start(f16[128,1024]{1,0:T(8,128)(2,1)S(1)} %slice.245), channel_id=1, source_target_pairs={{0,8},{4,12},{8,0},{12,4},{16,24},{20,28},{24,16},{28,20},{1,9},{5... | collective-permute-start | bytes 786440 | tf_op jit(solution)/shard_map/ppermute | solution.py:19
  388.7 4.2 %collective-permute-start.58 = (f16[1024,1024]{1,0:T(8,128)(2,1)S(1)}, f16[1024,1024]{1,0:T(8,128)(2,1)S(1)}, u32[]{:S(2)}, u32[]{:S(2)}) collective-permute-start(f16[1024,1024]{1,0:T(8,128)(2,1)S(1)} %constant_dynamic-update-slice_fusion.20), channel_id=1, source_target_pairs={{0,4},{4,0},{8,12},{12,8},{16,20},{20,16},{24,28},{28,24},{1,5},{5... | collective-permute-start | bytes 6291464 | tf_op jit(solution)/shard_map/ppermute | solution.py:19
  (30 other events, 153.5 us)
Sparse Core Ops, SparseCore 0:
  23.0 81.1 all-gather.4
  105.8 79.4 all-gather.6
